TPU v7x, 256 devices: a whole 4x4x8 slice. The times are simulated.
256 devices in a mesh: dp: 32 (over y, z_lo, core), tensor: 8 (over z_hi, x).
Axes of the slice: x: 4, y: 4, z: 8 (z_hi: 2, z_lo: 4; z = z_hi * 4 + z_lo), core: 2. Of those that a mesh axis runs over, the one named last changes fastest.
Arguments:
- momentum: float32 [32, 4, 128, 8192], P('dp', None, None, 'tensor'), may hold values from -200 to 200
- gradient: bfloat16 [32, 4, 128, 8192], P('dp', None, None, 'tensor'), may hold values from -2 to 2
- kept_index: int32 [32, 4, 2, 128, 32], P(None, None, None, 'tensor'), may hold values from 0 to 4095, as said below
Outputs:
- momentum_out: float32 [32, 4, 128, 8192], P('dp', None, None, 'tensor')
- update: float32 [4, 128, 8192], P(None, None, 'tensor')
Inputs may be any that keep to these rules, and one draw needn't show every extreme that they name: `kept_index`: for each replica and block the 32 positions are distinct, each f_r * 64 + f_c with f_r, f_c below 64.
All inputs are finite; a program needn't handle non-finite values.
Results may differ from a plain program's by a relative error of at most 0.0003.
Values sent between devices are 32-bit elements; how exact they have to be, the bound alone decides.
No kernel may reach another device: no remote copies, remote signals or barrier semaphores. Data moves between devices by JAX's collectives and lax.ppermute only.
A program may use at most 64 MiB of HBM per device.

v0:
```python
import math

import jax
import jax.numpy as jnp
from jax import lax
from jax.sharding import PartitionSpec as P

GROUP = 64
TOPK = 32


decay_rate = 0.999
epsilon = 1e-06


def cosine_rows(frequency, length):
    points = jnp.arange(length, dtype=jnp.float32)
    waves = frequency.astype(jnp.float32)[..., None]
    factor = jnp.where(frequency == 0, math.sqrt(1.0 / length), math.sqrt(2.0 / length))[..., None]
    return factor * jnp.cos(math.pi * (2.0 * points + 1.0) * waves / (2.0 * length))


def on_device(momentum, gradient, kept_index):
    accumulated = decay_rate * momentum[0] + gradient[0].astype(jnp.float32)
    layers, rows, cols = accumulated.shape
    group_count = layers * (rows // GROUP) * (cols // GROUP)
    row_ids = jnp.arange(group_count, dtype=jnp.int32)[:, None]
    whole_basis = cosine_rows(jnp.arange(GROUP, dtype=jnp.int32), GROUP)
    blocks = accumulated.reshape(layers, rows // GROUP, GROUP, cols // GROUP, GROUP)
    spectrum = jnp.einsum(
        "kr,larcb,mb->lackm", whole_basis, blocks, whole_basis, precision=lax.Precision.HIGHEST
    )
    spectrum = spectrum.reshape(group_count, GROUP * GROUP)
    my_positions = lax.dynamic_index_in_dim(
        kept_index, lax.axis_index("dp"), 0, keepdims=False
    ).reshape(group_count, TOPK)
    own_values = jnp.take_along_axis(spectrum, my_positions, axis=1)
    own_grid = jnp.zeros_like(spectrum).at[row_ids, my_positions].add(own_values)

    def decode(coef_grid):
        shaped = coef_grid.reshape(layers, rows // GROUP, cols // GROUP, GROUP, GROUP)
        out_blocks = jnp.einsum(
            "kr,lackm,mb->larcb", whole_basis, shaped, whole_basis, precision=lax.Precision.HIGHEST
        )
        return out_blocks.reshape(layers, rows, cols)

    summed = lax.psum(own_grid, "dp")
    momentum_out = accumulated - decode(own_grid)
    decoded = decode(summed)
    local_squares = jnp.sum(decoded * decoded, axis=(1, 2))
    all_squares = lax.psum(local_squares, "tensor")
    entries = rows * cols * lax.axis_size("tensor")
    update = decoded * lax.rsqrt(all_squares / entries + epsilon)[:, None, None]
    return (momentum_out[None], update)


def solution(mesh):
    placed = (
        P("dp", None, None, "tensor"),
        P("dp", None, None, "tensor"),
        P(None, None, None, "tensor", None),
    )
    return jax.shard_map(
        on_device,
        mesh=mesh,
        in_specs=placed,
        out_specs=(P("dp", None, None, "tensor"), P(None, None, "tensor")),
        check_vma=False,
    )
```

profile of v0, /device:TPU:1, one launch (start us, length us, event | category | flops | bytes accessed | tf_op | source)
XLA Modules:
  0.0 457.8 jit_solution(1868638747005229415)
XLA Ops:
  7.3 1.5 copy-done
  8.9 0.8 and_reduce_fusion
  9.7 0.7 multiply_reduce_fusion.1
  10.6 2.2 convert_add_fusion
  12.9 2.7 add.72
  15.5 7.5 %fusion = f32[4,2,16,64,64]{3,4,2,1,0:T(8,128)S(1)} fusion(f32[4,2,64,16,64]{4,3,2,1,0:T(8,128)} %add.72, f32[64]{0:T(128)S(1)} %iota_convert_fusion, f32[64]{0:T(128)S(1)} %get-tuple-element.7, f32[64]{0:T(128)S(1)} %get-tuple-element.6), kind=kOutput, calls=%fused_computation.2 | convolution fusion | flops 402665472 | bytes 4195072 | tf_op jit(solution)/shard_map/kr,larcb,mb->lackm/dot_general | solution.py:30
  23.0 5.3 %fusion.10 = f32[4,2,16,64,64]{4,3,2,1,0:T(8,128)} fusion(f32[4,2,16,64,64]{3,4,2,1,0:T(8,128)S(1)} %fusion, f32[64]{0:T(128)S(1)} %iota_convert_fusion, f32[64]{0:T(128)S(1)} %get-tuple-element.7, f32[64]{0:T(128)S(1)} %get-tuple-element.6), kind=kOutput, calls=%fused_computation.22 | convolution fusion | flops 402665472 | bytes 4195072 | tf_op jit(solution)/shard_map/kr,larcb,mb->lackm/dot_general | solution.py:30
  28.4 3.5 reshape.89
  31.9 32.8 %gather_fusion = f32[4096]{0:T(1024)S(1)} fusion(f32[128,4096]{1,0:T(8,128)S(1)} %reshape.89, s32[4096]{0:T(1024)S(1)} %reshape.99), kind=kCustom, calls=%fused_computation | custom fusion | bytes 65536 | tf_op jit(solution)/shard_map/jit(take_along_axis)/gather | solution.py:37
  64.8 22.8 %scatter_custom_fusion = f32[524288]{0:T(1024)S(1)} fusion(s32[4096]{0:T(1024)S(1)} %reshape.105, f32[4096]{0:T(1024)S(1)} %reshape.107, f32[]{:T(128)} %constant.18.clone.1), kind=kCustom, calls=%fused_computation.8 | custom fusion | flops 4096 | bytes 2097156
  87.6 2.3 reshape.90
  90.0 5.4 %copy.33 = f32[4,2,16,64,64]{3,4,2,1,0:T(8,128)} copy(f32[4,2,16,64,64]{4,3,2,1,0:T(8,128)} %reshape.90) | data formatting | bytes 4194304 | tf_op jit(solution)/shard_map/reshape | solution.py:41
  95.4 5.9 %fusion.8 = f32[4,2,16,64,64]{3,4,2,1,0:T(8,128)S(1)} fusion(f32[4,2,16,64,64]{4,3,2,1,0:T(8,128)} %reshape.90, f32[64]{0:T(128)S(1)} %iota_convert_fusion, f32[64]{0:T(128)S(1)} %get-tuple-element.7, f32[64]{0:T(128)S(1)} %get-tuple-element.6), kind=kOutput, calls=%fused_computation.20 | convolution fusion | flops 402665472 | bytes 4195072 | tf_op jit(solution)/shard_map/kr,lackm,mb->larcb/dot_general | solution.py:42
  101.3 3.6 convolution_bitcast_fusion.1
  104.9 4.3 copy.32
  109.2 5.0 %reshape.91 = f32[1,4,128,1024]{3,2,1,0:T(8,128)} reshape(f32[4,2,64,16,64]{4,3,2,1,0:T(8,128)} %copy.32) | data formatting | bytes 4194304 | tf_op jit(solution)/shard_map/reshape | solution.py:45
  114.3 3.3 sub.4
  117.6 273.0 %all-reduce.2.cloned.1.call-done = f32[4,2,16,64,64]{3,4,2,1,0:T(8,128)} async-done(((f32[4,2,16,64,64]{3,4,2,1,0:T(8,128)}), f32[4,2,16,64,64]{3,4,2,1,0:T(8,128)}) %all-reduce.2.cloned.1.call-update) | async-done | bytes 2097168 | tf_op jit(solution)/shard_map/psum | solution.py:47
  390.5 14.1 %fusion.5 = f32[4,2,16,64,64]{3,4,2,1,0:T(8,128)S(1)} fusion(f32[4,2,16,64,64]{3,4,2,1,0:T(8,128)} %all-reduce.2.cloned.1.call-done, f32[64]{0:T(128)S(1)} %iota_convert_fusion, f32[64]{0:T(128)S(1)} %get-tuple-element.7, f32[64]{0:T(128)S(1)} %get-tuple-element.6), kind=kOutput, calls=%fused_computation.17 | convolution fusion | flops 402665472 | bytes 4195072 | tf_op jit(solution)/shard_map/kr,lackm,mb->larcb/dot_general | solution.py:42
  404.6 5.3 %multiply_reduce_fusion = (f32[4]{0:T(128)S(1)}, f32[4,2,64,16,64]{4,2,3,1,0:T(8,128)}) fusion(f32[4,2,16,64,64]{3,4,2,1,0:T(8,128)S(1)} %fusion.5, f32[64]{0:T(128)S(1)} %iota_convert_fusion, f32[64]{0:T(128)S(1)} %get-tuple-element.7, f32[64]{0:T(128)S(1)} %get-tuple-element.6), kind=kOutput, calls=%fused_computation.4 | convolution fusion | flops 403714048 | bytes 4195088 | tf_op jit(solution)/shard_map/kr,lackm,mb->larcb/dot_general | solution.py:42
  410.0 26.1 %psum.15 = f32[4]{0:T(128)S(1)} all-reduce(f32[4]{0:T(128)S(1)} %get-tuple-element.4), channel_id=1, replica_groups=mesh['dp'=32,'tensor'=8] {'tensor'}, use_global_device_ids=true, to_apply=%region_3.4 | all-reduce | flops 4 | bytes 32 | tf_op jit(solution)/shard_map/psum | solution.py:51
  436.1 6.7 %copy.35 = f32[4,2,64,16,64]{4,3,2,1,0:T(8,128)} copy(f32[4,2,64,16,64]{4,2,3,1,0:T(8,128)} %get-tuple-element.5) | data formatting | bytes 4194304 | tf_op jit(solution)/shard_map/kr,lackm,mb->larcb/transpose | solution.py:42
  442.8 4.8 %reshape.93 = f32[4,128,1024]{2,1,0:T(8,128)} reshape(f32[4,2,64,16,64]{4,3,2,1,0:T(8,128)} %copy.35) | data formatting | bytes 4194304 | tf_op jit(solution)/shard_map/reshape | solution.py:45
  447.6 3.3 broadcast_multiply_fusion
  (23 shorter events, 0.6 us)
Async XLA Ops:
  7.2 1.6 copy-start
  7.2 383.4 %all-reduce.2.cloned.1.call-start = ((), (), s32[]{:S(2)}) async-start(), calls=%async_computation | async-start | bytes 8388608 | tf_op jit(solution)/shard_map/psum | solution.py:47
  12.9 10.2 %copy-start.2 = (f32[1,4,128,1024]{3,2,1,0:T(8,128)}, f32[1,4,128,1024]{3,2,1,0:T(8,128)S(1)}, u32[]{:S(2)}) copy-start(f32[1,4,128,1024]{3,2,1,0:T(8,128)S(1)} %convert_add_fusion) | copy-start | bytes 6291460
  109.2 5.0 %copy-start.3 = (f32[1,4,128,1024]{3,2,1,0:T(8,128)S(1)}, f32[1,4,128,1024]{3,2,1,0:T(8,128)}, u32[]{:S(2)}) copy-start(f32[1,4,128,1024]{3,2,1,0:T(8,128)} %copy-done.2) | copy-start | bytes 6291460
  436.1 14.9 %copy-start.1 = (s32[32,4,2,16,32]{4,3,2,1,0:T(8,128)S(1)}, s32[32,4,2,16,32]{4,3,2,1,0:T(8,128)}, u32[]{:S(2)}) copy-start(s32[32,4,2,16,32]{4,3,2,1,0:T(8,128)} %param.5) | copy-start | bytes 1572868
Sparse Core Ops, SparseCore 0:
  95.5 294.9 all-reduce.1
where the time goes:
time: 462 us; the launch traced here: 458 us
  waiting for transfers between devices  273 us (59%)
  local copies, waits for them, and re-layouts  69.6 us (15%)
  matrix products  41.7 us (9%)
  other arithmetic  33.2 us (7%)
  blocking collectives  26.1 us (6%)
  between operations  14.2 us (3%)
    psum x1, waiting for transfers between devices, on_device(): summed = lax.psum(own_grid, 'dp')  273 us
    gather x2, local copies, waits for them, and re-layouts, on_device(): own_values = jnp.take_along_axis(spectrum, my_positions, axis=1)  32.8 us
    dot_general x4, matrix products, decode(): jnp.einsum('kr,lackm,mb->larcb', whole_basis, shaped, whole_basis, precis...  28.9 us
    psum x1, blocking collectives, on_device(): all_squares = lax.psum(local_squares, 'tensor')  26.1 us
    unnamed x4, other arithmetic  24.3 us
    dot_general x2, matrix products, on_device(): jnp.einsum('kr,larcb,mb->lackm', whole_basis, blocks, whole_basis, precis...  12.8 us
    transpose x2, local copies, waits for them, and re-layouts, decode(): jnp.einsum('kr,lackm,mb->larcb', whole_basis, shaped, whole_basis, precis...  11 us
    reshape x2, local copies, waits for them, and re-layouts, decode(): return out_blocks.reshape(layers, rows, cols)  9.86 us
  transfers between devices with their start and end apart: 1, of which 1 were waited for; matrix products, arithmetic and copies ran while one was open for 5% of the time, Pallas kernels for 0%

commit v1 on v0

v1 whole, which is shorter than its diff:
```python
import math

import jax
import jax.numpy as jnp
import ml_dtypes
import numpy as np
from jax import lax
from jax.experimental import pallas as pl
from jax.experimental.pallas import tpu as pltpu
from jax.sharding import PartitionSpec as P

GROUP = 64
TOPK = 32
REPLICAS = 32
LAYERS = 4
ROWS = 128
COLS = 1024
TILES = COLS // 256
BLOCKS = 128

decay_rate = 0.999
epsilon = 1e-06

BF = jnp.bfloat16
F32 = jnp.float32


def basis_matrix():
    f = np.arange(GROUP, dtype=np.float64)[:, None]
    n = np.arange(GROUP, dtype=np.float64)[None, :]
    scale = np.where(f == 0, math.sqrt(1.0 / GROUP), math.sqrt(2.0 / GROUP))
    return scale * np.cos(math.pi * (2.0 * n + 1.0) * f / (2.0 * GROUP))


def halves(x):
    x = x.astype(np.float32)
    hi = x.astype(ml_dtypes.bfloat16)
    lo = (x - hi.astype(np.float32)).astype(ml_dtypes.bfloat16)
    return hi, lo


def constants():
    b = basis_matrix()
    two, four = np.kron(np.eye(2), b), np.kron(np.eye(4), b)
    row_hi, row_lo = halves(two)
    col_hi, col_lo = halves(four)
    forward_rows = np.concatenate([row_hi, row_hi, row_lo], axis=1)
    forward_cols = np.concatenate([col_hi, col_lo], axis=0)
    back_hi, back_lo = halves(two.T)
    back_rows = np.concatenate([back_hi, back_hi, back_lo], axis=1)
    return forward_rows, forward_cols, back_rows


def split(x):
    hi = x.astype(BF)
    return hi, (x - hi.astype(F32)).astype(BF)


def mm(a, b):
    return jnp.dot(a, b, preferred_element_type=F32)


def mm_t(a, b):
    return lax.dot_general(a, b, (((1,), (1,)), ((), ())), preferred_element_type=F32)


def rows_apply(rows, x):
    hi, lo = split(x)
    return mm(rows[:, :256], jnp.concatenate([hi, lo], axis=0)) + mm(rows[:, 256:], hi)


def cols_apply(x, cols):
    hi, lo = split(x)
    both = mm(jnp.concatenate([hi, lo], axis=0), cols[:256])
    return both[:128] + both[128:] + mm(hi, cols[256:])


def own_rows(idx_ref):
    return jnp.concatenate([idx_ref[pl.ds(cj, 32, stride=4), :] for cj in range(4)], axis=1)


def lane_block(shape):
    return lax.shift_right_logical(lax.broadcasted_iota(jnp.int32, shape, len(shape) - 1), 5) & 3


def pick_kernel(p_ref, m_ref, g_ref, idx_ref, rows_ref, cols_ref, v_ref, own_ref):
    layer = pl.program_id(0)

    @pl.when(layer == 0)
    def _():
        own_ref[...] = own_rows(idx_ref)

    acc = decay_rate * m_ref[0] + g_ref[0].astype(F32)
    y = rows_apply(rows_ref[...], acc)
    y_hi, y_lo = split(y)
    freq = lax.broadcasted_iota(jnp.int32, (GROUP, 128), 0)
    place = lax.broadcasted_iota(jnp.int32, (256, 256), 0)
    zeros = jnp.zeros((GROUP, 128), BF)
    for t in range(TILES):
        s = slice(t * 256, t * 256 + 256)
        both = mm_t(cols_ref[:256], jnp.concatenate([y_hi[:, s], y_lo[:, s]], axis=0))
        spec = both[:, :128] + both[:, 128:] + mm_t(cols_ref[256:], y_hi[:, s])
        spec_hi, spec_lo = split(spec)
        pos = [own_ref[pl.ds(layer * 8 + a * 4 + t, 1), :] for a in range(2)]
        fr = [lax.shift_right_logical(x, 6) for x in pos]
        hot = [(freq == x).astype(F32).astype(BF) for x in fr]
        pick = jnp.concatenate(
            [
                jnp.concatenate([hot[0], zeros], axis=1),
                jnp.concatenate([zeros, hot[1]], axis=1),
            ],
            axis=0,
        )
        got = mm(jnp.concatenate([spec_hi, spec_lo], axis=1), jnp.concatenate([pick, pick], axis=0))
        where = jnp.concatenate([(x & 63) + 64 * lane_block((1, 128)) for x in pos], axis=1)
        v = jnp.sum(jnp.where(place == where, got, 0.0), axis=0, keepdims=True)
        for a in range(2):
            v_ref[pl.ds(layer * 8 + a * 4 + t, 1), :] = v[:, a * 128 : a * 128 + 128]


def own_kernel(m_ref, g_ref, own_ref, v_ref, rows_ref, cols_ref, out_ref):
    layer = pl.program_id(0)
    freq = lax.broadcasted_iota(jnp.int32, (GROUP, 128), 0)
    place = lax.broadcasted_iota(jnp.int32, (256, 128), 0)
    for t in range(TILES):
        s = slice(t * 256, t * 256 + 256)
        grids = []
        for a in range(2):
            row = layer * 8 + a * 4 + t
            pos = own_ref[pl.ds(row, 1), :]
            v = v_ref[pl.ds(row, 1), :]
            left = jnp.where(freq == lax.shift_right_logical(pos, 6), v, 0.0)
            hi, lo = split(left)
            right = (place == (pos & 63) + 64 * lane_block((1, 128))).astype(F32).astype(BF)
            both = mm_t(jnp.concatenate([hi, lo], axis=0), right)
            grids.append(both[:GROUP] + both[GROUP:])
        grid = jnp.concatenate(grids, axis=0)
        back = cols_apply(rows_apply(rows_ref[...], grid), cols_ref[...])
        out_ref[0, :, s] = decay_rate * m_ref[0, :, s] + g_ref[0, :, s].astype(F32) - back


def arrange_kernel(p_ref, idx_ref, fr_ref, fc_ref):
    p = p_ref[0]
    for q in range(REPLICAS // 4):
        pos = jnp.concatenate([idx_ref[pl.ds((p ^ (4 * q + j)) * BLOCKS, BLOCKS), :] for j in range(4)], axis=1)
        fr_ref[:, q * 128 : q * 128 + 128] = lax.shift_right_logical(pos, 6).astype(F32)
        fc_ref[:, q * 128 : q * 128 + 128] = (pos & 63).astype(F32)


def sum_kernel(v_ref, fr_ref, fc_ref, rows_ref, cols_ref, out_ref, sq_ref, val_ref, grid_ref):
    layer = pl.program_id(0)
    lane = lane_block((8, 128))

    for q in range(REPLICAS // 4):
        x = [v_ref[4 * q + j, pl.ds(layer * 8, 8), :] for j in range(4)]
        for cj in range(4):
            y = jnp.zeros((8, 128), F32)
            for j in range(4):
                moved = x[j] if j == cj else pltpu.roll(x[j], ((j - cj) * 32) % 128, 1)
                y = jnp.where(lane == j, moved, y)
            val_ref[cj, :, q * 128 : q * 128 + 128] = y

    freq = lax.broadcasted_iota(jnp.int32, (GROUP, 1024), 0).astype(F32).astype(BF)

    def body(i, carry):
        grids = []
        for cj in range(4):
            row = layer * 32 + i * 4 + cj
            fr = fr_ref[pl.ds(row, 1), :].astype(BF)
            fc = fc_ref[pl.ds(row, 1), :].astype(BF)
            hi, lo = split(val_ref[cj, pl.ds(i, 1), :])
            at = freq == fr
            zero = jnp.zeros((), BF)
            left = jnp.concatenate([jnp.where(at, hi, zero), jnp.where(at, lo, zero)], axis=0)
            right = jnp.where(freq == fc, jnp.ones((), BF), zero)
            both = mm_t(left, right)
            grids.append(both[:GROUP] + both[GROUP:])
        a, cq = i // 4, i % 4
        grid_ref[cq, pl.ds(pl.multiple_of(a * GROUP, GROUP), GROUP), :] = jnp.concatenate(grids, axis=1)
        return carry

    lax.fori_loop(0, 8, body, 0)
    squares = jnp.zeros((1, 256), F32)
    for t in range(TILES):
        s = slice(t * 256, t * 256 + 256)
        grid = grid_ref[t]
        squares = squares + jnp.sum(grid * grid, axis=0, keepdims=True)
        out_ref[0, :, s] = cols_apply(rows_apply(rows_ref[...], grid), cols_ref[...])
    sq_ref[0] = squares[:, :128] + squares[:, 128:]


def whole(shape):
    return pl.BlockSpec(shape, lambda *_: (0,) * len(shape))


def params():
    return pltpu.CompilerParams(vmem_limit_bytes=40 * 2**20)


def pick(p, m, g, idx, rows, cols):
    layer = lambda l, p: (l, 0, 0)
    return pl.pallas_call(
        pick_kernel,
        grid_spec=pltpu.PrefetchScalarGridSpec(
            num_scalar_prefetch=1,
            grid=(LAYERS,),
            in_specs=[
                pl.BlockSpec((1, ROWS, COLS), layer),
                pl.BlockSpec((1, ROWS, COLS), layer),
                pl.BlockSpec((BLOCKS, TOPK), lambda l, p: (p[0], 0)),
                whole(rows.shape),
                whole(cols.shape),
            ],
            out_specs=[whole((32, 128)), whole((32, 128))],
        ),
        out_shape=[jax.ShapeDtypeStruct((32, 128), F32), jax.ShapeDtypeStruct((32, 128), jnp.int32)],
        compiler_params=params(),
        name="pick",
    )(p, m, g, idx, rows, cols)


def own_update(m, g, own, v, rows, cols):
    layer = lambda l: (l, 0, 0)
    return pl.pallas_call(
        own_kernel,
        grid=(LAYERS,),
        in_specs=[
            pl.BlockSpec((1, ROWS, COLS), layer),
            pl.BlockSpec((1, ROWS, COLS), layer),
            whole((32, 128)),
            whole((32, 128)),
            whole(rows.shape),
            whole(cols.shape),
        ],
        out_specs=pl.BlockSpec((1, ROWS, COLS), layer),
        out_shape=jax.ShapeDtypeStruct((LAYERS, ROWS, COLS), F32),
        compiler_params=params(),
        name="own",
    )(m, g, own, v, rows, cols)


def arrange(p, idx):
    return pl.pallas_call(
        arrange_kernel,
        grid_spec=pltpu.PrefetchScalarGridSpec(
            num_scalar_prefetch=1,
            grid=(1,),
            in_specs=[whole(idx.shape)],
            out_specs=[whole((BLOCKS, 1024)), whole((BLOCKS, 1024))],
        ),
        out_shape=[jax.ShapeDtypeStruct((BLOCKS, 1024), F32)] * 2,
        compiler_params=params(),
        name="arrange",
    )(p, idx)


def sum_decode(v, fr, fc, rows, cols):
    layer = lambda l: (l, 0, 0)
    return pl.pallas_call(
        sum_kernel,
        grid=(LAYERS,),
        in_specs=[
            whole(v.shape),
            whole(fr.shape),
            whole(fc.shape),
            whole(rows.shape),
            whole(cols.shape),
        ],
        out_specs=[pl.BlockSpec((1, ROWS, COLS), layer), pl.BlockSpec((1, 1, 128), layer)],
        out_shape=[
            jax.ShapeDtypeStruct((LAYERS, ROWS, COLS), F32),
            jax.ShapeDtypeStruct((LAYERS, 1, 128), F32),
        ],
        scratch_shapes=[pltpu.VMEM((4, 8, 1024), F32), pltpu.VMEM((TILES, 128, 256), F32)],
        compiler_params=params(),
        name="sum_decode",
    )(v, fr, fc, rows, cols)


def gather_values(v):
    def turn(x, bit):
        return lax.ppermute(x, "dp", [(i, i ^ bit) for i in range(REPLICAS)])

    v = v[None, None]
    v = jnp.concatenate([v] + [turn(v, b) for b in (2, 4, 6)], axis=0)
    v = jnp.concatenate([v] + [turn(v, b) for b in (8, 16, 24)], axis=0)
    v = jnp.concatenate([v, turn(v, 1)], axis=1)
    return v.reshape(REPLICAS, 32, 128)


def on_device(momentum, gradient, kept_index):
    m, g = momentum[0], gradient[0]
    idx = kept_index.reshape(REPLICAS * BLOCKS, TOPK)
    forward_rows, forward_cols, back_rows = (jnp.asarray(x) for x in constants())
    p = lax.axis_index("dp").astype(jnp.int32).reshape(1)
    v, own = pick(p, m, g, idx, forward_rows, forward_cols)
    values = gather_values(v)
    fr, fc = arrange(p, idx)
    momentum_out = own_update(m, g, own, v, back_rows, forward_cols)
    decoded, squares = sum_decode(values, fr, fc, back_rows, forward_cols)
    squares = jnp.sum(squares, axis=(1, 2))
    total = squares
    for bits in ((1, 2, 3), (4,)):
        total = total + sum(
            lax.ppermute(total, "tensor", [(i, i ^ b) for i in range(8)]) for b in bits
        )
    entries = ROWS * COLS * lax.axis_size("tensor")
    update = decoded * lax.rsqrt(total / entries + epsilon)[:, None, None]
    return (momentum_out[None], update)


def solution(mesh):
    placed = (
        P("dp", None, None, "tensor"),
        P("dp", None, None, "tensor"),
        P(None, None, None, "tensor", None),
    )
    return jax.shard_map(
        on_device,
        mesh=mesh,
        in_specs=placed,
        out_specs=(P("dp", None, None, "tensor"), P(None, None, "tensor")),
        check_vma=False,
    )
```

time: 462 us -> 74.1 us (0.16)
  waiting for transfers between devices: 273 us -> 12.4 us
  local copies, waits for them, and re-layouts: 69.6 us -> 6.29 us
  matrix products: 41.7 us -> 0 us
  Pallas kernels: 0 us -> 32.2 us
  other arithmetic: 33.2 us -> 1.79 us
  blocking collectives: 26.1 us -> 0 us
  starting transfers between devices: 0.04 us -> 20.2 us
  between operations: 14.2 us -> 0.77 us
    psum x1 -> x0, waiting for transfers between devices: 273 us -> none  [on_device(): summed = lax.psum(own_grid, 'dp')]
    dot_general x6 -> x0, matrix products: 41.7 us -> none  [the longest x4 28.9 us: decode(): jnp.einsum('kr,lackm,mb->larcb', whole_basis, shaped, whole_basis, precis...]
    gather x2 -> x0, local copies, waits for them, and re-layouts: 32.8 us -> none  [on_device(): own_values = jnp.take_along_axis(spectrum, my_positions, axis=1)]
    pallas_call x0 -> x4, Pallas kernels: none -> 32.2 us  [the longest x1 20.3 us: sum_decode(): pl.pallas_call(sum_kernel, grid=(LAYERS,), in_specs=[whole(v.shape), whol...]
    psum x1 -> x0, blocking collectives: 26.1 us -> none  [on_device(): all_squares = lax.psum(local_squares, 'tensor')]
    unnamed x4 -> x0, other arithmetic: 24.3 us -> none
    reshape x5 -> x0, local copies, waits for them, and re-layouts: 21.1 us -> none  [the longest x2 9.86 us: decode(): return out_blocks.reshape(layers, rows, cols)]
    ppermute x0 -> x11, starting transfers between devices: none -> 20.2 us  [the longest x7 12.5 us: turn(): return lax.ppermute(x, 'dp', [(i, i ^ bit) for i in range(REPLICAS)])]
  transfers between devices with their start and end apart: 1 -> 11, of which waited for: 1 -> 7; matrix products, arithmetic and copies ran while one was open for 5% -> 0% of each run, Pallas kernels for 0% -> 9%
where the time goes in v1:
time: 74.1 us; the launch traced here: 73.7 us
  Pallas kernels  32.2 us (43%)
  starting transfers between devices  20.2 us (27%)
  waiting for transfers between devices  12.4 us (17%)
  local copies, waits for them, and re-layouts  6.29 us (8%)
  other arithmetic  1.79 us (2%)
  between operations  0.77 us (1%)
    pallas_call x1, Pallas kernels, sum_decode(): pl.pallas_call(sum_kernel, grid=(LAYERS,), in_specs=[whole(v.shape), whol...  20.3 us
    ppermute x7, starting transfers between devices, turn(): return lax.ppermute(x, 'dp', [(i, i ^ bit) for i in range(REPLICAS)])  12.5 us
    ppermute x4, starting transfers between devices, on_device(): lax.ppermute(total, 'tensor', [(i, i ^ b) for i in range(8)])  7.69 us
    ppermute x7, waiting for transfers between devices, turn(): return lax.ppermute(x, 'dp', [(i, i ^ bit) for i in range(REPLICAS)])  7.27 us
    unnamed x24, local copies, waits for them, and re-layouts  6.28 us
    pallas_call x1, Pallas kernels, own_update(): pl.pallas_call(own_kernel, grid=(LAYERS,), in_specs=[pl.BlockSpec((1, ROW...  6.26 us
    ppermute x4, waiting for transfers between devices, on_device(): lax.ppermute(total, 'tensor', [(i, i ^ b) for i in range(8)])  5.14 us
    pallas_call x1, Pallas kernels, pick(): pl.pallas_call(pick_kernel, grid_spec=pltpu.PrefetchScalarGridSpec(num_sc...  5.14 us
  transfers between devices with their start and end apart: 11, of which 7 were waited for; matrix products, arithmetic and copies ran while one was open for 0% of the time, Pallas kernels for 9%

profile of v1, /device:TPU:1, one launch (start us, length us, event | category | flops | bytes accessed | tf_op | source)
XLA Modules:
  0.0 73.7 jit_solution(2201582899627454851)
XLA Ops:
  0.6 1.6 %copy-done = s32[32,4,2,16,32]{4,3,2,1,0:T(8,128)S(1)} copy-done((s32[32,4,2,16,32]{4,3,2,1,0:T(8,128)S(1)}, s32[32,4,2,16,32]{4,3,2,1,0:T(8,128)}, u32[]{:S(2)}) %copy-start) | copy-done | bytes 524312
  2.2 1.6 %copy-done.1 = f32[1,4,128,1024]{3,2,1,0:T(8,128)S(1)} copy-done((f32[1,4,128,1024]{3,2,1,0:T(8,128)S(1)}, f32[1,4,128,1024]{3,2,1,0:T(8,128)}, u32[]{:S(2)}) %copy-start.1) | copy-done | bytes 2097176
  3.8 1.2 %copy-done.3 = bf16[1,4,128,1024]{3,2,1,0:T(8,128)(2,1)S(1)} copy-done((bf16[1,4,128,1024]{3,2,1,0:T(8,128)(2,1)S(1)}, bf16[1,4,128,1024]{3,2,1,0:T(8,128)(2,1)}, u32[]{:S(2)}) %copy-start.3) | copy-done | bytes 1048600
  5.0 0.9 %copy-done.5 = bf16[512,256]{1,0:T(8,128)(2,1)S(1)} copy-done((bf16[512,256]{1,0:T(8,128)(2,1)S(1)}, bf16[512,256]{1,0:T(8,128)(2,1)}, u32[]{:S(2)}) %copy-start.5) | copy-done | bytes 262168
  6.0 0.9 %copy-done.8 = bf16[128,384]{1,0:T(8,128)(2,1)S(1)} copy-done((bf16[128,384]{1,0:T(8,128)(2,1)S(1)}, bf16[128,384]{1,0:T(8,128)(2,1)}, u32[]{:S(2)}) %copy-start.8) | copy-done | bytes 98328
  6.9 5.1 %pick.1 = (f32[32,128]{1,0:T(8,128)S(1)}, s32[32,128]{1,0:T(8,128)S(1)}) custom-call(s32[1]{0:T(128)} %bitcast.2.p_ref, f32[4,128,1024]{2,1,0:T(8,128)S(1)} %bitcast.10, bf16[4,128,1024]{2,1,0:T(8,128)(2,1)S(1)} %bitcast.12, s32[4096,32]{1,0:T(8,128)S(1)} %bitcast.8, bf16[128,384]{1,0:T(8,128)(2,1)S(1)} %copy-done.8, bf16[512,256]{1,0:T(8,128)(2,1)S(1)} %copy-done.5), custom_call_target="tpu_custom_call" | custom-call | tf_op jit(solution)/shard_map/pick/pallas_call | solution.py:202
  12.1 5.3 %collective-permute-start.2 = (f32[1,1,32,128]{3,2,1,0:T(8,128)S(1)}, f32[1,1,32,128]{3,2,1,0:T(8,128)S(1)}, u32[]{:S(2)}, u32[]{:S(2)}) collective-permute-start(f32[1,1,32,128]{3,2,1,0:T(8,128)S(1)} %bitcast.15), channel_id=1, source_target_pairs={{0,48},{8,56},{16,32},{24,40},{32,16},{40,24},{48,0},{56,8},{64,11... | collective-permute-start | bytes 49160 | tf_op jit(solution)/shard_map/ppermute | solution.py:282
  17.3 0.4 collective-permute-start
  17.7 0.7 %collective-permute-done.2 = f32[1,1,32,128]{3,2,1,0:T(8,128)S(1)} collective-permute-done((f32[1,1,32,128]{3,2,1,0:T(8,128)S(1)}, f32[1,1,32,128]{3,2,1,0:T(8,128)S(1)}, u32[]{:S(2)}, u32[]{:S(2)}) %collective-permute-start.2) | collective-permute-done | bytes 16416 | tf_op jit(solution)/shard_map/ppermute | solution.py:282
  18.5 2.5 %collective-permute-done.1 = f32[1,1,32,128]{3,2,1,0:T(8,128)S(1)} collective-permute-done((f32[1,1,32,128]{3,2,1,0:T(8,128)S(1)}, f32[1,1,32,128]{3,2,1,0:T(8,128)S(1)}, u32[]{:S(2)}, u32[]{:S(2)}) %collective-permute-start.1) | collective-permute-done | bytes 16416 | tf_op jit(solution)/shard_map/ppermute | solution.py:282
  21.0 2.8 %collective-permute-start.5 = (f32[4,1,32,128]{3,2,1,0:T(8,128)S(1)}, f32[4,1,32,128]{3,2,1,0:T(8,128)S(1)}, u32[]{:S(2)}, u32[]{:S(2)}) collective-permute-start(f32[4,1,32,128]{3,2,1,0:T(8,128)S(1)} %pad_maximum_fusion.1), channel_id=1, source_target_pairs={{0,192},{8,200},{16,208},{24,216},{32,224},{40,232},{48,240},{56,2... | collective-permute-start | bytes 196616 | tf_op jit(solution)/shard_map/ppermute | solution.py:282
  23.8 0.3 collective-permute-start.4
  24.5 3.1 %collective-permute-done.3 = f32[4,1,32,128]{3,2,1,0:T(8,128)S(1)} collective-permute-done((f32[4,1,32,128]{3,2,1,0:T(8,128)S(1)}, f32[4,1,32,128]{3,2,1,0:T(8,128)S(1)}, u32[]{:S(2)}, u32[]{:S(2)}) %collective-permute-start.3) | collective-permute-done | bytes 65568 | tf_op jit(solution)/shard_map/ppermute | solution.py:282
  27.6 0.9 %collective-permute-done.4 = f32[4,1,32,128]{3,2,1,0:T(8,128)S(1)} collective-permute-done((f32[4,1,32,128]{3,2,1,0:T(8,128)S(1)}, f32[4,1,32,128]{3,2,1,0:T(8,128)S(1)}, u32[]{:S(2)}, u32[]{:S(2)}) %collective-permute-start.4) | collective-permute-done | bytes 65568 | tf_op jit(solution)/shard_map/ppermute | solution.py:282
  28.5 3.4 %collective-permute-start.6 = (f32[16,1,32,128]{3,2,1,0:T(8,128)S(1)}, f32[16,1,32,128]{3,2,1,0:T(8,128)S(1)}, u32[]{:S(2)}, u32[]{:S(2)}) collective-permute-start(f32[16,1,32,128]{3,2,1,0:T(8,128)S(1)} %constant_dynamic-update-slice_fusion), channel_id=1, source_target_pairs={{0,8},{8,0},{16,24},{24,16},{32,40},{40,32},{48,56},{56,48},{64,72... | collective-permute-start | bytes 786440 | tf_op jit(solution)/shard_map/ppermute | solution.py:282
  31.9 0.5 arrange.1
  32.5 6.3 %own.1 = f32[4,128,1024]{2,1,0:T(8,128)} custom-call(f32[4,128,1024]{2,1,0:T(8,128)S(1)} %bitcast.11, bf16[4,128,1024]{2,1,0:T(8,128)(2,1)S(1)} %bitcast.13, s32[32,128]{1,0:T(8,128)S(1)} %get-tuple-element.8.own_ref, f32[32,128]{1,0:T(8,128)S(1)} %get-tuple-element.9.v_ref, bf16[128,384]{1,0:T(8,128)(2,1)S(1)} %copy-done.7, bf16[512,256]{1,0:T(8,128)(2,1)S(1)} %copy-done.6), custom_call_target="tpu_custom_call" | custom-call | tf_op jit(solution)/shard_map/own/pallas_call | solution.py:224
  38.8 20.3 %sum_decode.1 = (f32[4,128,1024]{2,1,0:T(8,128)S(1)}, f32[4,1,128]{2,1,0:T(1,128)S(1)}) custom-call(f32[32,32,128]{2,1,0:T(8,128)S(1)} %bitcast.14, f32[128,1024]{1,0:T(8,128)S(1)} %get-tuple-element.10.fr_ref, f32[128,1024]{1,0:T(8,128)S(1)} %get-tuple-element.11.fc_ref, bf16[128,384]{1,0:T(8,128)(2,1)S(1)} %copy-done.7, bf16[512,256]{1,0:T(8,128)(2,1)S(1)} %copy-done.6), custom_call_target="tpu_custom_call" | custom-call | tf_op jit(solution)/shard_map/sum_decode/pallas_call | solution.py:259
  59.2 2.6 %collective-permute-start.9 = (f32[4]{0:T(128)S(1)}, f32[4]{0:T(128)S(1)}, u32[]{:S(2)}, u32[]{:S(2)}) collective-permute-start(f32[4]{0:T(128)S(1)} %reduce_sum.9), channel_id=1, source_target_pairs={{0,3},{1,2},{2,1},{3,0},{4,7},{5,6},{6,5},{7,4},{8,11},{9,10},{10,... | collective-permute-start | bytes 56 | tf_op jit(solution)/shard_map/ppermute | solution.py:305
  61.8 0.5 collective-permute-start.8
  62.9 2.8 %collective-permute-done.8 = f32[4]{0:T(128)S(1)} collective-permute-done((f32[4]{0:T(128)S(1)}, f32[4]{0:T(128)S(1)}, u32[]{:S(2)}, u32[]{:S(2)}) %collective-permute-start.8) | collective-permute-done | bytes 48 | tf_op jit(solution)/shard_map/ppermute | solution.py:305
  65.7 4.4 %collective-permute-start.10 = (f32[4]{0:T(128)S(1)}, f32[4]{0:T(128)S(1)}, u32[]{:S(2)}, u32[]{:S(2)}) collective-permute-start(f32[4]{0:T(128)S(1)} %add_add_fusion), channel_id=1, source_target_pairs={{0,4},{1,5},{2,6},{3,7},{4,0},{5,1},{6,2},{7,3},{8,12},{9,13},{10,... | collective-permute-start | bytes 56 | tf_op jit(solution)/shard_map/ppermute | solution.py:305
  70.0 2.0 %collective-permute-done.10 = f32[4]{0:T(128)S(1)} collective-permute-done((f32[4]{0:T(128)S(1)}, f32[4]{0:T(128)S(1)}, u32[]{:S(2)}, u32[]{:S(2)}) %collective-permute-start.10) | collective-permute-done | bytes 48 | tf_op jit(solution)/shard_map/ppermute | solution.py:305
  72.1 1.6 %broadcast_multiply_fusion = f32[4,128,1024]{2,1,0:T(8,128)} fusion(f32[4,128,1024]{2,1,0:T(8,128)S(1)} %get-tuple-element.12, f32[4]{0:T(128)S(1)} %add_rsqrt_fusion), kind=kLoop, calls=%fused_computation | loop fusion | flops 524288 | bytes 4194320 | tf_op jit(solution)/shard_map/mul | solution.py:308
  (33 shorter events, 1.2 us)
Async XLA Ops:
  0.6 1.6 %copy-start = (s32[32,4,2,16,32]{4,3,2,1,0:T(8,128)S(1)}, s32[32,4,2,16,32]{4,3,2,1,0:T(8,128)}, u32[]{:S(2)}) copy-start(s32[32,4,2,16,32]{4,3,2,1,0:T(8,128)} %param.8) | copy-start | bytes 1572868
  2.2 1.6 %copy-start.1 = (f32[1,4,128,1024]{3,2,1,0:T(8,128)S(1)}, f32[1,4,128,1024]{3,2,1,0:T(8,128)}, u32[]{:S(2)}) copy-start(f32[1,4,128,1024]{3,2,1,0:T(8,128)} %param.6) | copy-start | bytes 6291460
  3.8 1.2 %copy-start.3 = (bf16[1,4,128,1024]{3,2,1,0:T(8,128)(2,1)S(1)}, bf16[1,4,128,1024]{3,2,1,0:T(8,128)(2,1)}, u32[]{:S(2)}) copy-start(bf16[1,4,128,1024]{3,2,1,0:T(8,128)(2,1)} %param.7) | copy-start | bytes 3145732
  5.0 0.9 %copy-start.5 = (bf16[512,256]{1,0:T(8,128)(2,1)S(1)}, bf16[512,256]{1,0:T(8,128)(2,1)}, u32[]{:S(2)}) copy-start(bf16[512,256]{1,0:T(8,128)(2,1)} %constant.20.clone.cols_ref) | copy-start | bytes 786436
  6.0 0.9 %copy-start.8 = (bf16[128,384]{1,0:T(8,128)(2,1)S(1)}, bf16[128,384]{1,0:T(8,128)(2,1)}, u32[]{:S(2)}) copy-start(bf16[128,384]{1,0:T(8,128)(2,1)} %constant.19.clone.rows_ref) | copy-start | bytes 294916
  6.9 25.6 %copy-start.4 = (bf16[1,4,128,1024]{3,2,1,0:T(8,128)(2,1)S(1)}, bf16[1,4,128,1024]{3,2,1,0:T(8,128)(2,1)}, u32[]{:S(2)}) copy-start(bf16[1,4,128,1024]{3,2,1,0:T(8,128)(2,1)} %param.7) | copy-start | bytes 3145732
  12.0 20.4 %copy-start.2 = (f32[1,4,128,1024]{3,2,1,0:T(8,128)S(1)}, f32[1,4,128,1024]{3,2,1,0:T(8,128)}, u32[]{:S(2)}) copy-start(f32[1,4,128,1024]{3,2,1,0:T(8,128)} %param.6) | copy-start | bytes 6291460
  12.1 20.4 %copy-start.6 = (bf16[512,256]{1,0:T(8,128)(2,1)S(1)}, bf16[512,256]{1,0:T(8,128)(2,1)}, u32[]{:S(2)}) copy-start(bf16[512,256]{1,0:T(8,128)(2,1)} %constant.20.clone.cols_ref) | copy-start | bytes 786436
  12.1 20.4 %copy-start.7 = (bf16[128,384]{1,0:T(8,128)(2,1)S(1)}, bf16[128,384]{1,0:T(8,128)(2,1)}, u32[]{:S(2)}) copy-start(bf16[128,384]{1,0:T(8,128)(2,1)} %constant.21.clone.rows_ref) | copy-start | bytes 294916
  12.1 6.4 %collective-permute-start.2 = (f32[1,1,32,128]{3,2,1,0:T(8,128)S(1)}, f32[1,1,32,128]{3,2,1,0:T(8,128)S(1)}, u32[]{:S(2)}, u32[]{:S(2)}) collective-permute-start(f32[1,1,32,128]{3,2,1,0:T(8,128)S(1)} %bitcast.15), channel_id=1, source_target_pairs={{0,48},{8,56},{16,32},{24,40},{32,16},{40,24},{48,0},{56,8},{64,11... | collective-permute-start | bytes 49160 | tf_op jit(solution)/shard_map/ppermute | solution.py:282
  17.3 3.7 %collective-permute-start.1 = (f32[1,1,32,128]{3,2,1,0:T(8,128)S(1)}, f32[1,1,32,128]{3,2,1,0:T(8,128)S(1)}, u32[]{:S(2)}, u32[]{:S(2)}) collective-permute-start(f32[1,1,32,128]{3,2,1,0:T(8,128)S(1)} %bitcast.16), channel_id=1, source_target_pairs={{0,32},{8,40},{16,48},{24,56},{32,0},{40,8},{48,16},{56,24},{64,96... | collective-permute-start | bytes 49160 | tf_op jit(solution)/shard_map/ppermute | solution.py:282
  17.3 3.7 %collective-permute-start = (f32[1,1,32,128]{3,2,1,0:T(8,128)S(1)}, f32[1,1,32,128]{3,2,1,0:T(8,128)S(1)}, u32[]{:S(2)}, u32[]{:S(2)}) collective-permute-start(f32[1,1,32,128]{3,2,1,0:T(8,128)S(1)} %bitcast.17), channel_id=1, source_target_pairs={{0,16},{8,24},{16,0},{24,8},{32,48},{40,56},{48,32},{56,40},{64,80... | collective-permute-start | bytes 49160 | tf_op jit(solution)/shard_map/ppermute | solution.py:282
  21.0 7.5 %collective-permute-start.5 = (f32[4,1,32,128]{3,2,1,0:T(8,128)S(1)}, f32[4,1,32,128]{3,2,1,0:T(8,128)S(1)}, u32[]{:S(2)}, u32[]{:S(2)}) collective-permute-start(f32[4,1,32,128]{3,2,1,0:T(8,128)S(1)} %pad_maximum_fusion.1), channel_id=1, source_target_pairs={{0,192},{8,200},{16,208},{24,216},{32,224},{40,232},{48,240},{56,2... | collective-permute-start | bytes 196616 | tf_op jit(solution)/shard_map/ppermute | solution.py:282
  23.8 4.7 %collective-permute-start.4 = (f32[4,1,32,128]{3,2,1,0:T(8,128)S(1)}, f32[4,1,32,128]{3,2,1,0:T(8,128)S(1)}, u32[]{:S(2)}, u32[]{:S(2)}) collective-permute-start(f32[4,1,32,128]{3,2,1,0:T(8,128)S(1)} %pad_maximum_fusion.1), channel_id=1, source_target_pairs={{0,128},{8,136},{16,144},{24,152},{32,160},{40,168},{48,176},{56,1... | collective-permute-start | bytes 196616 | tf_op jit(solution)/shard_map/ppermute | solution.py:282
  24.2 3.4 %collective-permute-start.3 = (f32[4,1,32,128]{3,2,1,0:T(8,128)S(1)}, f32[4,1,32,128]{3,2,1,0:T(8,128)S(1)}, u32[]{:S(2)}, u32[]{:S(2)}) collective-permute-start(f32[4,1,32,128]{3,2,1,0:T(8,128)S(1)} %pad_maximum_fusion.1), channel_id=1, source_target_pairs={{0,64},{8,72},{16,80},{24,88},{32,96},{40,104},{48,112},{56,120},{... | collective-permute-start | bytes 196616 | tf_op jit(solution)/shard_map/ppermute | solution.py:282
  28.5 10.2 %collective-permute-start.6 = (f32[16,1,32,128]{3,2,1,0:T(8,128)S(1)}, f32[16,1,32,128]{3,2,1,0:T(8,128)S(1)}, u32[]{:S(2)}, u32[]{:S(2)}) collective-permute-start(f32[16,1,32,128]{3,2,1,0:T(8,128)S(1)} %constant_dynamic-update-slice_fusion), channel_id=1, source_target_pairs={{0,8},{8,0},{16,24},{24,16},{32,40},{40,32},{48,56},{56,48},{64,72... | collective-permute-start | bytes 786440 | tf_op jit(solution)/shard_map/ppermute | solution.py:282
  59.2 3.7 %collective-permute-start.9 = (f32[4]{0:T(128)S(1)}, f32[4]{0:T(128)S(1)}, u32[]{:S(2)}, u32[]{:S(2)}) collective-permute-start(f32[4]{0:T(128)S(1)} %reduce_sum.9), channel_id=1, source_target_pairs={{0,3},{1,2},{2,1},{3,0},{4,7},{5,6},{6,5},{7,4},{8,11},{9,10},{10,... | collective-permute-start | bytes 56 | tf_op jit(solution)/shard_map/ppermute | solution.py:305
  61.8 3.9 %collective-permute-start.8 = (f32[4]{0:T(128)S(1)}, f32[4]{0:T(128)S(1)}, u32[]{:S(2)}, u32[]{:S(2)}) collective-permute-start(f32[4]{0:T(128)S(1)} %reduce_sum.9), channel_id=1, source_target_pairs={{0,2},{1,3},{2,0},{3,1},{4,6},{5,7},{6,4},{7,5},{8,10},{9,11},{10,... | collective-permute-start | bytes 56 | tf_op jit(solution)/shard_map/ppermute | solution.py:305
  62.3 3.4 %collective-permute-start.7 = (f32[4]{0:T(128)S(1)}, f32[4]{0:T(128)S(1)}, u32[]{:S(2)}, u32[]{:S(2)}) collective-permute-start(f32[4]{0:T(128)S(1)} %reduce_sum.9), channel_id=1, source_target_pairs={{0,1},{1,0},{2,3},{3,2},{4,5},{5,4},{6,7},{7,6},{8,9},{9,8},{10,11... | collective-permute-start | bytes 56 | tf_op jit(solution)/shard_map/ppermute | solution.py:305
  65.7 6.4 %collective-permute-start.10 = (f32[4]{0:T(128)S(1)}, f32[4]{0:T(128)S(1)}, u32[]{:S(2)}, u32[]{:S(2)}) collective-permute-start(f32[4]{0:T(128)S(1)} %add_add_fusion), channel_id=1, source_target_pairs={{0,4},{1,5},{2,6},{3,7},{4,0},{5,1},{6,2},{7,3},{8,12},{9,13},{10,... | collective-permute-start | bytes 56 | tf_op jit(solution)/shard_map/ppermute | solution.py:305

commit v2 on v0

v2 whole, which is shorter than its diff:
```python
import math

import jax
import jax.numpy as jnp
import ml_dtypes
import numpy as np
from jax import lax
from jax.experimental import pallas as pl
from jax.experimental.pallas import tpu as pltpu
from jax.sharding import PartitionSpec as P

GROUP = 64
TOPK = 32
REPLICAS = 32
LAYERS = 4
ROWS = 128
COLS = 1024
TILES = COLS // 256
BLOCKS = 128
SET = 8
ENTRIES = 128 * 8192

decay_rate = 0.999
epsilon = 1e-06

BF = jnp.bfloat16
F32 = jnp.float32


def basis_matrix():
    f = np.arange(GROUP, dtype=np.float64)[:, None]
    n = np.arange(GROUP, dtype=np.float64)[None, :]
    scale = np.where(f == 0, math.sqrt(1.0 / GROUP), math.sqrt(2.0 / GROUP))
    return scale * np.cos(math.pi * (2.0 * n + 1.0) * f / (2.0 * GROUP))


def halves(x):
    x = x.astype(np.float32)
    hi = x.astype(ml_dtypes.bfloat16)
    lo = (x - hi.astype(np.float32)).astype(ml_dtypes.bfloat16)
    return hi, lo


def constants():
    b = basis_matrix()
    two, four = np.kron(np.eye(2), b), np.kron(np.eye(4), b)
    t_hi, t_lo = halves(two.T)
    none = np.zeros_like(t_lo)
    forward_cols = np.concatenate(halves(four.T), axis=0)
    forward_rows = np.block([[t_hi, t_lo], [t_hi, none]])
    back_cols = np.concatenate(halves(four), axis=0)
    back_rows = np.block([[t_hi, t_hi], [t_lo, none]])
    return forward_cols, forward_rows, back_cols, back_rows


def split(x):
    hi = x.astype(BF)
    return hi, (x - hi.astype(F32)).astype(BF)


def mm(a, b):
    return jnp.dot(a, b, preferred_element_type=F32)


def mm_t(a, b):
    return lax.dot_general(a, b, (((1,), (1,)), ((), ())), preferred_element_type=F32)


def cols_apply(x, cols):
    n = x.shape[0]
    hi, lo = split(x)
    both = mm(jnp.concatenate([hi, lo], axis=0), cols[:256])
    return both[:n] + both[n:] + mm(hi, cols[256:])


def back(grids, cols, rows):
    half = cols_apply(jnp.concatenate(grids, axis=0), cols)
    out = []
    for t in range(TILES):
        hi, lo = split(half[t * 128 : t * 128 + 128])
        both = mm(rows, jnp.concatenate([hi, lo], axis=0))
        out.append(both[:128] + both[128:])
    return out


def lane_block(shape):
    return lax.shift_right_logical(lax.broadcasted_iota(jnp.int32, shape, len(shape) - 1), 5) & 3


def pick_kernel(m_hbm, g_hbm, idx_hbm, cols_hbm, rows_hbm, v_ref, own_ref, m_buf, g_buf, idx_buf, cols_ref, rows_ref, sems):
    p = lax.axis_index("dp")
    copies = [pltpu.make_async_copy(idx_hbm.at[pl.ds(p * BLOCKS, BLOCKS)], idx_buf, sems.at[0])]
    copies += [pltpu.make_async_copy(cols_hbm, cols_ref, sems.at[1])]
    copies += [pltpu.make_async_copy(rows_hbm, rows_ref, sems.at[2])]
    for l in range(LAYERS):
        copies.append(pltpu.make_async_copy(m_hbm.at[l], m_buf.at[l], sems.at[3 + 2 * l]))
        copies.append(pltpu.make_async_copy(g_hbm.at[l], g_buf.at[l], sems.at[4 + 2 * l]))
    order = [3, 4, 1, 0, 2] + list(range(5, 3 + 2 * LAYERS))
    for i in order:
        copies[i].start()
    for i in range(3):
        copies[i].wait()
    own_ref[...] = jnp.concatenate([idx_buf[pl.ds(cj, 32, stride=4), :] for cj in range(4)], axis=1)
    freq = lax.broadcasted_iota(jnp.int32, (GROUP, 128), 0)
    place = lax.broadcasted_iota(jnp.int32, (256, 256), 0)
    zeros = jnp.zeros((GROUP, 128), BF)
    for l in range(LAYERS):
        copies[3 + 2 * l].wait()
        copies[4 + 2 * l].wait()
        acc = decay_rate * m_buf[l] + g_buf[l].astype(F32)
        tiles = jnp.concatenate([acc[:, t * 256 : t * 256 + 256] for t in range(TILES)], axis=0)
        half = cols_apply(tiles, cols_ref)
        for t in range(TILES):
            hi, lo = split(half[t * 128 : t * 128 + 128].T)
            both = mm(jnp.concatenate([hi, lo], axis=1), rows_ref[...])
            hi, lo = split(both[:, :128] + both[:, 128:])
            pos = [own_ref[pl.ds(l * 8 + a * 4 + t, 1), :] for a in range(2)]
            hot = [(freq == lax.shift_right_logical(x, 6)).astype(F32).astype(BF) for x in pos]
            pick = jnp.concatenate(
                [
                    jnp.concatenate([hot[0], zeros], axis=1),
                    jnp.concatenate([zeros, hot[1]], axis=1),
                ],
                axis=0,
            )
            got = mm(jnp.concatenate([hi, lo], axis=1), jnp.concatenate([pick, pick], axis=0))
            where = jnp.concatenate([(x & 63) + 64 * lane_block((1, 128)) for x in pos], axis=1)
            v = jnp.sum(jnp.where(place == where, got, 0.0), axis=0, keepdims=True)
            for a in range(2):
                v_ref[pl.ds(l * 8 + a * 4 + t, 1), :] = v[:, a * 128 : a * 128 + 128]


def own_kernel(m_ref, g_ref, own_ref, v_ref, cols_ref, rows_ref, out_hbm, out_buf, sems):
    freq = lax.broadcasted_iota(jnp.int32, (GROUP, 128), 0)
    place = lax.broadcasted_iota(jnp.int32, (256, 128), 0)
    copies = []
    for l in range(LAYERS):
        grids = []
        for t in range(TILES):
            parts = []
            for a in range(2):
                row = l * 8 + a * 4 + t
                pos = own_ref[pl.ds(row, 1), :]
                v = v_ref[pl.ds(row, 1), :]
                hi, lo = split(jnp.where(freq == lax.shift_right_logical(pos, 6), v, 0.0))
                right = (place == (pos & 63) + 64 * lane_block((1, 128))).astype(F32).astype(BF)
                both = mm_t(jnp.concatenate([hi, lo], axis=0), right)
                parts.append(both[:GROUP] + both[GROUP:])
            grids.append(jnp.concatenate(parts, axis=0))
        for t, tile in enumerate(back(grids, cols_ref, rows_ref[...])):
            s = slice(t * 256, t * 256 + 256)
            acc = decay_rate * m_ref[l, :, s] + g_ref[l, :, s].astype(F32)
            out_buf[l, :, s] = acc - tile
        copies.append(pltpu.make_async_copy(out_buf.at[l], out_hbm.at[l], sems.at[l]))
        copies[-1].start()
    for copy in copies:
        copy.wait()


def arrange_kernel(idx_ref, fr_ref, fc_ref):
    p = lax.axis_index("dp")
    for q in range(REPLICAS // 4):
        pos = jnp.concatenate([idx_ref[pl.ds((p ^ (4 * q + j)) * BLOCKS, BLOCKS), :] for j in range(4)], axis=1)
        fr_ref[:, q * 128 : q * 128 + 128] = lax.shift_right_logical(pos, 6).astype(F32)
        fc_ref[:, q * 128 : q * 128 + 128] = (pos & 63).astype(F32)


def set_kernel(number, first, last, v_ref, fr_ref, fc_ref, *rest):
    old_ref = None
    if not first:
        old_ref, rest = rest[0], rest[1:]
    if last:
        grid_ref, sq_ref, val_ref = rest
        sq_ref[...] = jnp.zeros_like(sq_ref)
    else:
        grid_ref, val_ref = rest
    lane = lane_block((32, 128))
    for q in range(SET // 4):
        x = [v_ref[4 * q + j] for j in range(4)]
        for cj in range(4):
            y = jnp.zeros((32, 128), F32)
            for j in range(4):
                moved = x[j] if j == cj else pltpu.roll(x[j], ((j - cj) * 32) % 128, 1)
                y = jnp.where(lane == j, moved, y)
            val_ref[cj, :, q * 128 : q * 128 + 128] = y
    wide = 32 * SET
    freq = lax.broadcasted_iota(jnp.int32, (GROUP, wide), 0).astype(F32).astype(BF)
    s = slice(number * wide, number * wide + wide)
    zero, one = jnp.zeros((), BF), jnp.ones((), BF)

    def body(l, carry):
        squares = jnp.zeros((1, 256), F32)
        for i in range(2 * TILES):
            a, t = i // TILES, i % TILES
            parts = []
            for cj in range(4):
                row = l * 32 + i * 4 + cj
                fr = fr_ref[pl.ds(row, 1), s].astype(BF)
                fc = fc_ref[pl.ds(row, 1), s].astype(BF)
                hi, lo = split(val_ref[cj, pl.ds(l * 8 + i, 1), :])
                at = freq == fr
                left = jnp.concatenate([jnp.where(at, hi, zero), jnp.where(at, lo, zero)], axis=0)
                both = mm_t(left, jnp.where(freq == fc, one, zero))
                parts.append(both[:GROUP] + both[GROUP:])
            grid = jnp.concatenate(parts, axis=1)
            if old_ref is not None:
                grid = grid + old_ref[l, t, a * GROUP : a * GROUP + GROUP, :]
            grid_ref[l, t, a * GROUP : a * GROUP + GROUP, :] = grid
            if last:
                squares = squares + jnp.sum(grid * grid, axis=0, keepdims=True)
        if last:
            sq_ref[pl.ds(l, 1), :] = squares[:, :128] + squares[:, 128:]
        return carry

    lax.fori_loop(0, LAYERS, body, 0)


def decode_kernel(grid_ref, cols_ref, rows_ref, out_ref):
    def body(l, carry):
        tiles = back([grid_ref[l, t] for t in range(TILES)], cols_ref, rows_ref[...])
        for t, tile in enumerate(tiles):
            out_ref[l, :, t * 256 : t * 256 + 256] = tile
        return carry

    lax.fori_loop(0, LAYERS, body, 0)


def scale_kernel(x_ref, a_ref, b_ref, out_hbm, out_buf, sems):
    total = jnp.sum(a_ref[...] + b_ref[...], axis=1, keepdims=True)
    factor = lax.rsqrt(jnp.broadcast_to(total, (8, 128)) / ENTRIES + epsilon)
    copies = []
    for l in range(LAYERS):
        row = factor[l : l + 1]
        for t in range(COLS // 128):
            s = slice(t * 128, t * 128 + 128)
            out_buf[l, :, s] = x_ref[l, :, s] * row
        copies.append(pltpu.make_async_copy(out_buf.at[l], out_hbm.at[l], sems.at[l]))
        copies[-1].start()
    for copy in copies:
        copy.wait()


VM = pl.BlockSpec(memory_space=pltpu.VMEM)
HB = pl.BlockSpec(memory_space=pltpu.HBM)
DECODED = jax.ShapeDtypeStruct((LAYERS, ROWS, COLS), F32)
GRIDS = jax.ShapeDtypeStruct((LAYERS, TILES, 128, 256), F32)


def call(kernel, name, ins, outs, shapes, scratch=(), us=1.0, mib=32, **more):
    return pl.pallas_call(
        kernel,
        in_specs=ins,
        out_specs=outs,
        out_shape=shapes,
        scratch_shapes=list(scratch),
        compiler_params=pltpu.CompilerParams(vmem_limit_bytes=mib * 2**20),
        cost_estimate=pl.CostEstimate(flops=int(us * 1e9), bytes_accessed=int(us * 2e6), transcendentals=0),
        name=name,
        **more,
    )


def pick(m, g, idx, cols, rows):
    return call(
        pick_kernel,
        "pick",
        [HB] * 5,
        [VM] * 2,
        [jax.ShapeDtypeStruct((32, 128), F32), jax.ShapeDtypeStruct((32, 128), jnp.int32)],
        [
            pltpu.VMEM((LAYERS, ROWS, COLS), F32),
            pltpu.VMEM((LAYERS, ROWS, COLS), BF),
            pltpu.VMEM((BLOCKS, TOPK), jnp.int32),
            pltpu.VMEM(cols.shape, BF),
            pltpu.VMEM(rows.shape, BF),
            pltpu.SemaphoreType.DMA((3 + 2 * LAYERS,)),
        ],
        4.0,
        60,
    )(m, g, idx, cols, rows)


def own_update(m, g, own, v, cols, rows):
    return call(
        own_kernel,
        "own",
        [VM] * 6,
        HB,
        DECODED,
        [pltpu.VMEM((LAYERS, ROWS, COLS), F32), pltpu.SemaphoreType.DMA((LAYERS,))],
        3.0,
    )(m, g, own, v, cols, rows)


def arrange(idx):
    shape = jax.ShapeDtypeStruct((BLOCKS, 1024), F32)
    return call(arrange_kernel, "arrange", [VM], [VM, VM], [shape, shape], (), 0.5)(idx)


def add_set(number, last, v, fr, fc, old):
    ins, outs, shapes, more = [v, fr, fc], [VM], [GRIDS], {}
    first = old is None
    if not first:
        ins.append(old)
        more = dict(input_output_aliases={3: 0})
    if last:
        outs.append(VM)
        shapes.append(jax.ShapeDtypeStruct((8, 128), F32))
    return call(
        lambda *refs: set_kernel(number, first, last, *refs),
        f"set{number}",
        [VM] * len(ins),
        outs,
        shapes,
        [pltpu.VMEM((4, 32, 32 * SET), F32)],
        2.6,
        **more,
    )(*ins)


def decode(grid, cols, rows):
    return call(decode_kernel, "decode", [VM] * 3, VM, DECODED, (), 3.0)(grid, cols, rows)


def rescale(x, a, b):
    return call(
        scale_kernel,
        "rescale",
        [VM] * 3,
        HB,
        DECODED,
        [pltpu.VMEM((LAYERS, ROWS, COLS), F32), pltpu.SemaphoreType.DMA((LAYERS,))],
        1.0,
    )(x, a, b)


def turn(x, axis, size, bit):
    return lax.ppermute(x, axis, [(i, i ^ bit) for i in range(size)])


def on_device(momentum, gradient, kept_index):
    m, g = momentum[0], gradient[0]
    idx = kept_index.reshape(REPLICAS * BLOCKS, TOPK)
    forward_cols, forward_rows, back_cols, back_rows = (jnp.asarray(x) for x in constants())
    v, own = pick(m, g, idx, forward_cols, forward_rows)

    x = jnp.stack([v, turn(v, "dp", REPLICAS, 1)])
    x = jnp.concatenate([x] + [turn(x, "dp", REPLICAS, b) for b in (2, 4, 6)], axis=0)
    order = (0, 1, 3, 2)
    sets = {s: x if s == 0 else turn(x, "dp", REPLICAS, 8 * s) for s in order}
    fr, fc = arrange(idx)
    momentum_out = own_update(m, g, own, v, back_cols, back_rows)
    grid = None
    for s in order[:-1]:
        (grid,) = add_set(s, False, sets[s], fr, fc, grid)
    grid, squares = add_set(order[-1], True, sets[order[-1]], fr, fc, grid)

    total = squares
    for b in (1, 3):
        total = total + turn(total, "tensor", 8, b)
    other = turn(total, "tensor", 8, 4)
    decoded = decode(grid, back_cols, back_rows)
    update = rescale(decoded, total, other)
    return (momentum_out[None], update)


def solution(mesh):
    placed = (
        P("dp", None, None, "tensor"),
        P("dp", None, None, "tensor"),
        P(None, None, None, "tensor", None),
    )
    return jax.shard_map(
        on_device,
        mesh=mesh,
        in_specs=placed,
        out_specs=(P("dp", None, None, "tensor"), P(None, None, "tensor")),
        check_vma=False,
    )
```

time: 462 us -> 58.4 us (0.13)
  the two profiles are of different devices: /device:TPU:1 before, /device:TPU:16 now
where the time goes in v2:
time: 58.4 us; the launch traced here: 58.2 us
  Pallas kernels  30.2 us (52%)
  starting transfers between devices  18.3 us (31%)
  waiting for transfers between devices  7.98 us (14%)
  between operations  1 us (2%)
  local copies, waits for them, and re-layouts  0.78 us (1%)
    ppermute x10, starting transfers between devices, turn(): return lax.ppermute(x, axis, [(i, i ^ bit) for i in range(size)])  18.3 us
    pallas_call x4, Pallas kernels, add_set(): call(lambda *refs: set_kernel(number, first, last, *refs), f'set{number}'...  13.2 us
    ppermute x10, waiting for transfers between devices, turn(): return lax.ppermute(x, axis, [(i, i ^ bit) for i in range(size)])  7.98 us
    pallas_call x1, Pallas kernels, pick(): call(pick_kernel, 'pick', [HB] * 5, [VM] * 2, [jax.ShapeDtypeStruct((32,...  7.23 us
    pallas_call x1, Pallas kernels, own_update(): call(own_kernel, 'own', [VM] * 6, HB, DECODED, [pltpu.VMEM((LAYERS, ROWS,...  4.53 us
    pallas_call x1, Pallas kernels, decode(): call(decode_kernel, 'decode', [VM] * 3, VM, DECODED, (), 3.0)  3.25 us
    pallas_call x1, Pallas kernels, rescale(): call(scale_kernel, 'rescale', [VM] * 3, HB, DECODED, [pltpu.VMEM((LAYERS,...  1.49 us
  transfers between devices with their start and end apart: 10, of which 4 were waited for; matrix products, arithmetic and copies ran while one was open for 1% of the time, Pallas kernels for 31%

profile of v2, /device:TPU:16, one launch (start us, length us, event | category | flops | bytes accessed | tf_op | source)
XLA Modules:
  0.0 58.2 jit_solution(14937566942163356749)
XLA Ops:
  0.6 7.2 %pick.1 = (f32[32,128]{1,0:T(8,128)}, s32[32,128]{1,0:T(8,128)}) custom-call(f32[4,128,1024]{2,1,0:T(8,128)} %bitcast.11, bf16[4,128,1024]{2,1,0:T(8,128)(2,1)} %bitcast.13, s32[4096,32]{1,0:T(8,128)} %bitcast.8, bf16[512,256]{1,0:T(8,128)(2,1)} %constant.8.clone.cols_hbm, bf16[256,256]{1,0:T(8,128)(2,1)} %constant.9.clone.rows_hbm), custom_call_target="tpu_custom_call" | custom-call | flops 4000000000 | bytes 8000000 | tf_op jit(solution)/shard_map/pick/pallas_call | solution.py:264
  7.9 0.1 collective-permute-start
  8.0 0.7 %constant_dynamic-update-slice_fusion.4 = f32[8,32,128]{2,1,0:T(8,128)S(1)} fusion(f32[32,128]{1,0:T(8,128)} %get-tuple-element.9.v_ref), kind=kLoop, calls=%fused_computation.5 | loop fusion | bytes 32768
  8.7 0.5 arrange.1
  9.2 0.2 collective-permute-done
  9.4 1.9 %collective-permute-start.1 = (f32[2,32,128]{2,1,0:T(8,128)S(1)}, f32[2,32,128]{2,1,0:T(8,128)S(1)}, u32[]{:S(2)}, u32[]{:S(2)}) collective-permute-start(f32[2,32,128]{2,1,0:T(8,128)S(1)} %pad_maximum_fusion), channel_id=1, source_target_pairs={{0,16},{8,24},{16,0},{24,8},{32,48},{40,56},{48,32},{56,40},{64,80... | collective-permute-start | bytes 98312 | tf_op jit(solution)/shard_map/ppermute | solution.py:338
  11.3 3.3 %collective-permute-start.2 = (f32[2,32,128]{2,1,0:T(8,128)S(1)}, f32[2,32,128]{2,1,0:T(8,128)S(1)}, u32[]{:S(2)}, u32[]{:S(2)}) collective-permute-start(f32[2,32,128]{2,1,0:T(8,128)S(1)} %pad_maximum_fusion), channel_id=1, source_target_pairs={{0,32},{8,40},{16,48},{24,56},{32,0},{40,8},{48,16},{56,24},{64,96... | collective-permute-start | bytes 98312 | tf_op jit(solution)/shard_map/ppermute | solution.py:338
  14.6 2.5 %collective-permute-done.2 = f32[2,32,128]{2,1,0:T(8,128)S(1)} collective-permute-done((f32[2,32,128]{2,1,0:T(8,128)S(1)}, f32[2,32,128]{2,1,0:T(8,128)S(1)}, u32[]{:S(2)}, u32[]{:S(2)}) %collective-permute-start.2) | collective-permute-done | bytes 32800 | tf_op jit(solution)/shard_map/ppermute | solution.py:338
  17.1 3.2 %collective-permute-done.3 = f32[2,32,128]{2,1,0:T(8,128)S(1)} collective-permute-done((f32[2,32,128]{2,1,0:T(8,128)S(1)}, f32[2,32,128]{2,1,0:T(8,128)S(1)}, u32[]{:S(2)}, u32[]{:S(2)}) %collective-permute-start.3) | collective-permute-done | bytes 32800 | tf_op jit(solution)/shard_map/ppermute | solution.py:338
  20.3 1.3 %collective-permute-start.6 = (f32[8,32,128]{2,1,0:T(8,128)S(1)}, f32[8,32,128]{2,1,0:T(8,128)S(1)}, u32[]{:S(2)}, u32[]{:S(2)}) collective-permute-start(f32[8,32,128]{2,1,0:T(8,128)S(1)} %constant_dynamic-update-slice_fusion.refs_0_), channel_id=1, source_target_pairs={{0,64},{8,72},{16,80},{24,88},{32,96},{40,104},{48,112},{56,120},{... | collective-permute-start | bytes 393224 | tf_op jit(solution)/shard_map/ppermute | solution.py:338
  21.6 2.8 %collective-permute-start.4 = (f32[8,32,128]{2,1,0:T(8,128)S(1)}, f32[8,32,128]{2,1,0:T(8,128)S(1)}, u32[]{:S(2)}, u32[]{:S(2)}) collective-permute-start(f32[8,32,128]{2,1,0:T(8,128)S(1)} %constant_dynamic-update-slice_fusion.refs_0_), channel_id=1, source_target_pairs={{0,128},{8,136},{16,144},{24,152},{32,160},{40,168},{48,176},{56,1... | collective-permute-start | bytes 393224 | tf_op jit(solution)/shard_map/ppermute | solution.py:338
  24.4 3.3 %set0.1.refs_3_ = f32[4,4,128,256]{3,2,1,0:T(8,128)S(1)} custom-call(f32[8,32,128]{2,1,0:T(8,128)S(1)} %constant_dynamic-update-slice_fusion.refs_0_, f32[128,1024]{1,0:T(8,128)S(1)} %get-tuple-element.10.refs_1_, f32[128,1024]{1,0:T(8,128)S(1)} %get-tuple-element.11.refs_2_), custom_call_target="tpu_custom_call" | custom-call | flops 2600000000 | bytes 5200000 | tf_op jit(solution)/shard_map/set0/pallas_call | solution.py:309
  27.7 3.3 %set1.1.refs_3_ = f32[4,4,128,256]{3,2,1,0:T(8,128)S(1)} custom-call(f32[8,32,128]{2,1,0:T(8,128)S(1)} %collective-permute-done.6.refs_0_, f32[128,1024]{1,0:T(8,128)S(1)} %get-tuple-element.10.refs_1_, f32[128,1024]{1,0:T(8,128)S(1)} %get-tuple-element.11.refs_2_, f32[4,4,128,256]{3,2,1,0:T(8,128)S(1)} %set0.1.refs_3_), custom_call_target="tpu_custom_call", output_to_operand_aliasing={{}: (3, {})} | custom-call | flops 2600000000 | bytes 5200000 | tf_op jit(solution)/shard_map/set1/pallas_call | solution.py:309
  31.0 3.3 %set3.1.refs_3_ = f32[4,4,128,256]{3,2,1,0:T(8,128)S(1)} custom-call(f32[8,32,128]{2,1,0:T(8,128)S(1)} %collective-permute-done.5.refs_0_, f32[128,1024]{1,0:T(8,128)S(1)} %get-tuple-element.10.refs_1_, f32[128,1024]{1,0:T(8,128)S(1)} %get-tuple-element.11.refs_2_, f32[4,4,128,256]{3,2,1,0:T(8,128)S(1)} %set1.1.refs_3_), custom_call_target="tpu_custom_call", output_to_operand_aliasing={{}: (3, {})} | custom-call | flops 2600000000 | bytes 5200000 | tf_op jit(solution)/shard_map/set3/pallas_call | solution.py:309
  34.3 0.0 copy-start.4
  34.3 0.0 copy-start.5
  34.3 3.3 %set2.1 = (f32[4,4,128,256]{3,2,1,0:T(8,128)S(1)}, f32[8,128]{1,0:T(8,128)S(1)}) custom-call(f32[8,32,128]{2,1,0:T(8,128)S(1)} %collective-permute-done.4.refs_0_, f32[128,1024]{1,0:T(8,128)S(1)} %get-tuple-element.10.refs_1_, f32[128,1024]{1,0:T(8,128)S(1)} %get-tuple-element.11.refs_2_, ...), custom_call_target="tpu_custom_call", output_to_operand_aliasing={{0}: (3, {})} | custom-call | flops 2600000000 | bytes 5200000 | tf_op jit(solution)/shard_map/set2/pallas_call | solution.py:309
  37.7 1.6 %collective-permute-start.7 = (f32[8,128]{1,0:T(8,128)S(1)}, f32[8,128]{1,0:T(8,128)S(1)}, u32[]{:S(2)}, u32[]{:S(2)}) collective-permute-start(f32[8,128]{1,0:T(8,128)S(1)} %get-tuple-element.13), channel_id=1, source_target_pairs={{0,1},{1,0},{2,3},{3,2},{4,5},{5,4},{6,7},{7,6},{8,9},{9,8},{10,11... | collective-permute-start | bytes 12296 | tf_op jit(solution)/shard_map/ppermute | solution.py:338
  39.3 2.1 %collective-permute-done.7 = f32[8,128]{1,0:T(8,128)S(1)} collective-permute-done((f32[8,128]{1,0:T(8,128)S(1)}, f32[8,128]{1,0:T(8,128)S(1)}, u32[]{:S(2)}, u32[]{:S(2)}) %collective-permute-start.7) | collective-permute-done | bytes 4128 | tf_op jit(solution)/shard_map/ppermute | solution.py:338
  41.4 2.8 %collective-permute-start.8 = (f32[8,128]{1,0:T(8,128)S(1)}, f32[8,128]{1,0:T(8,128)S(1)}, u32[]{:S(2)}, u32[]{:S(2)}) collective-permute-start(f32[8,128]{1,0:T(8,128)S(1)} %add.6), channel_id=1, source_target_pairs={{0,3},{1,2},{2,1},{3,0},{4,7},{5,6},{6,5},{7,4},{8,11},{9,10},{10,... | collective-permute-start | bytes 12296 | tf_op jit(solution)/shard_map/ppermute | solution.py:338
  44.2 4.5 %own.1 = f32[4,128,1024]{2,1,0:T(8,128)} custom-call(f32[4,128,1024]{2,1,0:T(8,128)S(1)} %bitcast.12, bf16[4,128,1024]{2,1,0:T(8,128)(2,1)S(1)} %bitcast.14, s32[32,128]{1,0:T(8,128)S(1)} %copy-done.6, f32[32,128]{1,0:T(8,128)S(1)} %copy-done.1, bf16[512,256]{1,0:T(8,128)(2,1)S(1)} %copy-done.4, bf16[256,256]{1,0:T(8,128)(2,1)S(1)} %copy-done.5), custom_call_target="tpu_custom_call" | custom-call | flops 3000000000 | bytes 6000000 | tf_op jit(solution)/shard_map/own/pallas_call | solution.py:284
  48.7 4.6 %collective-permute-start.9 = (f32[8,128]{1,0:T(8,128)S(1)}, f32[8,128]{1,0:T(8,128)S(1)}, u32[]{:S(2)}, u32[]{:S(2)}) collective-permute-start(f32[8,128]{1,0:T(8,128)S(1)} %add.7.a_ref), channel_id=1, source_target_pairs={{0,4},{1,5},{2,6},{3,7},{4,0},{5,1},{6,2},{7,3},{8,12},{9,13},{10,... | collective-permute-start | bytes 12296 | tf_op jit(solution)/shard_map/ppermute | solution.py:338
  53.3 3.3 %decode.1.x_ref = f32[4,128,1024]{2,1,0:T(8,128)S(1)} custom-call(f32[4,4,128,256]{3,2,1,0:T(8,128)S(1)} %get-tuple-element.12.grid_ref, bf16[512,256]{1,0:T(8,128)(2,1)S(1)} %copy-done.4, bf16[256,256]{1,0:T(8,128)(2,1)S(1)} %copy-done.5), custom_call_target="tpu_custom_call" | custom-call | flops 3000000000 | bytes 6000000 | tf_op jit(solution)/shard_map/decode/pallas_call | solution.py:322
  56.6 1.5 %rescale.1 = f32[4,128,1024]{2,1,0:T(8,128)} custom-call(f32[4,128,1024]{2,1,0:T(8,128)S(1)} %decode.1.x_ref, f32[8,128]{1,0:T(8,128)S(1)} %add.7.a_ref, f32[8,128]{1,0:T(8,128)S(1)} %collective-permute-done.9.b_ref), custom_call_target="tpu_custom_call" | custom-call | flops 1000000000 | bytes 2000000 | tf_op jit(solution)/shard_map/rescale/pallas_call | solution.py:326
  (27 shorter events, 0.1 us)
Async XLA Ops:
  0.6 8.1 %copy-start = (s32[32,4,2,16,32]{4,3,2,1,0:T(8,128)S(1)}, s32[32,4,2,16,32]{4,3,2,1,0:T(8,128)}, u32[]{:S(2)}) copy-start(s32[32,4,2,16,32]{4,3,2,1,0:T(8,128)} %param.9) | copy-start | bytes 1572868
  7.9 1.5 %copy-start.1 = (f32[32,128]{1,0:T(8,128)S(1)}, f32[32,128]{1,0:T(8,128)}, u32[]{:S(2)}) copy-start(f32[32,128]{1,0:T(8,128)} %get-tuple-element.9.v_ref) | copy-start | bytes 49156
  7.9 1.5 %collective-permute-start = (f32[32,128]{1,0:T(8,128)}, f32[32,128]{1,0:T(8,128)S(1)}, u32[]{:S(2)}, u32[]{:S(2)}) collective-permute-start(f32[32,128]{1,0:T(8,128)} %get-tuple-element.9.v_ref), channel_id=1, source_target_pairs={{0,8},{8,0},{16,24},{24,16},{32,40},{40,32},{48,56},{56,48},{64,72... | collective-permute-start | bytes 49160 | tf_op jit(solution)/shard_map/ppermute | solution.py:338
  9.4 5.2 %collective-permute-start.1 = (f32[2,32,128]{2,1,0:T(8,128)S(1)}, f32[2,32,128]{2,1,0:T(8,128)S(1)}, u32[]{:S(2)}, u32[]{:S(2)}) collective-permute-start(f32[2,32,128]{2,1,0:T(8,128)S(1)} %pad_maximum_fusion), channel_id=1, source_target_pairs={{0,16},{8,24},{16,0},{24,8},{32,48},{40,56},{48,32},{56,40},{64,80... | collective-permute-start | bytes 98312 | tf_op jit(solution)/shard_map/ppermute | solution.py:338
  11.3 5.8 %collective-permute-start.2 = (f32[2,32,128]{2,1,0:T(8,128)S(1)}, f32[2,32,128]{2,1,0:T(8,128)S(1)}, u32[]{:S(2)}, u32[]{:S(2)}) collective-permute-start(f32[2,32,128]{2,1,0:T(8,128)S(1)} %pad_maximum_fusion), channel_id=1, source_target_pairs={{0,32},{8,40},{16,48},{24,56},{32,0},{40,8},{48,16},{56,24},{64,96... | collective-permute-start | bytes 98312 | tf_op jit(solution)/shard_map/ppermute | solution.py:338
  14.6 5.7 %collective-permute-start.3 = (f32[2,32,128]{2,1,0:T(8,128)S(1)}, f32[2,32,128]{2,1,0:T(8,128)S(1)}, u32[]{:S(2)}, u32[]{:S(2)}) collective-permute-start(f32[2,32,128]{2,1,0:T(8,128)S(1)} %pad_maximum_fusion), channel_id=1, source_target_pairs={{0,48},{8,56},{16,32},{24,40},{32,16},{40,24},{48,0},{56,8},{64,11... | collective-permute-start | bytes 98312 | tf_op jit(solution)/shard_map/ppermute | solution.py:338
  20.3 7.4 %collective-permute-start.6 = (f32[8,32,128]{2,1,0:T(8,128)S(1)}, f32[8,32,128]{2,1,0:T(8,128)S(1)}, u32[]{:S(2)}, u32[]{:S(2)}) collective-permute-start(f32[8,32,128]{2,1,0:T(8,128)S(1)} %constant_dynamic-update-slice_fusion.refs_0_), channel_id=1, source_target_pairs={{0,64},{8,72},{16,80},{24,88},{32,96},{40,104},{48,112},{56,120},{... | collective-permute-start | bytes 393224 | tf_op jit(solution)/shard_map/ppermute | solution.py:338
  21.6 9.4 %collective-permute-start.5 = (f32[8,32,128]{2,1,0:T(8,128)S(1)}, f32[8,32,128]{2,1,0:T(8,128)S(1)}, u32[]{:S(2)}, u32[]{:S(2)}) collective-permute-start(f32[8,32,128]{2,1,0:T(8,128)S(1)} %constant_dynamic-update-slice_fusion.refs_0_), channel_id=1, source_target_pairs={{0,192},{8,200},{16,208},{24,216},{32,224},{40,232},{48,240},{56,2... | collective-permute-start | bytes 393224 | tf_op jit(solution)/shard_map/ppermute | solution.py:338
  21.6 12.8 %collective-permute-start.4 = (f32[8,32,128]{2,1,0:T(8,128)S(1)}, f32[8,32,128]{2,1,0:T(8,128)S(1)}, u32[]{:S(2)}, u32[]{:S(2)}) collective-permute-start(f32[8,32,128]{2,1,0:T(8,128)S(1)} %constant_dynamic-update-slice_fusion.refs_0_), channel_id=1, source_target_pairs={{0,128},{8,136},{16,144},{24,152},{32,160},{40,168},{48,176},{56,1... | collective-permute-start | bytes 393224 | tf_op jit(solution)/shard_map/ppermute | solution.py:338
  34.3 9.9 %copy-start.2 = (f32[1,4,128,1024]{3,2,1,0:T(8,128)S(1)}, f32[1,4,128,1024]{3,2,1,0:T(8,128)}, u32[]{:S(2)}) copy-start(f32[1,4,128,1024]{3,2,1,0:T(8,128)} %param.7) | copy-start | bytes 6291460
  34.3 9.9 %copy-start.3 = (bf16[1,4,128,1024]{3,2,1,0:T(8,128)(2,1)S(1)}, bf16[1,4,128,1024]{3,2,1,0:T(8,128)(2,1)}, u32[]{:S(2)}) copy-start(bf16[1,4,128,1024]{3,2,1,0:T(8,128)(2,1)} %param.8) | copy-start | bytes 3145732
  34.3 9.9 %copy-start.4 = (bf16[512,256]{1,0:T(8,128)(2,1)S(1)}, bf16[512,256]{1,0:T(8,128)(2,1)}, u32[]{:S(2)}) copy-start(bf16[512,256]{1,0:T(8,128)(2,1)} %constant.10.clone.cols_ref) | copy-start | bytes 786436
  34.3 9.9 %copy-start.5 = (bf16[256,256]{1,0:T(8,128)(2,1)S(1)}, bf16[256,256]{1,0:T(8,128)(2,1)}, u32[]{:S(2)}) copy-start(bf16[256,256]{1,0:T(8,128)(2,1)} %constant.11.clone.rows_ref) | copy-start | bytes 393220
  34.3 9.8 %copy-start.6 = (s32[32,128]{1,0:T(8,128)S(1)}, s32[32,128]{1,0:T(8,128)}, u32[]{:S(2)}) copy-start(s32[32,128]{1,0:T(8,128)} %get-tuple-element.8.own_ref) | copy-start | bytes 49156
  37.7 3.7 %collective-permute-start.7 = (f32[8,128]{1,0:T(8,128)S(1)}, f32[8,128]{1,0:T(8,128)S(1)}, u32[]{:S(2)}, u32[]{:S(2)}) collective-permute-start(f32[8,128]{1,0:T(8,128)S(1)} %get-tuple-element.13), channel_id=1, source_target_pairs={{0,1},{1,0},{2,3},{3,2},{4,5},{5,4},{6,7},{7,6},{8,9},{9,8},{10,11... | collective-permute-start | bytes 12296 | tf_op jit(solution)/shard_map/ppermute | solution.py:338
  41.4 7.3 %collective-permute-start.8 = (f32[8,128]{1,0:T(8,128)S(1)}, f32[8,128]{1,0:T(8,128)S(1)}, u32[]{:S(2)}, u32[]{:S(2)}) collective-permute-start(f32[8,128]{1,0:T(8,128)S(1)} %add.6), channel_id=1, source_target_pairs={{0,3},{1,2},{2,1},{3,0},{4,7},{5,6},{6,5},{7,4},{8,11},{9,10},{10,... | collective-permute-start | bytes 12296 | tf_op jit(solution)/shard_map/ppermute | solution.py:338
  48.7 7.8 %collective-permute-start.9 = (f32[8,128]{1,0:T(8,128)S(1)}, f32[8,128]{1,0:T(8,128)S(1)}, u32[]{:S(2)}, u32[]{:S(2)}) collective-permute-start(f32[8,128]{1,0:T(8,128)S(1)} %add.7.a_ref), channel_id=1, source_target_pairs={{0,4},{1,5},{2,6},{3,7},{4,0},{5,1},{6,2},{7,3},{8,12},{9,13},{10,... | collective-permute-start | bytes 12296 | tf_op jit(solution)/shard_map/ppermute | solution.py:338

commit v3 on v2

--- a/solution.py
+++ b/solution.py
@@ -19,6 +19,7 @@
 BLOCKS = 128
 SET = 8
 ENTRIES = 128 * 8192
+HALF = LAYERS // 2
 
 decay_rate = 0.999
 epsilon = 1e-06
@@ -87,29 +88,34 @@
     return lax.shift_right_logical(lax.broadcasted_iota(jnp.int32, shape, len(shape) - 1), 5) & 3
 
 
-def pick_kernel(m_hbm, g_hbm, idx_hbm, cols_hbm, rows_hbm, v_ref, own_ref, m_buf, g_buf, idx_buf, cols_ref, rows_ref, sems):
+def pick_kernel(m_hbm, g_hbm, idx_hbm, cols_hbm, rows_hbm, v_ref, own_ref, mine_ref, theirs_ref, acc_ref, m_buf, g_buf, idx_buf, cols_ref, rows_ref, sems):
     p = lax.axis_index("dp")
-    copies = [pltpu.make_async_copy(idx_hbm.at[pl.ds(p * BLOCKS, BLOCKS)], idx_buf, sems.at[0])]
-    copies += [pltpu.make_async_copy(cols_hbm, cols_ref, sems.at[1])]
-    copies += [pltpu.make_async_copy(rows_hbm, rows_ref, sems.at[2])]
-    for l in range(LAYERS):
-        copies.append(pltpu.make_async_copy(m_hbm.at[l], m_buf.at[l], sems.at[3 + 2 * l]))
-        copies.append(pltpu.make_async_copy(g_hbm.at[l], g_buf.at[l], sems.at[4 + 2 * l]))
-    order = [3, 4, 1, 0, 2] + list(range(5, 3 + 2 * LAYERS))
-    for i in order:
-        copies[i].start()
-    for i in range(3):
-        copies[i].wait()
-    own_ref[...] = jnp.concatenate([idx_buf[pl.ds(cj, 32, stride=4), :] for cj in range(4)], axis=1)
+    core = p & 1
+    small = [
+        pltpu.make_async_copy(cols_hbm, cols_ref, sems.at[0]),
+        pltpu.make_async_copy(rows_hbm, rows_ref, sems.at[1]),
+        pltpu.make_async_copy(idx_hbm.at[pl.ds(p * BLOCKS, BLOCKS)], idx_buf, sems.at[2]),
+    ]
+    large = [
+        (
+            pltpu.make_async_copy(m_hbm.at[l], m_buf.at[l], sems.at[3 + 2 * l]),
+            pltpu.make_async_copy(g_hbm.at[l], g_buf.at[l], sems.at[4 + 2 * l]),
+        )
+        for l in range(LAYERS)
+    ]
+    for copy in (*large[0], *small, *large[1], *large[2], *large[3]):
+        copy.start()
     freq = lax.broadcasted_iota(jnp.int32, (GROUP, 128), 0)
     place = lax.broadcasted_iota(jnp.int32, (256, 256), 0)
     zeros = jnp.zeros((GROUP, 128), BF)
-    for l in range(LAYERS):
-        copies[3 + 2 * l].wait()
-        copies[4 + 2 * l].wait()
+
+    def columns(l):
         acc = decay_rate * m_buf[l] + g_buf[l].astype(F32)
+        acc_ref[l] = acc
         tiles = jnp.concatenate([acc[:, t * 256 : t * 256 + 256] for t in range(TILES)], axis=0)
-        half = cols_apply(tiles, cols_ref)
+        return cols_apply(tiles, cols_ref)
+
+    def rows_and_pick(l, half):
         for t in range(TILES):
             hi, lo = split(half[t * 128 : t * 128 + 128].T)
             both = mm(jnp.concatenate([hi, lo], axis=1), rows_ref[...])
@@ -129,12 +135,31 @@
             for a in range(2):
                 v_ref[pl.ds(l * 8 + a * 4 + t, 1), :] = v[:, a * 128 : a * 128 + 128]
 
-
-def own_kernel(m_ref, g_ref, own_ref, v_ref, cols_ref, rows_ref, out_hbm, out_buf, sems):
+    before = None
+    for l in range(LAYERS):
+        for copy in large[l]:
+            copy.wait()
+        if l == 0:
+            small[0].wait()
+        if l == 1:
+            small[1].wait()
+            small[2].wait()
+            own_ref[...] = jnp.concatenate([idx_buf[pl.ds(cj, 32, stride=4), :] for cj in range(4)], axis=1)
+        half = columns(l)
+        if before is not None:
+            rows_and_pick(l - 1, before)
+        before = half
+    rows_and_pick(LAYERS - 1, before)
+    mine_ref[...] = v_ref[pl.ds(pl.multiple_of(core * 16, 16), 16), :]
+    theirs_ref[...] = v_ref[pl.ds(pl.multiple_of(16 - core * 16, 16), 16), :]
+
+
+def own_kernel(layers, acc_ref, own_ref, v_ref, cols_ref, rows_ref, *rest):
+    out_hbm, out_buf, sems = rest[-3:]
     freq = lax.broadcasted_iota(jnp.int32, (GROUP, 128), 0)
     place = lax.broadcasted_iota(jnp.int32, (256, 128), 0)
     copies = []
-    for l in range(LAYERS):
+    for i, l in enumerate(layers):
         grids = []
         for t in range(TILES):
             parts = []
@@ -149,9 +174,8 @@
             grids.append(jnp.concatenate(parts, axis=0))
         for t, tile in enumerate(back(grids, cols_ref, rows_ref[...])):
             s = slice(t * 256, t * 256 + 256)
-            acc = decay_rate * m_ref[l, :, s] + g_ref[l, :, s].astype(F32)
-            out_buf[l, :, s] = acc - tile
-        copies.append(pltpu.make_async_copy(out_buf.at[l], out_hbm.at[l], sems.at[l]))
+            out_buf[i, :, s] = acc_ref[l, :, s] - tile
+        copies.append(pltpu.make_async_copy(out_buf.at[i], out_hbm.at[l], sems.at[i]))
         copies[-1].start()
     for copy in copies:
         copy.wait()
@@ -159,8 +183,10 @@
 
 def arrange_kernel(idx_ref, fr_ref, fc_ref):
     p = lax.axis_index("dp")
+    half = BLOCKS // 2
+    start = (p & 1) * half
     for q in range(REPLICAS // 4):
-        pos = jnp.concatenate([idx_ref[pl.ds((p ^ (4 * q + j)) * BLOCKS, BLOCKS), :] for j in range(4)], axis=1)
+        pos = jnp.concatenate([idx_ref[pl.ds(pl.multiple_of((p ^ (4 * q + j)) * BLOCKS + start, half), half), :] for j in range(4)], axis=1)
         fr_ref[:, q * 128 : q * 128 + 128] = lax.shift_right_logical(pos, 6).astype(F32)
         fc_ref[:, q * 128 : q * 128 + 128] = (pos & 63).astype(F32)
 
@@ -171,14 +197,15 @@
         old_ref, rest = rest[0], rest[1:]
     if last:
         grid_ref, sq_ref, val_ref = rest
+        first_layer = (lax.axis_index("dp") & 1) * HALF
         sq_ref[...] = jnp.zeros_like(sq_ref)
     else:
         grid_ref, val_ref = rest
-    lane = lane_block((32, 128))
+    lane = lane_block((16, 128))
     for q in range(SET // 4):
         x = [v_ref[4 * q + j] for j in range(4)]
         for cj in range(4):
-            y = jnp.zeros((32, 128), F32)
+            y = jnp.zeros((16, 128), F32)
             for j in range(4):
                 moved = x[j] if j == cj else pltpu.roll(x[j], ((j - cj) * 32) % 128, 1)
                 y = jnp.where(lane == j, moved, y)
@@ -209,10 +236,11 @@
             if last:
                 squares = squares + jnp.sum(grid * grid, axis=0, keepdims=True)
         if last:
-            sq_ref[pl.ds(l, 1), :] = squares[:, :128] + squares[:, 128:]
+            sq_ref[pl.ds(first_layer + l, 1), :] = squares[:, :128] + squares[:, 128:]
         return carry
 
-    lax.fori_loop(0, LAYERS, body, 0)
+    for l in range(HALF):
+        body(l, 0)
 
 
 def decode_kernel(grid_ref, cols_ref, rows_ref, out_ref):
@@ -222,20 +250,24 @@
             out_ref[l, :, t * 256 : t * 256 + 256] = tile
         return carry
 
-    lax.fori_loop(0, LAYERS, body, 0)
-
-
-def scale_kernel(x_ref, a_ref, b_ref, out_hbm, out_buf, sems):
+    for l in range(HALF):
+        body(l, 0)
+
+
+def scale_kernel(mine_ref, theirs_ref, a_ref, b_ref, out_hbm, out_buf, factor_ref, sems):
+    core = lax.axis_index("dp") & 1
     total = jnp.sum(a_ref[...] + b_ref[...], axis=1, keepdims=True)
-    factor = lax.rsqrt(jnp.broadcast_to(total, (8, 128)) / ENTRIES + epsilon)
+    factor_ref[...] = lax.rsqrt(jnp.broadcast_to(total, (8, 128)) / ENTRIES + epsilon)
     copies = []
-    for l in range(LAYERS):
-        row = factor[l : l + 1]
-        for t in range(COLS // 128):
-            s = slice(t * 128, t * 128 + 128)
-            out_buf[l, :, s] = x_ref[l, :, s] * row
-        copies.append(pltpu.make_async_copy(out_buf.at[l], out_hbm.at[l], sems.at[l]))
-        copies[-1].start()
+    for ref, start in ((mine_ref, core * HALF), (theirs_ref, HALF - core * HALF)):
+        for i in range(HALF):
+            l = start + i
+            row = factor_ref[pl.ds(l, 1), :]
+            for t in range(COLS // 128):
+                s = slice(t * 128, t * 128 + 128)
+                out_buf[l, :, s] = ref[i, :, s] * row
+            copies.append(pltpu.make_async_copy(out_buf.at[l], out_hbm.at[l], sems.at[len(copies)]))
+            copies[-1].start()
     for copy in copies:
         copy.wait()
 
@@ -243,7 +275,8 @@
 VM = pl.BlockSpec(memory_space=pltpu.VMEM)
 HB = pl.BlockSpec(memory_space=pltpu.HBM)
 DECODED = jax.ShapeDtypeStruct((LAYERS, ROWS, COLS), F32)
-GRIDS = jax.ShapeDtypeStruct((LAYERS, TILES, 128, 256), F32)
+GRIDS = jax.ShapeDtypeStruct((HALF, TILES, 128, 256), F32)
+HALVED = jax.ShapeDtypeStruct((HALF, ROWS, COLS), F32)
 
 
 def call(kernel, name, ins, outs, shapes, scratch=(), us=1.0, mib=32, **more):
@@ -265,8 +298,14 @@
         pick_kernel,
         "pick",
         [HB] * 5,
-        [VM] * 2,
-        [jax.ShapeDtypeStruct((32, 128), F32), jax.ShapeDtypeStruct((32, 128), jnp.int32)],
+        [VM] * 5,
+        [
+            jax.ShapeDtypeStruct((32, 128), F32),
+            jax.ShapeDtypeStruct((32, 128), jnp.int32),
+            jax.ShapeDtypeStruct((16, 128), F32),
+            jax.ShapeDtypeStruct((16, 128), F32),
+            DECODED,
+        ],
         [
             pltpu.VMEM((LAYERS, ROWS, COLS), F32),
             pltpu.VMEM((LAYERS, ROWS, COLS), BF),
@@ -276,24 +315,28 @@
             pltpu.SemaphoreType.DMA((3 + 2 * LAYERS,)),
         ],
         4.0,
-        60,
     )(m, g, idx, cols, rows)
 
 
-def own_update(m, g, own, v, cols, rows):
+def own_update(layers, acc, own, v, cols, rows, out=None):
+    ins, more = [acc, own, v, cols, rows], {}
+    if out is not None:
+        ins.append(out)
+        more = dict(input_output_aliases={5: 0})
     return call(
-        own_kernel,
-        "own",
-        [VM] * 6,
+        lambda *refs: own_kernel(layers, *refs),
+        f"own{layers[0]}",
+        [VM] * 5 + [HB] * (len(ins) - 5),
         HB,
         DECODED,
-        [pltpu.VMEM((LAYERS, ROWS, COLS), F32), pltpu.SemaphoreType.DMA((LAYERS,))],
-        3.0,
-    )(m, g, own, v, cols, rows)
+        [pltpu.VMEM((len(layers), ROWS, COLS), F32), pltpu.SemaphoreType.DMA((len(layers),))],
+        2.2,
+        **more,
+    )(*ins)
 
 
 def arrange(idx):
-    shape = jax.ShapeDtypeStruct((BLOCKS, 1024), F32)
+    shape = jax.ShapeDtypeStruct((BLOCKS // 2, 1024), F32)
     return call(arrange_kernel, "arrange", [VM], [VM, VM], [shape, shape], (), 0.5)(idx)
 
 
@@ -312,55 +355,80 @@
         [VM] * len(ins),
         outs,
         shapes,
-        [pltpu.VMEM((4, 32, 32 * SET), F32)],
-        2.6,
+        [pltpu.VMEM((4, 16, 32 * SET), F32)],
+        1.6,
         **more,
     )(*ins)
 
 
 def decode(grid, cols, rows):
-    return call(decode_kernel, "decode", [VM] * 3, VM, DECODED, (), 3.0)(grid, cols, rows)
-
-
-def rescale(x, a, b):
+    return call(decode_kernel, "decode", [VM] * 3, VM, HALVED, (), 1.6)(grid, cols, rows)
+
+
+def rescale(mine, theirs, a, b):
     return call(
         scale_kernel,
         "rescale",
-        [VM] * 3,
+        [VM] * 4,
         HB,
         DECODED,
-        [pltpu.VMEM((LAYERS, ROWS, COLS), F32), pltpu.SemaphoreType.DMA((LAYERS,))],
+        [pltpu.VMEM((LAYERS, ROWS, COLS), F32), pltpu.VMEM((8, 128), F32), pltpu.SemaphoreType.DMA((LAYERS,))],
         1.0,
-    )(x, a, b)
+    )(mine, theirs, a, b)
 
 
 def turn(x, axis, size, bit):
     return lax.ppermute(x, axis, [(i, i ^ bit) for i in range(size)])
+
+
+def near_other_core(x):
+    pairs = [(p * 8 + t, (p ^ 1) * 8 + (t ^ 1)) for p in range(REPLICAS) for t in range(8)]
+    return lax.ppermute(x, ("dp", "tensor"), pairs)
+
+
+def across(x):
+    pairs = []
+    for y in range(4):
+        for z in range(8):
+            for core in range(2):
+                for tx in range(4):
+                    to = (z + 6) % 8 if z in (0, 1, 4, 5) else (z + 2) % 8
+                    place = [((y * 4 + k % 4) * 2 + core) * 8 + (k // 4) * 4 + tx for k in (z, to)]
+                    pairs.append(tuple(place))
+    return lax.ppermute(x, ("dp", "tensor"), pairs)
 
 
 def on_device(momentum, gradient, kept_index):
     m, g = momentum[0], gradient[0]
     idx = kept_index.reshape(REPLICAS * BLOCKS, TOPK)
     forward_cols, forward_rows, back_cols, back_rows = (jnp.asarray(x) for x in constants())
-    v, own = pick(m, g, idx, forward_cols, forward_rows)
-
-    x = jnp.stack([v, turn(v, "dp", REPLICAS, 1)])
+    held = [pltpu.with_memory_space_constraint(x, pltpu.HBM) for x in (m, g, idx, forward_cols, forward_rows)]
+    v, own, mine, theirs, acc = pick(*held)
+
+    x = jnp.stack([mine, turn(theirs, "dp", REPLICAS, 1)])
+    x, v, idx = lax.optimization_barrier((x, v, idx))
     x = jnp.concatenate([x] + [turn(x, "dp", REPLICAS, b) for b in (2, 4, 6)], axis=0)
+    fr, fc = arrange(idx)
+    momentum_out = own_update((0, 1), acc, own, v, back_cols, back_rows)
+    x, momentum_out = lax.optimization_barrier((x, momentum_out))
     order = (0, 1, 3, 2)
     sets = {s: x if s == 0 else turn(x, "dp", REPLICAS, 8 * s) for s in order}
-    fr, fc = arrange(idx)
-    momentum_out = own_update(m, g, own, v, back_cols, back_rows)
     grid = None
     for s in order[:-1]:
         (grid,) = add_set(s, False, sets[s], fr, fc, grid)
     grid, squares = add_set(order[-1], True, sets[order[-1]], fr, fc, grid)
 
-    total = squares
-    for b in (1, 3):
-        total = total + turn(total, "tensor", 8, b)
-    other = turn(total, "tensor", 8, 4)
+    other_grid = turn(grid, "dp", REPLICAS, 1)
+    beside = turn(squares, "dp", REPLICAS, 1)
+    near = turn(squares, "tensor", 8, 1)
+    across_near = near_other_core(squares)
+    squares, v = lax.optimization_barrier((squares, v))
+    momentum_out = own_update((2, 3), acc, own, v, back_cols, back_rows, momentum_out)
     decoded = decode(grid, back_cols, back_rows)
-    update = rescale(decoded, total, other)
+    other = decode(other_grid, back_cols, back_rows)
+    total = squares + beside + near + across_near
+    total = total + turn(total, "tensor", 8, 3)
+    update = rescale(decoded, other, total, across(total))
     return (momentum_out[None], update)
 
 

time: 58.4 us -> 44.8 us (0.77)
  the two profiles are of different devices: /device:TPU:16 before, /device:TPU:1 now
where the time goes in v3:
time: 44.8 us; the launch traced here: 44.7 us
  starting transfers between devices  21.8 us (49%)
  Pallas kernels  20.4 us (46%)
  waiting for transfers between devices  1.43 us (3%)
  between operations  1 us (2%)
    ppermute x11, starting transfers between devices, turn(): return lax.ppermute(x, axis, [(i, i ^ bit) for i in range(size)])  16.7 us
    pallas_call x4, Pallas kernels, add_set(): call(lambda *refs: set_kernel(number, first, last, *refs), f'set{number}'...  5.45 us
    pallas_call x2, Pallas kernels, own_update(): call(lambda *refs: own_kernel(layers, *refs), f'own{layers[0]}', [VM] * 5...  5.36 us
    pallas_call x1, Pallas kernels, pick(): call(pick_kernel, 'pick', [HB] * 5, [VM] * 5, [jax.ShapeDtypeStruct((32,...  4.74 us
    ppermute x1, starting transfers between devices, across(): return lax.ppermute(x, ('dp', 'tensor'), pairs)  3.87 us
    pallas_call x2, Pallas kernels, decode(): call(decode_kernel, 'decode', [VM] * 3, VM, HALVED, (), 1.6)  3.12 us
    pallas_call x1, Pallas kernels, rescale(): call(scale_kernel, 'rescale', [VM] * 4, HB, DECODED, [pltpu.VMEM((LAYERS,...  1.49 us
    ppermute x11, waiting for transfers between devices, turn(): return lax.ppermute(x, axis, [(i, i ^ bit) for i in range(size)])  1.43 us
  transfers between devices with their start and end apart: 13, of which 2 were waited for; matrix products, arithmetic and copies ran while one was open for 0% of the time, Pallas kernels for 29%

profile of v3, /device:TPU:1, one launch (start us, length us, event | category | flops | bytes accessed | tf_op | source)
XLA Modules:
  0.0 44.7 jit_solution(859307700233072147)
XLA Ops:
  0.7 4.7 %pick.1 = (f32[32,128]{1,0:T(8,128)S(1)}, s32[32,128]{1,0:T(8,128)S(1)}, f32[16,128]{1,0:T(8,128)S(1)}, f32[16,128]{1,0:T(8,128)S(1)}, f32[4,128,1024]{2,1,0:T(8,128)S(1)}) custom-call(f32[4,128,1024]{2,1,0:T(8,128)} %bitcast.10, bf16[4,128,1024]{2,1,0:T(8,128)(2,1)} %bitcast.11, s32[4096,32]{1,0:T(8,128)} %bitcast.6, ...), custom_call_target="tpu_custom_call" | custom-call | flops 4000000000 | bytes 8000000 | tf_op jit(solution)/shard_map/pick/pallas_call | solution.py:297
  5.4 3.3 %collective-permute-start = (f32[16,128]{1,0:T(8,128)S(1)}, f32[16,128]{1,0:T(8,128)S(1)}, u32[]{:S(2)}, u32[]{:S(2)}) collective-permute-start(f32[16,128]{1,0:T(8,128)S(1)} %get-tuple-element.21), channel_id=1, source_target_pairs={{0,8},{8,0},{16,24},{24,16},{32,40},{40,32},{48,56},{56,48},{64,72... | collective-permute-start | bytes 24584 | tf_op jit(solution)/shard_map/ppermute | solution.py:381
  8.7 0.8 %collective-permute-done = f32[16,128]{1,0:T(8,128)S(1)} collective-permute-done((f32[16,128]{1,0:T(8,128)S(1)}, f32[16,128]{1,0:T(8,128)S(1)}, u32[]{:S(2)}, u32[]{:S(2)}) %collective-permute-start) | collective-permute-done | bytes 8224 | tf_op jit(solution)/shard_map/ppermute | solution.py:381
  9.6 2.6 %collective-permute-start.3 = (f32[2,16,128]{2,1,0:T(8,128)S(1)}, f32[2,16,128]{2,1,0:T(8,128)S(1)}, u32[]{:S(2)}, u32[]{:S(2)}) collective-permute-start(f32[2,16,128]{2,1,0:T(8,128)S(1)} %pad_maximum_fusion.1), channel_id=1, source_target_pairs={{0,48},{8,56},{16,32},{24,40},{32,16},{40,24},{48,0},{56,8},{64,11... | collective-permute-start | bytes 49160 | tf_op jit(solution)/shard_map/ppermute | solution.py:381
  12.2 0.9 %collective-permute-start.1 = (f32[2,16,128]{2,1,0:T(8,128)S(1)}, f32[2,16,128]{2,1,0:T(8,128)S(1)}, u32[]{:S(2)}, u32[]{:S(2)}) collective-permute-start(f32[2,16,128]{2,1,0:T(8,128)S(1)} %pad_maximum_fusion.1), channel_id=1, source_target_pairs={{0,16},{8,24},{16,0},{24,8},{32,48},{40,56},{48,32},{56,40},{64,80... | collective-permute-start | bytes 49160 | tf_op jit(solution)/shard_map/ppermute | solution.py:381
  13.1 2.7 %own0.1.refs_5_ = f32[4,128,1024]{2,1,0:T(8,128)} custom-call(f32[4,128,1024]{2,1,0:T(8,128)S(1)} %get-tuple-element.18.refs_0_, s32[32,128]{1,0:T(8,128)S(1)} %get-tuple-element.19.refs_1_, f32[32,128]{1,0:T(8,128)S(1)} %get-tuple-element.30.refs_2_, bf16[512,256]{1,0:T(8,128)(2,1)S(1)} %copy-done.1, bf16[256,256]{1,0:T(8,128)(2,1)S(1)} %copy-done.2), custom_call_target="tpu_custom_call" | custom-call | flops 2200000000 | bytes 4400000 | tf_op jit(solution)/shard_map/own0/pallas_call | solution.py:326
  15.8 0.3 arrange.1
  16.2 0.9 %collective-permute-start.6 = (f32[8,16,128]{2,1,0:T(8,128)S(1)}, f32[8,16,128]{2,1,0:T(8,128)S(1)}, u32[]{:S(2)}, u32[]{:S(2)}) collective-permute-start(f32[8,16,128]{2,1,0:T(8,128)S(1)} %pad_maximum_fusion.refs_0_), channel_id=1, source_target_pairs={{0,64},{8,72},{16,80},{24,88},{32,96},{40,104},{48,112},{56,120},{... | collective-permute-start | bytes 196616 | tf_op jit(solution)/shard_map/ppermute | solution.py:381
  17.1 1.9 %collective-permute-start.5 = (f32[8,16,128]{2,1,0:T(8,128)S(1)}, f32[8,16,128]{2,1,0:T(8,128)S(1)}, u32[]{:S(2)}, u32[]{:S(2)}) collective-permute-start(f32[8,16,128]{2,1,0:T(8,128)S(1)} %pad_maximum_fusion.refs_0_), channel_id=1, source_target_pairs={{0,192},{8,200},{16,208},{24,216},{32,224},{40,232},{48,240},{56,2... | collective-permute-start | bytes 196616 | tf_op jit(solution)/shard_map/ppermute | solution.py:381
  18.9 0.7 %collective-permute-start.4 = (f32[8,16,128]{2,1,0:T(8,128)S(1)}, f32[8,16,128]{2,1,0:T(8,128)S(1)}, u32[]{:S(2)}, u32[]{:S(2)}) collective-permute-start(f32[8,16,128]{2,1,0:T(8,128)S(1)} %pad_maximum_fusion.refs_0_), channel_id=1, source_target_pairs={{0,128},{8,136},{16,144},{24,152},{32,160},{40,168},{48,176},{56,1... | collective-permute-start | bytes 196616 | tf_op jit(solution)/shard_map/ppermute | solution.py:381
  19.7 1.4 %set0.1.refs_3_ = f32[2,4,128,256]{3,2,1,0:T(8,128)S(1)} custom-call(f32[8,16,128]{2,1,0:T(8,128)S(1)} %pad_maximum_fusion.refs_0_, f32[64,1024]{1,0:T(8,128)S(1)} %get-tuple-element.27.refs_1_, f32[64,1024]{1,0:T(8,128)S(1)} %get-tuple-element.28.refs_2_), custom_call_target="tpu_custom_call" | custom-call | flops 1600000000 | bytes 3200000 | tf_op jit(solution)/shard_map/set0/pallas_call | solution.py:352
  21.0 1.4 %set1.1.refs_3_ = f32[2,4,128,256]{3,2,1,0:T(8,128)S(1)} custom-call(f32[8,16,128]{2,1,0:T(8,128)S(1)} %collective-permute-done.6.refs_0_, f32[64,1024]{1,0:T(8,128)S(1)} %get-tuple-element.27.refs_1_, f32[64,1024]{1,0:T(8,128)S(1)} %get-tuple-element.28.refs_2_, f32[2,4,128,256]{3,2,1,0:T(8,128)S(1)} %set0.1.refs_3_), custom_call_target="tpu_custom_call", output_to_operand_aliasing={{}: (3, {})} | custom-call | flops 1600000000 | bytes 3200000 | tf_op jit(solution)/shard_map/set1/pallas_call | solution.py:352
  22.4 1.4 %set3.1.refs_3_ = f32[2,4,128,256]{3,2,1,0:T(8,128)S(1)} custom-call(f32[8,16,128]{2,1,0:T(8,128)S(1)} %collective-permute-done.5.refs_0_, f32[64,1024]{1,0:T(8,128)S(1)} %get-tuple-element.27.refs_1_, f32[64,1024]{1,0:T(8,128)S(1)} %get-tuple-element.28.refs_2_, f32[2,4,128,256]{3,2,1,0:T(8,128)S(1)} %set1.1.refs_3_), custom_call_target="tpu_custom_call", output_to_operand_aliasing={{}: (3, {})} | custom-call | flops 1600000000 | bytes 3200000 | tf_op jit(solution)/shard_map/set3/pallas_call | solution.py:352
  23.8 0.6 %collective-permute-done.4.refs_0_ = f32[8,16,128]{2,1,0:T(8,128)S(1)} collective-permute-done((f32[8,16,128]{2,1,0:T(8,128)S(1)}, f32[8,16,128]{2,1,0:T(8,128)S(1)}, u32[]{:S(2)}, u32[]{:S(2)}) %collective-permute-start.4) | collective-permute-done | bytes 65568 | tf_op jit(solution)/shard_map/ppermute | solution.py:381
  24.4 1.4 %set2.1 = (f32[2,4,128,256]{3,2,1,0:T(8,128)S(1)}, f32[8,128]{1,0:T(8,128)S(1)}) custom-call(f32[8,16,128]{2,1,0:T(8,128)S(1)} %collective-permute-done.4.refs_0_, f32[64,1024]{1,0:T(8,128)S(1)} %get-tuple-element.27.refs_1_, f32[64,1024]{1,0:T(8,128)S(1)} %get-tuple-element.28.refs_2_, ...), custom_call_target="tpu_custom_call", output_to_operand_aliasing={{0}: (3, {})} | custom-call | flops 1600000000 | bytes 3200000 | tf_op jit(solution)/shard_map/set2/pallas_call | solution.py:352
  25.7 2.8 %collective-permute-start.7 = (f32[2,4,128,256]{3,2,1,0:T(8,128)S(1)}, f32[2,4,128,256]{3,2,1,0:T(8,128)S(1)}, u32[]{:S(2)}, u32[]{:S(2)}) collective-permute-start(f32[2,4,128,256]{3,2,1,0:T(8,128)S(1)} %get-tuple-element.32.grid_ref), channel_id=1, source_target_pairs={{0,8},{8,0},{16,24},{24,16},{32,40},{40,32},{48,56},{56,48},{64,72... | collective-permute-start | bytes 3145736 | tf_op jit(solution)/shard_map/ppermute | solution.py:381
  28.5 1.2 %collective-permute-start.10 = (f32[8,128]{1,0:T(8,128)S(1)}, f32[8,128]{1,0:T(8,128)S(1)}, u32[]{:S(2)}, u32[]{:S(2)}) collective-permute-start(f32[8,128]{1,0:T(8,128)S(1)} %get-tuple-element.33), channel_id=1, source_target_pairs={{0,9},{1,8},{2,11},{3,10},{4,13},{5,12},{6,15},{7,14},{8,1},{9,0},... | collective-permute-start | bytes 12296 | tf_op jit(solution)/shard_map/ppermute | solution.py:386
  30.0 0.7 %collective-permute-start.8 = (f32[8,128]{1,0:T(8,128)S(1)}, f32[8,128]{1,0:T(8,128)S(1)}, u32[]{:S(2)}, u32[]{:S(2)}) collective-permute-start(f32[8,128]{1,0:T(8,128)S(1)} %get-tuple-element.33), channel_id=1, source_target_pairs={{0,8},{8,0},{16,24},{24,16},{32,40},{40,32},{48,56},{56,48},{64,72... | collective-permute-start | bytes 12296 | tf_op jit(solution)/shard_map/ppermute | solution.py:381
  30.7 2.7 %own2.1 = f32[4,128,1024]{2,1,0:T(8,128)} custom-call(f32[4,128,1024]{2,1,0:T(8,128)S(1)} %get-tuple-element.18.refs_0_, s32[32,128]{1,0:T(8,128)S(1)} %get-tuple-element.19.refs_1_, f32[32,128]{1,0:T(8,128)S(1)} %get-tuple-element.30.refs_2_, bf16[512,256]{1,0:T(8,128)(2,1)S(1)} %copy-done.1, ...), custom_call_target="tpu_custom_call", output_to_operand_aliasing={{}: (5, {})} | custom-call | flops 2200000000 | bytes 4400000 | tf_op jit(solution)/shard_map/own2/pallas_call | solution.py:326
  33.4 2.6 %collective-permute-start.11 = (f32[8,128]{1,0:T(8,128)S(1)}, f32[8,128]{1,0:T(8,128)S(1)}, u32[]{:S(2)}, u32[]{:S(2)}) collective-permute-start(f32[8,128]{1,0:T(8,128)S(1)} %add_add_fusion), channel_id=1, source_target_pairs={{0,3},{1,2},{2,1},{3,0},{4,7},{5,6},{6,5},{7,4},{8,11},{9,10},{10,... | collective-permute-start | bytes 12296 | tf_op jit(solution)/shard_map/ppermute | solution.py:381
  36.0 1.6 %decode.2.mine_ref = f32[2,128,1024]{2,1,0:T(8,128)S(1)} custom-call(f32[2,4,128,256]{3,2,1,0:T(8,128)S(1)} %get-tuple-element.32.grid_ref, bf16[512,256]{1,0:T(8,128)(2,1)S(1)} %copy-done.1, bf16[256,256]{1,0:T(8,128)(2,1)S(1)} %copy-done.2), custom_call_target="tpu_custom_call" | custom-call | flops 1600000000 | bytes 3200000 | tf_op jit(solution)/shard_map/decode/pallas_call | solution.py:365
  37.6 3.9 %collective-permute-start.12 = (f32[8,128]{1,0:T(8,128)S(1)}, f32[8,128]{1,0:T(8,128)S(1)}, u32[]{:S(2)}, u32[]{:S(2)}) collective-permute-start(f32[8,128]{1,0:T(8,128)S(1)} %add.15.a_ref), channel_id=1, source_target_pairs={{0,36},{1,37},{2,38},{3,39},{8,44},{9,45},{10,46},{11,47},{16,52},... | collective-permute-start | bytes 12296 | tf_op jit(solution)/shard_map/ppermute | solution.py:398
  41.5 1.6 %decode.3.theirs_ref = f32[2,128,1024]{2,1,0:T(8,128)S(1)} custom-call(f32[2,4,128,256]{3,2,1,0:T(8,128)S(1)} %collective-permute-done.7.grid_ref, bf16[512,256]{1,0:T(8,128)(2,1)S(1)} %copy-done.1, bf16[256,256]{1,0:T(8,128)(2,1)S(1)} %copy-done.2), custom_call_target="tpu_custom_call" | custom-call | flops 1600000000 | bytes 3200000 | tf_op jit(solution)/shard_map/decode/pallas_call | solution.py:365
  43.0 1.5 %rescale.1 = f32[4,128,1024]{2,1,0:T(8,128)} custom-call(f32[2,128,1024]{2,1,0:T(8,128)S(1)} %decode.2.mine_ref, f32[2,128,1024]{2,1,0:T(8,128)S(1)} %decode.3.theirs_ref, f32[8,128]{1,0:T(8,128)S(1)} %add.15.a_ref, f32[8,128]{1,0:T(8,128)S(1)} %collective-permute-done.12.b_ref), custom_call_target="tpu_custom_call" | custom-call | flops 1000000000 | bytes 2000000 | tf_op jit(solution)/shard_map/rescale/pallas_call | solution.py:369
  (23 shorter events, 0.3 us)
Async XLA Ops:
  0.6 12.5 %copy-start.1 = (bf16[512,256]{1,0:T(8,128)(2,1)S(1)}, bf16[512,256]{1,0:T(8,128)(2,1)}, u32[]{:S(2)}) copy-start(bf16[512,256]{1,0:T(8,128)(2,1)} %constant.10.clone.refs_3_.cols_ref) | copy-start | bytes 786436
  0.6 12.5 %copy-start.2 = (bf16[256,256]{1,0:T(8,128)(2,1)S(1)}, bf16[256,256]{1,0:T(8,128)(2,1)}, u32[]{:S(2)}) copy-start(bf16[256,256]{1,0:T(8,128)(2,1)} %constant.11.clone.refs_4_.rows_ref) | copy-start | bytes 393220
  5.4 4.2 %collective-permute-start = (f32[16,128]{1,0:T(8,128)S(1)}, f32[16,128]{1,0:T(8,128)S(1)}, u32[]{:S(2)}, u32[]{:S(2)}) collective-permute-start(f32[16,128]{1,0:T(8,128)S(1)} %get-tuple-element.21), channel_id=1, source_target_pairs={{0,8},{8,0},{16,24},{24,16},{32,40},{40,32},{48,56},{56,48},{64,72... | collective-permute-start | bytes 24584 | tf_op jit(solution)/shard_map/ppermute | solution.py:381
  9.6 6.6 %collective-permute-start.3 = (f32[2,16,128]{2,1,0:T(8,128)S(1)}, f32[2,16,128]{2,1,0:T(8,128)S(1)}, u32[]{:S(2)}, u32[]{:S(2)}) collective-permute-start(f32[2,16,128]{2,1,0:T(8,128)S(1)} %pad_maximum_fusion.1), channel_id=1, source_target_pairs={{0,48},{8,56},{16,32},{24,40},{32,16},{40,24},{48,0},{56,8},{64,11... | collective-permute-start | bytes 49160 | tf_op jit(solution)/shard_map/ppermute | solution.py:381
  12.2 4.0 %collective-permute-start.2 = (f32[2,16,128]{2,1,0:T(8,128)S(1)}, f32[2,16,128]{2,1,0:T(8,128)S(1)}, u32[]{:S(2)}, u32[]{:S(2)}) collective-permute-start(f32[2,16,128]{2,1,0:T(8,128)S(1)} %pad_maximum_fusion.1), channel_id=1, source_target_pairs={{0,32},{8,40},{16,48},{24,56},{32,0},{40,8},{48,16},{56,24},{64,96... | collective-permute-start | bytes 49160 | tf_op jit(solution)/shard_map/ppermute | solution.py:381
  12.2 4.0 %collective-permute-start.1 = (f32[2,16,128]{2,1,0:T(8,128)S(1)}, f32[2,16,128]{2,1,0:T(8,128)S(1)}, u32[]{:S(2)}, u32[]{:S(2)}) collective-permute-start(f32[2,16,128]{2,1,0:T(8,128)S(1)} %pad_maximum_fusion.1), channel_id=1, source_target_pairs={{0,16},{8,24},{16,0},{24,8},{32,48},{40,56},{48,32},{56,40},{64,80... | collective-permute-start | bytes 49160 | tf_op jit(solution)/shard_map/ppermute | solution.py:381
  13.1 2.7 %copy-start = (s32[32,4,2,16,32]{4,3,2,1,0:T(8,128)S(1)}, s32[32,4,2,16,32]{4,3,2,1,0:T(8,128)}, u32[]{:S(2)}) copy-start(s32[32,4,2,16,32]{4,3,2,1,0:T(8,128)} %param.9) | copy-start | bytes 1572868
  16.2 4.9 %collective-permute-start.6 = (f32[8,16,128]{2,1,0:T(8,128)S(1)}, f32[8,16,128]{2,1,0:T(8,128)S(1)}, u32[]{:S(2)}, u32[]{:S(2)}) collective-permute-start(f32[8,16,128]{2,1,0:T(8,128)S(1)} %pad_maximum_fusion.refs_0_), channel_id=1, source_target_pairs={{0,64},{8,72},{16,80},{24,88},{32,96},{40,104},{48,112},{56,120},{... | collective-permute-start | bytes 196616 | tf_op jit(solution)/shard_map/ppermute | solution.py:381
  17.1 5.4 %collective-permute-start.5 = (f32[8,16,128]{2,1,0:T(8,128)S(1)}, f32[8,16,128]{2,1,0:T(8,128)S(1)}, u32[]{:S(2)}, u32[]{:S(2)}) collective-permute-start(f32[8,16,128]{2,1,0:T(8,128)S(1)} %pad_maximum_fusion.refs_0_), channel_id=1, source_target_pairs={{0,192},{8,200},{16,208},{24,216},{32,224},{40,232},{48,240},{56,2... | collective-permute-start | bytes 196616 | tf_op jit(solution)/shard_map/ppermute | solution.py:381
  18.9 5.4 %collective-permute-start.4 = (f32[8,16,128]{2,1,0:T(8,128)S(1)}, f32[8,16,128]{2,1,0:T(8,128)S(1)}, u32[]{:S(2)}, u32[]{:S(2)}) collective-permute-start(f32[8,16,128]{2,1,0:T(8,128)S(1)} %pad_maximum_fusion.refs_0_), channel_id=1, source_target_pairs={{0,128},{8,136},{16,144},{24,152},{32,160},{40,168},{48,176},{56,1... | collective-permute-start | bytes 196616 | tf_op jit(solution)/shard_map/ppermute | solution.py:381
  25.7 15.7 %collective-permute-start.7 = (f32[2,4,128,256]{3,2,1,0:T(8,128)S(1)}, f32[2,4,128,256]{3,2,1,0:T(8,128)S(1)}, u32[]{:S(2)}, u32[]{:S(2)}) collective-permute-start(f32[2,4,128,256]{3,2,1,0:T(8,128)S(1)} %get-tuple-element.32.grid_ref), channel_id=1, source_target_pairs={{0,8},{8,0},{16,24},{24,16},{32,40},{40,32},{48,56},{56,48},{64,72... | collective-permute-start | bytes 3145736 | tf_op jit(solution)/shard_map/ppermute | solution.py:381
  28.5 4.9 %collective-permute-start.10 = (f32[8,128]{1,0:T(8,128)S(1)}, f32[8,128]{1,0:T(8,128)S(1)}, u32[]{:S(2)}, u32[]{:S(2)}) collective-permute-start(f32[8,128]{1,0:T(8,128)S(1)} %get-tuple-element.33), channel_id=1, source_target_pairs={{0,9},{1,8},{2,11},{3,10},{4,13},{5,12},{6,15},{7,14},{8,1},{9,0},... | collective-permute-start | bytes 12296 | tf_op jit(solution)/shard_map/ppermute | solution.py:386
  29.7 3.7 %collective-permute-start.9 = (f32[8,128]{1,0:T(8,128)S(1)}, f32[8,128]{1,0:T(8,128)S(1)}, u32[]{:S(2)}, u32[]{:S(2)}) collective-permute-start(f32[8,128]{1,0:T(8,128)S(1)} %get-tuple-element.33), channel_id=1, source_target_pairs={{0,1},{1,0},{2,3},{3,2},{4,5},{5,4},{6,7},{7,6},{8,9},{9,8},{10,11... | collective-permute-start | bytes 12296 | tf_op jit(solution)/shard_map/ppermute | solution.py:381
  30.0 3.4 %collective-permute-start.8 = (f32[8,128]{1,0:T(8,128)S(1)}, f32[8,128]{1,0:T(8,128)S(1)}, u32[]{:S(2)}, u32[]{:S(2)}) collective-permute-start(f32[8,128]{1,0:T(8,128)S(1)} %get-tuple-element.33), channel_id=1, source_target_pairs={{0,8},{8,0},{16,24},{24,16},{32,40},{40,32},{48,56},{56,48},{64,72... | collective-permute-start | bytes 12296 | tf_op jit(solution)/shard_map/ppermute | solution.py:381
  33.4 4.1 %collective-permute-start.11 = (f32[8,128]{1,0:T(8,128)S(1)}, f32[8,128]{1,0:T(8,128)S(1)}, u32[]{:S(2)}, u32[]{:S(2)}) collective-permute-start(f32[8,128]{1,0:T(8,128)S(1)} %add_add_fusion), channel_id=1, source_target_pairs={{0,3},{1,2},{2,1},{3,0},{4,7},{5,6},{6,5},{7,4},{8,11},{9,10},{10,... | collective-permute-start | bytes 12296 | tf_op jit(solution)/shard_map/ppermute | solution.py:381
  37.6 5.4 %collective-permute-start.12 = (f32[8,128]{1,0:T(8,128)S(1)}, f32[8,128]{1,0:T(8,128)S(1)}, u32[]{:S(2)}, u32[]{:S(2)}) collective-permute-start(f32[8,128]{1,0:T(8,128)S(1)} %add.15.a_ref), channel_id=1, source_target_pairs={{0,36},{1,37},{2,38},{3,39},{8,44},{9,45},{10,46},{11,47},{16,52},... | collective-permute-start | bytes 12296 | tf_op jit(solution)/shard_map/ppermute | solution.py:398

commit v4 on v3

--- a/solution.py
+++ b/solution.py
@@ -43,15 +43,13 @@
 
 
 def constants():
-    b = basis_matrix()
-    two, four = np.kron(np.eye(2), b), np.kron(np.eye(4), b)
-    t_hi, t_lo = halves(two.T)
-    none = np.zeros_like(t_lo)
-    forward_cols = np.concatenate(halves(four.T), axis=0)
-    forward_rows = np.block([[t_hi, t_lo], [t_hi, none]])
-    back_cols = np.concatenate(halves(four), axis=0)
+    w_hi, w_lo = halves(np.kron(np.eye(2), basis_matrix()))
+    t_hi, t_lo = w_hi.T, w_lo.T
+    none = np.zeros_like(w_lo)
+    forward = np.block([[t_hi, t_lo], [t_hi, none]])
+    back_cols = np.block([[w_hi, w_lo], [w_hi, none]])
     back_rows = np.block([[t_hi, t_hi], [t_lo, none]])
-    return forward_cols, forward_rows, back_cols, back_rows
+    return forward, back_cols, back_rows
 
 
 def split(x):
@@ -67,18 +65,21 @@
     return lax.dot_general(a, b, (((1,), (1,)), ((), ())), preferred_element_type=F32)
 
 
-def cols_apply(x, cols):
-    n = x.shape[0]
-    hi, lo = split(x)
-    both = mm(jnp.concatenate([hi, lo], axis=0), cols[:256])
-    return both[:n] + both[n:] + mm(hi, cols[256:])
+def times(x, weights):
+    both = mm(jnp.concatenate(split(x), axis=1), weights)
+    return both[:, :128] + both[:, 128:]
+
+
+def lane_tiles(x):
+    return jnp.concatenate([x[:, j : j + 128] for j in range(0, x.shape[1], 128)], axis=0)
 
 
 def back(grids, cols, rows):
-    half = cols_apply(jnp.concatenate(grids, axis=0), cols)
+    half = times(jnp.concatenate([lane_tiles(x) for x in grids], axis=0), cols)
     out = []
     for t in range(TILES):
-        hi, lo = split(half[t * 128 : t * 128 + 128])
+        part = half[t * 256 : t * 256 + 256]
+        hi, lo = split(jnp.concatenate([part[:128], part[128:]], axis=1))
         both = mm(rows, jnp.concatenate([hi, lo], axis=0))
         out.append(both[:128] + both[128:])
     return out
@@ -88,18 +89,17 @@
     return lax.shift_right_logical(lax.broadcasted_iota(jnp.int32, shape, len(shape) - 1), 5) & 3
 
 
-def pick_kernel(m_hbm, g_hbm, idx_hbm, cols_hbm, rows_hbm, v_ref, own_ref, mine_ref, theirs_ref, acc_ref, m_buf, g_buf, idx_buf, cols_ref, rows_ref, sems):
+def pick_kernel(m_hbm, g_hbm, idx_hbm, weights_hbm, v_ref, own_ref, mine_ref, theirs_ref, acc_ref, m_buf, g_buf, idx_buf, weights_ref, sems):
     p = lax.axis_index("dp")
     core = p & 1
     small = [
-        pltpu.make_async_copy(cols_hbm, cols_ref, sems.at[0]),
-        pltpu.make_async_copy(rows_hbm, rows_ref, sems.at[1]),
-        pltpu.make_async_copy(idx_hbm.at[pl.ds(p * BLOCKS, BLOCKS)], idx_buf, sems.at[2]),
+        pltpu.make_async_copy(weights_hbm, weights_ref, sems.at[0]),
+        pltpu.make_async_copy(idx_hbm.at[pl.ds(p * BLOCKS, BLOCKS)], idx_buf, sems.at[1]),
     ]
     large = [
         (
-            pltpu.make_async_copy(m_hbm.at[l], m_buf.at[l], sems.at[3 + 2 * l]),
-            pltpu.make_async_copy(g_hbm.at[l], g_buf.at[l], sems.at[4 + 2 * l]),
+            pltpu.make_async_copy(m_hbm.at[l], m_buf.at[l], sems.at[2 + 2 * l]),
+            pltpu.make_async_copy(g_hbm.at[l], g_buf.at[l], sems.at[3 + 2 * l]),
         )
         for l in range(LAYERS)
     ]
@@ -112,14 +112,12 @@
     def columns(l):
         acc = decay_rate * m_buf[l] + g_buf[l].astype(F32)
         acc_ref[l] = acc
-        tiles = jnp.concatenate([acc[:, t * 256 : t * 256 + 256] for t in range(TILES)], axis=0)
-        return cols_apply(tiles, cols_ref)
+        return times(lane_tiles(acc), weights_ref[...])
 
     def rows_and_pick(l, half):
         for t in range(TILES):
-            hi, lo = split(half[t * 128 : t * 128 + 128].T)
-            both = mm(jnp.concatenate([hi, lo], axis=1), rows_ref[...])
-            hi, lo = split(both[:, :128] + both[:, 128:])
+            turned = [half[u * 128 : u * 128 + 128].T for u in (2 * t, 2 * t + 1)]
+            hi, lo = split(times(jnp.concatenate(turned, axis=0), weights_ref[...]))
             pos = [own_ref[pl.ds(l * 8 + a * 4 + t, 1), :] for a in range(2)]
             hot = [(freq == lax.shift_right_logical(x, 6)).astype(F32).astype(BF) for x in pos]
             pick = jnp.concatenate(
@@ -135,21 +133,20 @@
             for a in range(2):
                 v_ref[pl.ds(l * 8 + a * 4 + t, 1), :] = v[:, a * 128 : a * 128 + 128]
 
-    before = None
-    for l in range(LAYERS):
+    def wait(l):
         for copy in large[l]:
             copy.wait()
-        if l == 0:
-            small[0].wait()
-        if l == 1:
-            small[1].wait()
-            small[2].wait()
-            own_ref[...] = jnp.concatenate([idx_buf[pl.ds(cj, 32, stride=4), :] for cj in range(4)], axis=1)
-        half = columns(l)
-        if before is not None:
-            rows_and_pick(l - 1, before)
-        before = half
-    rows_and_pick(LAYERS - 1, before)
+
+    wait(0)
+    for copy in small:
+        copy.wait()
+    own_ref[...] = jnp.concatenate([idx_buf[pl.ds(cj, 32, stride=4), :] for cj in range(4)], axis=1)
+    rows_and_pick(0, columns(0))
+    for l in range(1, LAYERS):
+        wait(l)
+    later = [columns(l) for l in range(1, LAYERS)]
+    for l in range(1, LAYERS):
+        rows_and_pick(l, later[l - 1])
     mine_ref[...] = v_ref[pl.ds(pl.multiple_of(core * 16, 16), 16), :]
     theirs_ref[...] = v_ref[pl.ds(pl.multiple_of(16 - core * 16, 16), 16), :]
 
@@ -158,21 +155,25 @@
     out_hbm, out_buf, sems = rest[-3:]
     freq = lax.broadcasted_iota(jnp.int32, (GROUP, 128), 0)
     place = lax.broadcasted_iota(jnp.int32, (256, 128), 0)
+    zeros = jnp.zeros((GROUP, 128), BF)
     copies = []
     for i, l in enumerate(layers):
         grids = []
         for t in range(TILES):
-            parts = []
+            left, right = [], []
             for a in range(2):
                 row = l * 8 + a * 4 + t
                 pos = own_ref[pl.ds(row, 1), :]
                 v = v_ref[pl.ds(row, 1), :]
-                hi, lo = split(jnp.where(freq == lax.shift_right_logical(pos, 6), v, 0.0))
-                right = (place == (pos & 63) + 64 * lane_block((1, 128))).astype(F32).astype(BF)
-                both = mm_t(jnp.concatenate([hi, lo], axis=0), right)
-                parts.append(both[:GROUP] + both[GROUP:])
-            grids.append(jnp.concatenate(parts, axis=0))
-        for t, tile in enumerate(back(grids, cols_ref, rows_ref[...])):
+                left.append(split(jnp.where(freq == lax.shift_right_logical(pos, 6), v, 0.0)))
+                right.append((place == (pos & 63) + 64 * lane_block((1, 128))).astype(F32).astype(BF))
+            rows = []
+            for h in range(2):
+                rows.append(jnp.concatenate([left[0][h], zeros], axis=1))
+                rows.append(jnp.concatenate([zeros, left[1][h]], axis=1))
+            both = mm_t(jnp.concatenate(rows, axis=0), jnp.concatenate(right, axis=1))
+            grids.append(both[:128] + both[128:])
+        for t, tile in enumerate(back(grids, cols_ref[...], rows_ref[...])):
             s = slice(t * 256, t * 256 + 256)
             out_buf[i, :, s] = acc_ref[l, :, s] - tile
         copies.append(pltpu.make_async_copy(out_buf.at[i], out_hbm.at[l], sems.at[i]))
@@ -245,7 +246,7 @@
 
 def decode_kernel(grid_ref, cols_ref, rows_ref, out_ref):
     def body(l, carry):
-        tiles = back([grid_ref[l, t] for t in range(TILES)], cols_ref, rows_ref[...])
+        tiles = back([grid_ref[l, t] for t in range(TILES)], cols_ref[...], rows_ref[...])
         for t, tile in enumerate(tiles):
             out_ref[l, :, t * 256 : t * 256 + 256] = tile
         return carry
@@ -293,11 +294,11 @@
     )
 
 
-def pick(m, g, idx, cols, rows):
+def pick(m, g, idx, weights):
     return call(
         pick_kernel,
         "pick",
-        [HB] * 5,
+        [HB] * 4,
         [VM] * 5,
         [
             jax.ShapeDtypeStruct((32, 128), F32),
@@ -310,12 +311,11 @@
             pltpu.VMEM((LAYERS, ROWS, COLS), F32),
             pltpu.VMEM((LAYERS, ROWS, COLS), BF),
             pltpu.VMEM((BLOCKS, TOPK), jnp.int32),
-            pltpu.VMEM(cols.shape, BF),
-            pltpu.VMEM(rows.shape, BF),
-            pltpu.SemaphoreType.DMA((3 + 2 * LAYERS,)),
+            pltpu.VMEM(weights.shape, BF),
+            pltpu.SemaphoreType.DMA((2 + 2 * LAYERS,)),
         ],
         4.0,
-    )(m, g, idx, cols, rows)
+    )(m, g, idx, weights)
 
 
 def own_update(layers, acc, own, v, cols, rows, out=None):
@@ -401,8 +401,8 @@
 def on_device(momentum, gradient, kept_index):
     m, g = momentum[0], gradient[0]
     idx = kept_index.reshape(REPLICAS * BLOCKS, TOPK)
-    forward_cols, forward_rows, back_cols, back_rows = (jnp.asarray(x) for x in constants())
-    held = [pltpu.with_memory_space_constraint(x, pltpu.HBM) for x in (m, g, idx, forward_cols, forward_rows)]
+    forward, back_cols, back_rows = (jnp.asarray(x) for x in constants())
+    held = [pltpu.with_memory_space_constraint(x, pltpu.HBM) for x in (m, g, idx, forward)]
     v, own, mine, theirs, acc = pick(*held)
 
     x = jnp.stack([mine, turn(theirs, "dp", REPLICAS, 1)])

time: 44.8 us -> 43 us (0.960); the launches traced: 44.7 us -> 42.2 us
  Pallas kernels: 20.4 us -> 17.2 us
    pallas_call x2, Pallas kernels: 3.12 us -> 1.78 us  [decode(): call(decode_kernel, 'decode', [VM] * 3, VM, HALVED, (), 1.6)]
    pallas_call x1, Pallas kernels: 4.74 us -> 3.75 us  [pick(): call(pick_kernel, 'pick', [HB] * 4, [VM] * 5, [jax.ShapeDtypeStruct((32,...]
    pallas_call x2, Pallas kernels: 5.36 us -> 4.44 us  [own_update(): call(lambda *refs: own_kernel(layers, *refs), f'own{layers[0]}', [VM] * 5...]
    ppermute x11, starting transfers between devices: 16.7 us -> 17.2 us  [turn(): return lax.ppermute(x, axis, [(i, i ^ bit) for i in range(size)])]
  transfers between devices with their start and end apart: 13 -> 13, of which waited for: 2 -> 4; matrix products, arithmetic and copies ran while one was open for 0% -> 0% of each run, Pallas kernels for 29% -> 25%
where the time goes in v4:
time: 43 us; the launch traced here: 42.2 us
  starting transfers between devices  22.2 us (52%)
  Pallas kernels  17.2 us (40%)
  waiting for transfers between devices  1.81 us (4%)
  between operations  0.98 us (2%)
    ppermute x11, starting transfers between devices, turn(): return lax.ppermute(x, axis, [(i, i ^ bit) for i in range(size)])  17.2 us
    pallas_call x4, Pallas kernels, add_set(): call(lambda *refs: set_kernel(number, first, last, *refs), f'set{number}'...  5.45 us
    pallas_call x2, Pallas kernels, own_update(): call(lambda *refs: own_kernel(layers, *refs), f'own{layers[0]}', [VM] * 5...  4.44 us
    ppermute x1, starting transfers between devices, across(): return lax.ppermute(x, ('dp', 'tensor'), pairs)  3.78 us
    pallas_call x1, Pallas kernels, pick(): call(pick_kernel, 'pick', [HB] * 4, [VM] * 5, [jax.ShapeDtypeStruct((32,...  3.75 us
    pallas_call x2, Pallas kernels, decode(): call(decode_kernel, 'decode', [VM] * 3, VM, HALVED, (), 1.6)  1.78 us
    ppermute x11, waiting for transfers between devices, turn(): return lax.ppermute(x, axis, [(i, i ^ bit) for i in range(size)])  1.71 us
    pallas_call x1, Pallas kernels, rescale(): call(scale_kernel, 'rescale', [VM] * 4, HB, DECODED, [pltpu.VMEM((LAYERS,...  1.49 us
  transfers between devices with their start and end apart: 13, of which 4 were waited for; matrix products, arithmetic and copies ran while one was open for 0% of the time, Pallas kernels for 25%

profile of v4, /device:TPU:1, one launch (start us, length us, event | category | flops | bytes accessed | tf_op | source)
XLA Modules:
  0.0 42.2 jit_solution(11084576268359307834)
XLA Ops:
  0.7 3.8 %pick.1 = (f32[32,128]{1,0:T(8,128)S(1)}, s32[32,128]{1,0:T(8,128)S(1)}, f32[16,128]{1,0:T(8,128)S(1)}, f32[16,128]{1,0:T(8,128)S(1)}, f32[4,128,1024]{2,1,0:T(8,128)S(1)}) custom-call(f32[4,128,1024]{2,1,0:T(8,128)} %bitcast.10, bf16[4,128,1024]{2,1,0:T(8,128)(2,1)} %bitcast.11, s32[4096,32]{1,0:T(8,128)} %bitcast.6, bf16[256,256]{1,0:T(8,128)(2,1)} %constant.6.clone.weights_hbm), custom_call_target="tpu_custom_call" | custom-call | flops 4000000000 | bytes 8000000 | tf_op jit(solution)/shard_map/pick/pallas_call | solution.py:298
  4.4 3.3 %collective-permute-start = (f32[16,128]{1,0:T(8,128)S(1)}, f32[16,128]{1,0:T(8,128)S(1)}, u32[]{:S(2)}, u32[]{:S(2)}) collective-permute-start(f32[16,128]{1,0:T(8,128)S(1)} %get-tuple-element.21), channel_id=1, source_target_pairs={{0,8},{8,0},{16,24},{24,16},{32,40},{40,32},{48,56},{56,48},{64,72... | collective-permute-start | bytes 24584 | tf_op jit(solution)/shard_map/ppermute | solution.py:381
  7.7 0.8 %collective-permute-done = f32[16,128]{1,0:T(8,128)S(1)} collective-permute-done((f32[16,128]{1,0:T(8,128)S(1)}, f32[16,128]{1,0:T(8,128)S(1)}, u32[]{:S(2)}, u32[]{:S(2)}) %collective-permute-start) | collective-permute-done | bytes 8224 | tf_op jit(solution)/shard_map/ppermute | solution.py:381
  8.6 2.6 %collective-permute-start.3 = (f32[2,16,128]{2,1,0:T(8,128)S(1)}, f32[2,16,128]{2,1,0:T(8,128)S(1)}, u32[]{:S(2)}, u32[]{:S(2)}) collective-permute-start(f32[2,16,128]{2,1,0:T(8,128)S(1)} %pad_maximum_fusion.1), channel_id=1, source_target_pairs={{0,48},{8,56},{16,32},{24,40},{32,16},{40,24},{48,0},{56,8},{64,11... | collective-permute-start | bytes 49160 | tf_op jit(solution)/shard_map/ppermute | solution.py:381
  11.2 0.9 %collective-permute-start.1 = (f32[2,16,128]{2,1,0:T(8,128)S(1)}, f32[2,16,128]{2,1,0:T(8,128)S(1)}, u32[]{:S(2)}, u32[]{:S(2)}) collective-permute-start(f32[2,16,128]{2,1,0:T(8,128)S(1)} %pad_maximum_fusion.1), channel_id=1, source_target_pairs={{0,16},{8,24},{16,0},{24,8},{32,48},{40,56},{48,32},{56,40},{64,80... | collective-permute-start | bytes 49160 | tf_op jit(solution)/shard_map/ppermute | solution.py:381
  12.1 2.2 %own0.1.refs_5_ = f32[4,128,1024]{2,1,0:T(8,128)} custom-call(f32[4,128,1024]{2,1,0:T(8,128)S(1)} %get-tuple-element.18.refs_0_, s32[32,128]{1,0:T(8,128)S(1)} %get-tuple-element.19.refs_1_, f32[32,128]{1,0:T(8,128)S(1)} %get-tuple-element.30.refs_2_, bf16[256,256]{1,0:T(8,128)(2,1)S(1)} %copy-done.2, bf16[256,256]{1,0:T(8,128)(2,1)S(1)} %copy-done.1), custom_call_target="tpu_custom_call" | custom-call | flops 2200000000 | bytes 4400000 | tf_op jit(solution)/shard_map/own0/pallas_call | solution.py:326
  14.7 1.4 %collective-permute-start.6 = (f32[8,16,128]{2,1,0:T(8,128)S(1)}, f32[8,16,128]{2,1,0:T(8,128)S(1)}, u32[]{:S(2)}, u32[]{:S(2)}) collective-permute-start(f32[8,16,128]{2,1,0:T(8,128)S(1)} %pad_maximum_fusion.refs_0_), channel_id=1, source_target_pairs={{0,64},{8,72},{16,80},{24,88},{32,96},{40,104},{48,112},{56,120},{... | collective-permute-start | bytes 196616 | tf_op jit(solution)/shard_map/ppermute | solution.py:381
  16.1 1.9 %collective-permute-start.5 = (f32[8,16,128]{2,1,0:T(8,128)S(1)}, f32[8,16,128]{2,1,0:T(8,128)S(1)}, u32[]{:S(2)}, u32[]{:S(2)}) collective-permute-start(f32[8,16,128]{2,1,0:T(8,128)S(1)} %pad_maximum_fusion.refs_0_), channel_id=1, source_target_pairs={{0,192},{8,200},{16,208},{24,216},{32,224},{40,232},{48,240},{56,2... | collective-permute-start | bytes 196616 | tf_op jit(solution)/shard_map/ppermute | solution.py:381
  18.0 0.7 %collective-permute-start.4 = (f32[8,16,128]{2,1,0:T(8,128)S(1)}, f32[8,16,128]{2,1,0:T(8,128)S(1)}, u32[]{:S(2)}, u32[]{:S(2)}) collective-permute-start(f32[8,16,128]{2,1,0:T(8,128)S(1)} %pad_maximum_fusion.refs_0_), channel_id=1, source_target_pairs={{0,128},{8,136},{16,144},{24,152},{32,160},{40,168},{48,176},{56,1... | collective-permute-start | bytes 196616 | tf_op jit(solution)/shard_map/ppermute | solution.py:381
  18.7 1.4 %set0.1.refs_3_ = f32[2,4,128,256]{3,2,1,0:T(8,128)S(1)} custom-call(f32[8,16,128]{2,1,0:T(8,128)S(1)} %pad_maximum_fusion.refs_0_, f32[64,1024]{1,0:T(8,128)S(1)} %get-tuple-element.27.refs_1_, f32[64,1024]{1,0:T(8,128)S(1)} %get-tuple-element.28.refs_2_), custom_call_target="tpu_custom_call" | custom-call | flops 1600000000 | bytes 3200000 | tf_op jit(solution)/shard_map/set0/pallas_call | solution.py:352
  20.1 1.4 %set1.1.refs_3_ = f32[2,4,128,256]{3,2,1,0:T(8,128)S(1)} custom-call(f32[8,16,128]{2,1,0:T(8,128)S(1)} %collective-permute-done.6.refs_0_, f32[64,1024]{1,0:T(8,128)S(1)} %get-tuple-element.27.refs_1_, f32[64,1024]{1,0:T(8,128)S(1)} %get-tuple-element.28.refs_2_, f32[2,4,128,256]{3,2,1,0:T(8,128)S(1)} %set0.1.refs_3_), custom_call_target="tpu_custom_call", output_to_operand_aliasing={{}: (3, {})} | custom-call | flops 1600000000 | bytes 3200000 | tf_op jit(solution)/shard_map/set1/pallas_call | solution.py:352
  21.4 1.4 %set3.1.refs_3_ = f32[2,4,128,256]{3,2,1,0:T(8,128)S(1)} custom-call(f32[8,16,128]{2,1,0:T(8,128)S(1)} %collective-permute-done.5.refs_0_, f32[64,1024]{1,0:T(8,128)S(1)} %get-tuple-element.27.refs_1_, f32[64,1024]{1,0:T(8,128)S(1)} %get-tuple-element.28.refs_2_, f32[2,4,128,256]{3,2,1,0:T(8,128)S(1)} %set1.1.refs_3_), custom_call_target="tpu_custom_call", output_to_operand_aliasing={{}: (3, {})} | custom-call | flops 1600000000 | bytes 3200000 | tf_op jit(solution)/shard_map/set3/pallas_call | solution.py:352
  22.8 0.6 %collective-permute-done.4.refs_0_ = f32[8,16,128]{2,1,0:T(8,128)S(1)} collective-permute-done((f32[8,16,128]{2,1,0:T(8,128)S(1)}, f32[8,16,128]{2,1,0:T(8,128)S(1)}, u32[]{:S(2)}, u32[]{:S(2)}) %collective-permute-start.4) | collective-permute-done | bytes 65568 | tf_op jit(solution)/shard_map/ppermute | solution.py:381
  23.4 1.4 %set2.1 = (f32[2,4,128,256]{3,2,1,0:T(8,128)S(1)}, f32[8,128]{1,0:T(8,128)S(1)}) custom-call(f32[8,16,128]{2,1,0:T(8,128)S(1)} %collective-permute-done.4.refs_0_, f32[64,1024]{1,0:T(8,128)S(1)} %get-tuple-element.27.refs_1_, f32[64,1024]{1,0:T(8,128)S(1)} %get-tuple-element.28.refs_2_, ...), custom_call_target="tpu_custom_call", output_to_operand_aliasing={{0}: (3, {})} | custom-call | flops 1600000000 | bytes 3200000 | tf_op jit(solution)/shard_map/set2/pallas_call | solution.py:352
  24.8 2.8 %collective-permute-start.7 = (f32[2,4,128,256]{3,2,1,0:T(8,128)S(1)}, f32[2,4,128,256]{3,2,1,0:T(8,128)S(1)}, u32[]{:S(2)}, u32[]{:S(2)}) collective-permute-start(f32[2,4,128,256]{3,2,1,0:T(8,128)S(1)} %get-tuple-element.32.grid_ref), channel_id=1, source_target_pairs={{0,8},{8,0},{16,24},{24,16},{32,40},{40,32},{48,56},{56,48},{64,72... | collective-permute-start | bytes 3145736 | tf_op jit(solution)/shard_map/ppermute | solution.py:381
  27.5 1.2 %collective-permute-start.10 = (f32[8,128]{1,0:T(8,128)S(1)}, f32[8,128]{1,0:T(8,128)S(1)}, u32[]{:S(2)}, u32[]{:S(2)}) collective-permute-start(f32[8,128]{1,0:T(8,128)S(1)} %get-tuple-element.33), channel_id=1, source_target_pairs={{0,9},{1,8},{2,11},{3,10},{4,13},{5,12},{6,15},{7,14},{8,1},{9,0},... | collective-permute-start | bytes 12296 | tf_op jit(solution)/shard_map/ppermute | solution.py:386
  29.0 0.7 %collective-permute-start.8 = (f32[8,128]{1,0:T(8,128)S(1)}, f32[8,128]{1,0:T(8,128)S(1)}, u32[]{:S(2)}, u32[]{:S(2)}) collective-permute-start(f32[8,128]{1,0:T(8,128)S(1)} %get-tuple-element.33), channel_id=1, source_target_pairs={{0,8},{8,0},{16,24},{24,16},{32,40},{40,32},{48,56},{56,48},{64,72... | collective-permute-start | bytes 12296 | tf_op jit(solution)/shard_map/ppermute | solution.py:381
  29.7 2.2 %own2.1 = f32[4,128,1024]{2,1,0:T(8,128)} custom-call(f32[4,128,1024]{2,1,0:T(8,128)S(1)} %get-tuple-element.18.refs_0_, s32[32,128]{1,0:T(8,128)S(1)} %get-tuple-element.19.refs_1_, f32[32,128]{1,0:T(8,128)S(1)} %get-tuple-element.30.refs_2_, bf16[256,256]{1,0:T(8,128)(2,1)S(1)} %copy-done.2, ...), custom_call_target="tpu_custom_call", output_to_operand_aliasing={{}: (5, {})} | custom-call | flops 2200000000 | bytes 4400000 | tf_op jit(solution)/shard_map/own2/pallas_call | solution.py:326
  32.0 2.6 %collective-permute-start.11 = (f32[8,128]{1,0:T(8,128)S(1)}, f32[8,128]{1,0:T(8,128)S(1)}, u32[]{:S(2)}, u32[]{:S(2)}) collective-permute-start(f32[8,128]{1,0:T(8,128)S(1)} %add_add_fusion), channel_id=1, source_target_pairs={{0,3},{1,2},{2,1},{3,0},{4,7},{5,6},{6,5},{7,4},{8,11},{9,10},{10,... | collective-permute-start | bytes 12296 | tf_op jit(solution)/shard_map/ppermute | solution.py:381
  34.6 0.9 %decode.2.mine_ref = f32[2,128,1024]{2,1,0:T(8,128)S(1)} custom-call(f32[2,4,128,256]{3,2,1,0:T(8,128)S(1)} %get-tuple-element.32.grid_ref, bf16[256,256]{1,0:T(8,128)(2,1)S(1)} %copy-done.2, bf16[256,256]{1,0:T(8,128)(2,1)S(1)} %copy-done.1), custom_call_target="tpu_custom_call" | custom-call | flops 1600000000 | bytes 3200000 | tf_op jit(solution)/shard_map/decode/pallas_call | solution.py:365
  35.4 0.3 collective-permute-done.11
  35.7 3.8 %collective-permute-start.12 = (f32[8,128]{1,0:T(8,128)S(1)}, f32[8,128]{1,0:T(8,128)S(1)}, u32[]{:S(2)}, u32[]{:S(2)}) collective-permute-start(f32[8,128]{1,0:T(8,128)S(1)} %add.15.a_ref), channel_id=1, source_target_pairs={{0,36},{1,37},{2,38},{3,39},{8,44},{9,45},{10,46},{11,47},{16,52},... | collective-permute-start | bytes 12296 | tf_op jit(solution)/shard_map/ppermute | solution.py:398
  39.5 0.9 %decode.3.theirs_ref = f32[2,128,1024]{2,1,0:T(8,128)S(1)} custom-call(f32[2,4,128,256]{3,2,1,0:T(8,128)S(1)} %collective-permute-done.7.grid_ref, bf16[256,256]{1,0:T(8,128)(2,1)S(1)} %copy-done.2, bf16[256,256]{1,0:T(8,128)(2,1)S(1)} %copy-done.1), custom_call_target="tpu_custom_call" | custom-call | flops 1600000000 | bytes 3200000 | tf_op jit(solution)/shard_map/decode/pallas_call | solution.py:365
  40.5 1.5 %rescale.1 = f32[4,128,1024]{2,1,0:T(8,128)} custom-call(f32[2,128,1024]{2,1,0:T(8,128)S(1)} %decode.2.mine_ref, f32[2,128,1024]{2,1,0:T(8,128)S(1)} %decode.3.theirs_ref, f32[8,128]{1,0:T(8,128)S(1)} %add.15.a_ref, f32[8,128]{1,0:T(8,128)S(1)} %collective-permute-done.12.b_ref), custom_call_target="tpu_custom_call" | custom-call | flops 1000000000 | bytes 2000000 | tf_op jit(solution)/shard_map/rescale/pallas_call | solution.py:369
  (23 shorter events, 0.7 us)
Async XLA Ops:
  0.6 11.5 %copy-start.1 = (bf16[256,256]{1,0:T(8,128)(2,1)S(1)}, bf16[256,256]{1,0:T(8,128)(2,1)}, u32[]{:S(2)}) copy-start(bf16[256,256]{1,0:T(8,128)(2,1)} %constant.8.clone.refs_4_.rows_ref) | copy-start | bytes 393220
  0.6 11.5 %copy-start.2 = (bf16[256,256]{1,0:T(8,128)(2,1)S(1)}, bf16[256,256]{1,0:T(8,128)(2,1)}, u32[]{:S(2)}) copy-start(bf16[256,256]{1,0:T(8,128)(2,1)} %constant.7.clone.refs_3_.cols_ref) | copy-start | bytes 393220
  4.4 4.2 %collective-permute-start = (f32[16,128]{1,0:T(8,128)S(1)}, f32[16,128]{1,0:T(8,128)S(1)}, u32[]{:S(2)}, u32[]{:S(2)}) collective-permute-start(f32[16,128]{1,0:T(8,128)S(1)} %get-tuple-element.21), channel_id=1, source_target_pairs={{0,8},{8,0},{16,24},{24,16},{32,40},{40,32},{48,56},{56,48},{64,72... | collective-permute-start | bytes 24584 | tf_op jit(solution)/shard_map/ppermute | solution.py:381
  8.6 6.1 %collective-permute-start.3 = (f32[2,16,128]{2,1,0:T(8,128)S(1)}, f32[2,16,128]{2,1,0:T(8,128)S(1)}, u32[]{:S(2)}, u32[]{:S(2)}) collective-permute-start(f32[2,16,128]{2,1,0:T(8,128)S(1)} %pad_maximum_fusion.1), channel_id=1, source_target_pairs={{0,48},{8,56},{16,32},{24,40},{32,16},{40,24},{48,0},{56,8},{64,11... | collective-permute-start | bytes 49160 | tf_op jit(solution)/shard_map/ppermute | solution.py:381
  11.2 3.5 %collective-permute-start.2 = (f32[2,16,128]{2,1,0:T(8,128)S(1)}, f32[2,16,128]{2,1,0:T(8,128)S(1)}, u32[]{:S(2)}, u32[]{:S(2)}) collective-permute-start(f32[2,16,128]{2,1,0:T(8,128)S(1)} %pad_maximum_fusion.1), channel_id=1, source_target_pairs={{0,32},{8,40},{16,48},{24,56},{32,0},{40,8},{48,16},{56,24},{64,96... | collective-permute-start | bytes 49160 | tf_op jit(solution)/shard_map/ppermute | solution.py:381
  11.2 3.5 %collective-permute-start.1 = (f32[2,16,128]{2,1,0:T(8,128)S(1)}, f32[2,16,128]{2,1,0:T(8,128)S(1)}, u32[]{:S(2)}, u32[]{:S(2)}) collective-permute-start(f32[2,16,128]{2,1,0:T(8,128)S(1)} %pad_maximum_fusion.1), channel_id=1, source_target_pairs={{0,16},{8,24},{16,0},{24,8},{32,48},{40,56},{48,32},{56,40},{64,80... | collective-permute-start | bytes 49160 | tf_op jit(solution)/shard_map/ppermute | solution.py:381
  12.1 2.2 %copy-start = (s32[32,4,2,16,32]{4,3,2,1,0:T(8,128)S(1)}, s32[32,4,2,16,32]{4,3,2,1,0:T(8,128)}, u32[]{:S(2)}) copy-start(s32[32,4,2,16,32]{4,3,2,1,0:T(8,128)} %param.8) | copy-start | bytes 1572868
  14.7 5.3 %collective-permute-start.6 = (f32[8,16,128]{2,1,0:T(8,128)S(1)}, f32[8,16,128]{2,1,0:T(8,128)S(1)}, u32[]{:S(2)}, u32[]{:S(2)}) collective-permute-start(f32[8,16,128]{2,1,0:T(8,128)S(1)} %pad_maximum_fusion.refs_0_), channel_id=1, source_target_pairs={{0,64},{8,72},{16,80},{24,88},{32,96},{40,104},{48,112},{56,120},{... | collective-permute-start | bytes 196616 | tf_op jit(solution)/shard_map/ppermute | solution.py:381
  16.1 5.4 %collective-permute-start.5 = (f32[8,16,128]{2,1,0:T(8,128)S(1)}, f32[8,16,128]{2,1,0:T(8,128)S(1)}, u32[]{:S(2)}, u32[]{:S(2)}) collective-permute-start(f32[8,16,128]{2,1,0:T(8,128)S(1)} %pad_maximum_fusion.refs_0_), channel_id=1, source_target_pairs={{0,192},{8,200},{16,208},{24,216},{32,224},{40,232},{48,240},{56,2... | collective-permute-start | bytes 196616 | tf_op jit(solution)/shard_map/ppermute | solution.py:381
  18.0 5.4 %collective-permute-start.4 = (f32[8,16,128]{2,1,0:T(8,128)S(1)}, f32[8,16,128]{2,1,0:T(8,128)S(1)}, u32[]{:S(2)}, u32[]{:S(2)}) collective-permute-start(f32[8,16,128]{2,1,0:T(8,128)S(1)} %pad_maximum_fusion.refs_0_), channel_id=1, source_target_pairs={{0,128},{8,136},{16,144},{24,152},{32,160},{40,168},{48,176},{56,1... | collective-permute-start | bytes 196616 | tf_op jit(solution)/shard_map/ppermute | solution.py:381
  24.8 14.8 %collective-permute-start.7 = (f32[2,4,128,256]{3,2,1,0:T(8,128)S(1)}, f32[2,4,128,256]{3,2,1,0:T(8,128)S(1)}, u32[]{:S(2)}, u32[]{:S(2)}) collective-permute-start(f32[2,4,128,256]{3,2,1,0:T(8,128)S(1)} %get-tuple-element.32.grid_ref), channel_id=1, source_target_pairs={{0,8},{8,0},{16,24},{24,16},{32,40},{40,32},{48,56},{56,48},{64,72... | collective-permute-start | bytes 3145736 | tf_op jit(solution)/shard_map/ppermute | solution.py:381
  27.5 4.4 %collective-permute-start.10 = (f32[8,128]{1,0:T(8,128)S(1)}, f32[8,128]{1,0:T(8,128)S(1)}, u32[]{:S(2)}, u32[]{:S(2)}) collective-permute-start(f32[8,128]{1,0:T(8,128)S(1)} %get-tuple-element.33), channel_id=1, source_target_pairs={{0,9},{1,8},{2,11},{3,10},{4,13},{5,12},{6,15},{7,14},{8,1},{9,0},... | collective-permute-start | bytes 12296 | tf_op jit(solution)/shard_map/ppermute | solution.py:386
  28.7 3.2 %collective-permute-start.9 = (f32[8,128]{1,0:T(8,128)S(1)}, f32[8,128]{1,0:T(8,128)S(1)}, u32[]{:S(2)}, u32[]{:S(2)}) collective-permute-start(f32[8,128]{1,0:T(8,128)S(1)} %get-tuple-element.33), channel_id=1, source_target_pairs={{0,1},{1,0},{2,3},{3,2},{4,5},{5,4},{6,7},{7,6},{8,9},{9,8},{10,11... | collective-permute-start | bytes 12296 | tf_op jit(solution)/shard_map/ppermute | solution.py:381
  29.0 3.0 %collective-permute-start.8 = (f32[8,128]{1,0:T(8,128)S(1)}, f32[8,128]{1,0:T(8,128)S(1)}, u32[]{:S(2)}, u32[]{:S(2)}) collective-permute-start(f32[8,128]{1,0:T(8,128)S(1)} %get-tuple-element.33), channel_id=1, source_target_pairs={{0,8},{8,0},{16,24},{24,16},{32,40},{40,32},{48,56},{56,48},{64,72... | collective-permute-start | bytes 12296 | tf_op jit(solution)/shard_map/ppermute | solution.py:381
  32.0 3.8 %collective-permute-start.11 = (f32[8,128]{1,0:T(8,128)S(1)}, f32[8,128]{1,0:T(8,128)S(1)}, u32[]{:S(2)}, u32[]{:S(2)}) collective-permute-start(f32[8,128]{1,0:T(8,128)S(1)} %add_add_fusion), channel_id=1, source_target_pairs={{0,3},{1,2},{2,1},{3,0},{4,7},{5,6},{6,5},{7,4},{8,11},{9,10},{10,... | collective-permute-start | bytes 12296 | tf_op jit(solution)/shard_map/ppermute | solution.py:381
  35.7 4.8 %collective-permute-start.12 = (f32[8,128]{1,0:T(8,128)S(1)}, f32[8,128]{1,0:T(8,128)S(1)}, u32[]{:S(2)}, u32[]{:S(2)}) collective-permute-start(f32[8,128]{1,0:T(8,128)S(1)} %add.15.a_ref), channel_id=1, source_target_pairs={{0,36},{1,37},{2,38},{3,39},{8,44},{9,45},{10,46},{11,47},{16,52},... | collective-permute-start | bytes 12296 | tf_op jit(solution)/shard_map/ppermute | solution.py:398

commit v5 on v4

--- a/solution.py
+++ b/solution.py
@@ -89,82 +89,97 @@
     return lax.shift_right_logical(lax.broadcasted_iota(jnp.int32, shape, len(shape) - 1), 5) & 3
 
 
-def pick_kernel(m_hbm, g_hbm, idx_hbm, weights_hbm, v_ref, own_ref, mine_ref, theirs_ref, acc_ref, m_buf, g_buf, idx_buf, weights_ref, sems):
+def columns(acc, weights):
+    return times(lane_tiles(acc), weights)
+
+
+def rows_and_pick(half, weights, pos_ref, row, v_ref, to):
+    freq = lax.broadcasted_iota(jnp.int32, (GROUP, 128), 0)
+    place = lax.broadcasted_iota(jnp.int32, (256, 256), 0)
+    zeros = jnp.zeros((GROUP, 128), BF)
+    for t in range(TILES):
+        turned = [half[u * 128 : u * 128 + 128].T for u in (2 * t, 2 * t + 1)]
+        hi, lo = split(times(jnp.concatenate(turned, axis=0), weights))
+        pos = [pos_ref[pl.ds(row + a * 4 + t, 1), :] for a in range(2)]
+        hot = [(freq == lax.shift_right_logical(x, 6)).astype(F32).astype(BF) for x in pos]
+        pick = jnp.concatenate(
+            [
+                jnp.concatenate([hot[0], zeros], axis=1),
+                jnp.concatenate([zeros, hot[1]], axis=1),
+            ],
+            axis=0,
+        )
+        got = mm(jnp.concatenate([hi, lo], axis=1), jnp.concatenate([pick, pick], axis=0))
+        where = jnp.concatenate([(x & 63) + 64 * lane_block((1, 128)) for x in pos], axis=1)
+        v = jnp.sum(jnp.where(place == where, got, 0.0), axis=0, keepdims=True)
+        for a in range(2):
+            v_ref[pl.ds(to + a * 4 + t, 1), :] = v[:, a * 128 : a * 128 + 128]
+
+
+def theirs_kernel(m_hbm, g_hbm, idx_hbm, weights_hbm, v_ref, pos_ref, acc_ref, m_buf, g_buf, idx_buf, all_ref, weights_ref, sems):
     p = lax.axis_index("dp")
     core = p & 1
+    order = [HALF - HALF * core + i for i in range(HALF)] + [HALF * core + i for i in range(HALF)]
     small = [
         pltpu.make_async_copy(weights_hbm, weights_ref, sems.at[0]),
         pltpu.make_async_copy(idx_hbm.at[pl.ds(p * BLOCKS, BLOCKS)], idx_buf, sems.at[1]),
     ]
     large = [
         (
-            pltpu.make_async_copy(m_hbm.at[l], m_buf.at[l], sems.at[2 + 2 * l]),
-            pltpu.make_async_copy(g_hbm.at[l], g_buf.at[l], sems.at[3 + 2 * l]),
+            pltpu.make_async_copy(m_hbm.at[l], m_buf.at[i], sems.at[2 + 2 * i]),
+            pltpu.make_async_copy(g_hbm.at[l], g_buf.at[i], sems.at[3 + 2 * i]),
         )
-        for l in range(LAYERS)
+        for i, l in enumerate(order)
     ]
     for copy in (*large[0], *small, *large[1], *large[2], *large[3]):
         copy.start()
-    freq = lax.broadcasted_iota(jnp.int32, (GROUP, 128), 0)
-    place = lax.broadcasted_iota(jnp.int32, (256, 256), 0)
-    zeros = jnp.zeros((GROUP, 128), BF)
-
-    def columns(l):
-        acc = decay_rate * m_buf[l] + g_buf[l].astype(F32)
-        acc_ref[l] = acc
-        return times(lane_tiles(acc), weights_ref[...])
-
-    def rows_and_pick(l, half):
-        for t in range(TILES):
-            turned = [half[u * 128 : u * 128 + 128].T for u in (2 * t, 2 * t + 1)]
-            hi, lo = split(times(jnp.concatenate(turned, axis=0), weights_ref[...]))
-            pos = [own_ref[pl.ds(l * 8 + a * 4 + t, 1), :] for a in range(2)]
-            hot = [(freq == lax.shift_right_logical(x, 6)).astype(F32).astype(BF) for x in pos]
-            pick = jnp.concatenate(
-                [
-                    jnp.concatenate([hot[0], zeros], axis=1),
-                    jnp.concatenate([zeros, hot[1]], axis=1),
-                ],
-                axis=0,
-            )
-            got = mm(jnp.concatenate([hi, lo], axis=1), jnp.concatenate([pick, pick], axis=0))
-            where = jnp.concatenate([(x & 63) + 64 * lane_block((1, 128)) for x in pos], axis=1)
-            v = jnp.sum(jnp.where(place == where, got, 0.0), axis=0, keepdims=True)
-            for a in range(2):
-                v_ref[pl.ds(l * 8 + a * 4 + t, 1), :] = v[:, a * 128 : a * 128 + 128]
-
-    def wait(l):
-        for copy in large[l]:
+
+    def accumulate(i):
+        acc = decay_rate * m_buf[i] + g_buf[i].astype(F32)
+        acc_ref[i] = acc
+        return acc
+
+    def wait(i):
+        for copy in large[i]:
             copy.wait()
 
     wait(0)
     for copy in small:
         copy.wait()
-    own_ref[...] = jnp.concatenate([idx_buf[pl.ds(cj, 32, stride=4), :] for cj in range(4)], axis=1)
-    rows_and_pick(0, columns(0))
-    for l in range(1, LAYERS):
-        wait(l)
-    later = [columns(l) for l in range(1, LAYERS)]
-    for l in range(1, LAYERS):
-        rows_and_pick(l, later[l - 1])
-    mine_ref[...] = v_ref[pl.ds(pl.multiple_of(core * 16, 16), 16), :]
-    theirs_ref[...] = v_ref[pl.ds(pl.multiple_of(16 - core * 16, 16), 16), :]
-
-
-def own_kernel(layers, acc_ref, own_ref, v_ref, cols_ref, rows_ref, *rest):
+    all_ref[...] = jnp.concatenate([idx_buf[pl.ds(cj, 32, stride=4), :] for cj in range(4)], axis=1)
+    pos_ref[:16] = all_ref[pl.ds(pl.multiple_of(16 - core * 16, 16), 16), :]
+    pos_ref[16:] = all_ref[pl.ds(pl.multiple_of(core * 16, 16), 16), :]
+    rows_and_pick(columns(accumulate(0), weights_ref[...]), weights_ref[...], pos_ref, 0, v_ref, 0)
+    for i in range(1, LAYERS):
+        wait(i)
+    rows_and_pick(columns(accumulate(1), weights_ref[...]), weights_ref[...], pos_ref, 8, v_ref, 8)
+    for i in range(HALF, LAYERS):
+        accumulate(i)
+
+
+def mine_kernel(acc_ref, pos_ref, weights_ref, v_ref):
+    halves_of = [columns(acc_ref[HALF + i], weights_ref[...]) for i in range(HALF)]
+    for i in range(HALF):
+        rows_and_pick(halves_of[i], weights_ref[...], pos_ref, 16 + 8 * i, v_ref, 8 * i)
+
+
+def own_kernel(which, acc_ref, own_ref, v_ref, cols_ref, rows_ref, *rest):
     out_hbm, out_buf, sems = rest[-3:]
     freq = lax.broadcasted_iota(jnp.int32, (GROUP, 128), 0)
     place = lax.broadcasted_iota(jnp.int32, (256, 128), 0)
     zeros = jnp.zeros((GROUP, 128), BF)
     copies = []
-    for i, l in enumerate(layers):
+    core = lax.axis_index("dp") & 1
+    start = HALF - HALF * core if which == 0 else HALF * core
+    for i in range(HALF):
+        l = which * HALF + i
         grids = []
         for t in range(TILES):
             left, right = [], []
             for a in range(2):
                 row = l * 8 + a * 4 + t
                 pos = own_ref[pl.ds(row, 1), :]
-                v = v_ref[pl.ds(row, 1), :]
+                v = v_ref[pl.ds(i * 8 + a * 4 + t, 1), :]
                 left.append(split(jnp.where(freq == lax.shift_right_logical(pos, 6), v, 0.0)))
                 right.append((place == (pos & 63) + 64 * lane_block((1, 128))).astype(F32).astype(BF))
             rows = []
@@ -176,7 +191,7 @@
         for t, tile in enumerate(back(grids, cols_ref[...], rows_ref[...])):
             s = slice(t * 256, t * 256 + 256)
             out_buf[i, :, s] = acc_ref[l, :, s] - tile
-        copies.append(pltpu.make_async_copy(out_buf.at[i], out_hbm.at[l], sems.at[i]))
+        copies.append(pltpu.make_async_copy(out_buf.at[i], out_hbm.at[start + i], sems.at[i]))
         copies[-1].start()
     for copy in copies:
         copy.wait()
@@ -192,7 +207,8 @@
         fc_ref[:, q * 128 : q * 128 + 128] = (pos & 63).astype(F32)
 
 
-def set_kernel(number, first, last, v_ref, fr_ref, fc_ref, *rest):
+def set_kernel(places, first, last, *rest):
+    v_refs, (fr_ref, fc_ref), rest = rest[: len(places)], rest[len(places) : len(places) + 2], rest[len(places) + 2 :]
     old_ref = None
     if not first:
         old_ref, rest = rest[0], rest[1:]
@@ -203,32 +219,36 @@
     else:
         grid_ref, val_ref = rest
     lane = lane_block((16, 128))
-    for q in range(SET // 4):
-        x = [v_ref[4 * q + j] for j in range(4)]
-        for cj in range(4):
-            y = jnp.zeros((16, 128), F32)
-            for j in range(4):
-                moved = x[j] if j == cj else pltpu.roll(x[j], ((j - cj) * 32) % 128, 1)
-                y = jnp.where(lane == j, moved, y)
-            val_ref[cj, :, q * 128 : q * 128 + 128] = y
+    for n, v_ref in enumerate(v_refs):
+        for q in range(SET // 4):
+            x = [v_ref[4 * q + j] for j in range(4)]
+            for cj in range(4):
+                y = jnp.zeros((16, 128), F32)
+                for j in range(4):
+                    moved = x[j] if j == cj else pltpu.roll(x[j], ((j - cj) * 32) % 128, 1)
+                    y = jnp.where(lane == j, moved, y)
+                start = (n * SET // 4 + q) * 128
+                val_ref[cj, :, start : start + 128] = y
     wide = 32 * SET
     freq = lax.broadcasted_iota(jnp.int32, (GROUP, wide), 0).astype(F32).astype(BF)
-    s = slice(number * wide, number * wide + wide)
     zero, one = jnp.zeros((), BF), jnp.ones((), BF)
-
-    def body(l, carry):
+    for l in range(HALF):
         squares = jnp.zeros((1, 256), F32)
         for i in range(2 * TILES):
             a, t = i // TILES, i % TILES
             parts = []
             for cj in range(4):
                 row = l * 32 + i * 4 + cj
-                fr = fr_ref[pl.ds(row, 1), s].astype(BF)
-                fc = fc_ref[pl.ds(row, 1), s].astype(BF)
-                hi, lo = split(val_ref[cj, pl.ds(l * 8 + i, 1), :])
-                at = freq == fr
-                left = jnp.concatenate([jnp.where(at, hi, zero), jnp.where(at, lo, zero)], axis=0)
-                both = mm_t(left, jnp.where(freq == fc, one, zero))
+                left, right = [], []
+                for n, place in enumerate(places):
+                    s = slice(place * wide, place * wide + wide)
+                    fr = fr_ref[pl.ds(row, 1), s].astype(BF)
+                    fc = fc_ref[pl.ds(row, 1), s].astype(BF)
+                    hi, lo = split(val_ref[cj, pl.ds(l * 8 + i, 1), n * wide : n * wide + wide])
+                    at = freq == fr
+                    left.append(jnp.concatenate([jnp.where(at, hi, zero), jnp.where(at, lo, zero)], axis=0))
+                    right.append(jnp.where(freq == fc, one, zero))
+                both = mm_t(jnp.concatenate(left, axis=1), jnp.concatenate(right, axis=1))
                 parts.append(both[:GROUP] + both[GROUP:])
             grid = jnp.concatenate(parts, axis=1)
             if old_ref is not None:
@@ -238,10 +258,6 @@
                 squares = squares + jnp.sum(grid * grid, axis=0, keepdims=True)
         if last:
             sq_ref[pl.ds(first_layer + l, 1), :] = squares[:, :128] + squares[:, 128:]
-        return carry
-
-    for l in range(HALF):
-        body(l, 0)
 
 
 def decode_kernel(grid_ref, cols_ref, rows_ref, out_ref):
@@ -294,42 +310,45 @@
     )
 
 
-def pick(m, g, idx, weights):
+def pick_theirs(m, g, idx, weights):
     return call(
-        pick_kernel,
-        "pick",
+        theirs_kernel,
+        "theirs",
         [HB] * 4,
-        [VM] * 5,
+        [VM] * 3,
         [
-            jax.ShapeDtypeStruct((32, 128), F32),
+            jax.ShapeDtypeStruct((16, 128), F32),
             jax.ShapeDtypeStruct((32, 128), jnp.int32),
-            jax.ShapeDtypeStruct((16, 128), F32),
-            jax.ShapeDtypeStruct((16, 128), F32),
             DECODED,
         ],
         [
             pltpu.VMEM((LAYERS, ROWS, COLS), F32),
             pltpu.VMEM((LAYERS, ROWS, COLS), BF),
             pltpu.VMEM((BLOCKS, TOPK), jnp.int32),
+            pltpu.VMEM((32, 128), jnp.int32),
             pltpu.VMEM(weights.shape, BF),
             pltpu.SemaphoreType.DMA((2 + 2 * LAYERS,)),
         ],
-        4.0,
+        2.5,
     )(m, g, idx, weights)
 
 
-def own_update(layers, acc, own, v, cols, rows, out=None):
-    ins, more = [acc, own, v, cols, rows], {}
+def pick_mine(acc, pos, weights):
+    return call(mine_kernel, "mine", [VM] * 3, VM, jax.ShapeDtypeStruct((16, 128), F32), (), 1.7)(acc, pos, weights)
+
+
+def own_update(which, acc, pos, v, cols, rows, out=None):
+    ins, more = [acc, pos, v, cols, rows], {}
     if out is not None:
         ins.append(out)
         more = dict(input_output_aliases={5: 0})
     return call(
-        lambda *refs: own_kernel(layers, *refs),
-        f"own{layers[0]}",
+        lambda *refs: own_kernel(which, *refs),
+        f"own{which}",
         [VM] * 5 + [HB] * (len(ins) - 5),
         HB,
         DECODED,
-        [pltpu.VMEM((len(layers), ROWS, COLS), F32), pltpu.SemaphoreType.DMA((len(layers),))],
+        [pltpu.VMEM((HALF, ROWS, COLS), F32), pltpu.SemaphoreType.DMA((HALF,))],
         2.2,
         **more,
     )(*ins)
@@ -340,23 +359,23 @@
     return call(arrange_kernel, "arrange", [VM], [VM, VM], [shape, shape], (), 0.5)(idx)
 
 
-def add_set(number, last, v, fr, fc, old):
-    ins, outs, shapes, more = [v, fr, fc], [VM], [GRIDS], {}
+def add_sets(places, last, sets, fr, fc, old):
+    ins, outs, shapes, more = [*(sets[s] for s in places), fr, fc], [VM], [GRIDS], {}
     first = old is None
     if not first:
+        more = dict(input_output_aliases={len(ins): 0})
         ins.append(old)
-        more = dict(input_output_aliases={3: 0})
     if last:
         outs.append(VM)
         shapes.append(jax.ShapeDtypeStruct((8, 128), F32))
     return call(
-        lambda *refs: set_kernel(number, first, last, *refs),
-        f"set{number}",
+        lambda *refs: set_kernel(places, first, last, *refs),
+        "sets" + "".join(str(s) for s in places),
         [VM] * len(ins),
         outs,
         shapes,
-        [pltpu.VMEM((4, 16, 32 * SET), F32)],
-        1.6,
+        [pltpu.VMEM((4, 16, 32 * SET * len(places)), F32)],
+        1.4 * len(places),
         **more,
     )(*ins)
 
@@ -403,27 +422,28 @@
     idx = kept_index.reshape(REPLICAS * BLOCKS, TOPK)
     forward, back_cols, back_rows = (jnp.asarray(x) for x in constants())
     held = [pltpu.with_memory_space_constraint(x, pltpu.HBM) for x in (m, g, idx, forward)]
-    v, own, mine, theirs, acc = pick(*held)
+    theirs, pos, acc = pick_theirs(*held)
+    mine = pick_mine(acc, pos, forward)
 
     x = jnp.stack([mine, turn(theirs, "dp", REPLICAS, 1)])
-    x, v, idx = lax.optimization_barrier((x, v, idx))
+    x, theirs, idx = lax.optimization_barrier((x, theirs, idx))
     x = jnp.concatenate([x] + [turn(x, "dp", REPLICAS, b) for b in (2, 4, 6)], axis=0)
     fr, fc = arrange(idx)
-    momentum_out = own_update((0, 1), acc, own, v, back_cols, back_rows)
+    momentum_out = own_update(0, acc, pos, theirs, back_cols, back_rows)
     x, momentum_out = lax.optimization_barrier((x, momentum_out))
-    order = (0, 1, 3, 2)
-    sets = {s: x if s == 0 else turn(x, "dp", REPLICAS, 8 * s) for s in order}
+    calls = ((0,), (1,), (3,), (2,))
+    sets = {s: x if s == 0 else turn(x, "dp", REPLICAS, 8 * s) for c in calls for s in c}
     grid = None
-    for s in order[:-1]:
-        (grid,) = add_set(s, False, sets[s], fr, fc, grid)
-    grid, squares = add_set(order[-1], True, sets[order[-1]], fr, fc, grid)
+    for places in calls[:-1]:
+        (grid,) = add_sets(places, False, sets, fr, fc, grid)
+    grid, squares = add_sets(calls[-1], True, sets, fr, fc, grid)
 
     other_grid = turn(grid, "dp", REPLICAS, 1)
     beside = turn(squares, "dp", REPLICAS, 1)
     near = turn(squares, "tensor", 8, 1)
     across_near = near_other_core(squares)
-    squares, v = lax.optimization_barrier((squares, v))
-    momentum_out = own_update((2, 3), acc, own, v, back_cols, back_rows, momentum_out)
+    squares, mine = lax.optimization_barrier((squares, mine))
+    momentum_out = own_update(1, acc, pos, mine, back_cols, back_rows, momentum_out)
     decoded = decode(grid, back_cols, back_rows)
     other = decode(other_grid, back_cols, back_rows)
     total = squares + beside + near + across_near

time: 43 us -> 42.6 us (level)
  waiting for transfers between devices: 1.81 us -> 0.6 us
  Pallas kernels: 17.2 us -> 17.8 us
    ppermute x11, waiting for transfers between devices: 1.71 us -> 0.5 us  [turn(): return lax.ppermute(x, axis, [(i, i ^ bit) for i in range(size)])]
    pallas_call x7 -> x8, Pallas kernels: 13.6 us -> 14.3 us  [the longest x4 5.45 us: add_sets(): call(lambda *refs: set_kernel(places, first, last, *refs), 'sets' + ''.jo...]
  transfers between devices with their start and end apart: 13 -> 13, of which waited for: 4 -> 4; matrix products, arithmetic and copies ran while one was open for 0% -> 0% of each run, Pallas kernels for 25% -> 28%
where the time goes in v5:
time: 42.6 us; the launch traced here: 41.8 us
  starting transfers between devices  22.3 us (52%)
  Pallas kernels  17.8 us (42%)
  between operations  0.98 us (2%)
  waiting for transfers between devices  0.6 us (1%)
    ppermute x11, starting transfers between devices, turn(): return lax.ppermute(x, axis, [(i, i ^ bit) for i in range(size)])  17.3 us
    pallas_call x4, Pallas kernels, add_sets(): call(lambda *refs: set_kernel(places, first, last, *refs), 'sets' + ''.jo...  5.45 us
    pallas_call x2, Pallas kernels, own_update(): call(lambda *refs: own_kernel(which, *refs), f'own{which}', [VM] * 5 + [H...  4.45 us
    ppermute x1, starting transfers between devices, across(): return lax.ppermute(x, ('dp', 'tensor'), pairs)  3.78 us
    pallas_call x1, Pallas kernels, pick_theirs(): call(theirs_kernel, 'theirs', [HB] * 4, [VM] * 3, [jax.ShapeDtypeStruct((...  3.26 us
    pallas_call x2, Pallas kernels, decode(): call(decode_kernel, 'decode', [VM] * 3, VM, HALVED, (), 1.6)  1.78 us
    pallas_call x1, Pallas kernels, rescale(): call(scale_kernel, 'rescale', [VM] * 4, HB, DECODED, [pltpu.VMEM((LAYERS,...  1.49 us
    ppermute x1, starting transfers between devices, near_other_core(): return lax.ppermute(x, ('dp', 'tensor'), pairs)  1.2 us
  transfers between devices with their start and end apart: 13, of which 4 were waited for; matrix products, arithmetic and copies ran while one was open for 0% of the time, Pallas kernels for 28%

profile of v5, /device:TPU:1, one launch (start us, length us, event | category | flops | bytes accessed | tf_op | source)
XLA Modules:
  0.0 41.8 jit_solution(8732134591506481314)
XLA Ops:
  0.6 3.3 %theirs.1 = (f32[16,128]{1,0:T(8,128)S(1)}, s32[32,128]{1,0:T(8,128)S(1)}, f32[4,128,1024]{2,1,0:T(8,128)S(1)}) custom-call(f32[4,128,1024]{2,1,0:T(8,128)} %bitcast.10, bf16[4,128,1024]{2,1,0:T(8,128)(2,1)} %bitcast.11, s32[4096,32]{1,0:T(8,128)} %bitcast.6, bf16[256,256]{1,0:T(8,128)(2,1)} %constant.6.clone.weights_hbm.weights_ref), custom_call_target="tpu_custom_call" | custom-call | flops 2500000000 | bytes 5000000 | tf_op jit(solution)/shard_map/theirs/pallas_call | solution.py:314
  3.9 3.3 %collective-permute-start = (f32[16,128]{1,0:T(8,128)S(1)}, f32[16,128]{1,0:T(8,128)S(1)}, u32[]{:S(2)}, u32[]{:S(2)}) collective-permute-start(f32[16,128]{1,0:T(8,128)S(1)} %get-tuple-element.20.refs_2_), channel_id=1, source_target_pairs={{0,8},{8,0},{16,24},{24,16},{32,40},{40,32},{48,56},{56,48},{64,72... | collective-permute-start | bytes 24584 | tf_op jit(solution)/shard_map/ppermute | solution.py:400
  7.2 1.1 %mine.1.refs_2_ = f32[16,128]{1,0:T(8,128)S(1)} custom-call(f32[4,128,1024]{2,1,0:T(8,128)S(1)} %get-tuple-element.16.acc_ref.refs_0_, s32[32,128]{1,0:T(8,128)S(1)} %get-tuple-element.17.pos_ref.refs_1_, bf16[256,256]{1,0:T(8,128)(2,1)S(1)} %copy-done.3), custom_call_target="tpu_custom_call" | custom-call | flops 1700000000 | bytes 3400000 | tf_op jit(solution)/shard_map/mine/pallas_call | solution.py:337
  8.4 2.7 %collective-permute-start.3 = (f32[2,16,128]{2,1,0:T(8,128)S(1)}, f32[2,16,128]{2,1,0:T(8,128)S(1)}, u32[]{:S(2)}, u32[]{:S(2)}) collective-permute-start(f32[2,16,128]{2,1,0:T(8,128)S(1)} %pad_maximum_fusion.1), channel_id=1, source_target_pairs={{0,48},{8,56},{16,32},{24,40},{32,16},{40,24},{48,0},{56,8},{64,11... | collective-permute-start | bytes 49160 | tf_op jit(solution)/shard_map/ppermute | solution.py:400
  11.1 0.9 %collective-permute-start.1 = (f32[2,16,128]{2,1,0:T(8,128)S(1)}, f32[2,16,128]{2,1,0:T(8,128)S(1)}, u32[]{:S(2)}, u32[]{:S(2)}) collective-permute-start(f32[2,16,128]{2,1,0:T(8,128)S(1)} %pad_maximum_fusion.1), channel_id=1, source_target_pairs={{0,16},{8,24},{16,0},{24,8},{32,48},{40,56},{48,32},{56,40},{64,80... | collective-permute-start | bytes 49160 | tf_op jit(solution)/shard_map/ppermute | solution.py:400
  12.0 2.2 %own0.1.refs_5_ = f32[4,128,1024]{2,1,0:T(8,128)} custom-call(f32[4,128,1024]{2,1,0:T(8,128)S(1)} %get-tuple-element.16.acc_ref.refs_0_, s32[32,128]{1,0:T(8,128)S(1)} %get-tuple-element.17.pos_ref.refs_1_, f32[16,128]{1,0:T(8,128)S(1)} %get-tuple-element.20.refs_2_, bf16[256,256]{1,0:T(8,128)(2,1)S(1)} %copy-done.2, bf16[256,256]{1,0:T(8,128)(2,1)S(1)} %copy-done.1), custom_call_target="tpu_custom_call" | custom-call | flops 2200000000 | bytes 4400000 | tf_op jit(solution)/shard_map/own0/pallas_call | solution.py:345
  14.3 0.3 arrange.1
  14.6 1.4 %collective-permute-start.6 = (f32[8,16,128]{2,1,0:T(8,128)S(1)}, f32[8,16,128]{2,1,0:T(8,128)S(1)}, u32[]{:S(2)}, u32[]{:S(2)}) collective-permute-start(f32[8,16,128]{2,1,0:T(8,128)S(1)} %pad_maximum_fusion.refs_0_), channel_id=1, source_target_pairs={{0,64},{8,72},{16,80},{24,88},{32,96},{40,104},{48,112},{56,120},{... | collective-permute-start | bytes 196616 | tf_op jit(solution)/shard_map/ppermute | solution.py:400
  16.0 1.9 %collective-permute-start.5 = (f32[8,16,128]{2,1,0:T(8,128)S(1)}, f32[8,16,128]{2,1,0:T(8,128)S(1)}, u32[]{:S(2)}, u32[]{:S(2)}) collective-permute-start(f32[8,16,128]{2,1,0:T(8,128)S(1)} %pad_maximum_fusion.refs_0_), channel_id=1, source_target_pairs={{0,192},{8,200},{16,208},{24,216},{32,224},{40,232},{48,240},{56,2... | collective-permute-start | bytes 196616 | tf_op jit(solution)/shard_map/ppermute | solution.py:400
  17.9 0.7 %collective-permute-start.4 = (f32[8,16,128]{2,1,0:T(8,128)S(1)}, f32[8,16,128]{2,1,0:T(8,128)S(1)}, u32[]{:S(2)}, u32[]{:S(2)}) collective-permute-start(f32[8,16,128]{2,1,0:T(8,128)S(1)} %pad_maximum_fusion.refs_0_), channel_id=1, source_target_pairs={{0,128},{8,136},{16,144},{24,152},{32,160},{40,168},{48,176},{56,1... | collective-permute-start | bytes 196616 | tf_op jit(solution)/shard_map/ppermute | solution.py:400
  18.6 1.4 %sets0.1.refs_3_ = f32[2,4,128,256]{3,2,1,0:T(8,128)S(1)} custom-call(f32[8,16,128]{2,1,0:T(8,128)S(1)} %pad_maximum_fusion.refs_0_, f32[64,1024]{1,0:T(8,128)S(1)} %get-tuple-element.23.refs_1_, f32[64,1024]{1,0:T(8,128)S(1)} %get-tuple-element.24.refs_2_), custom_call_target="tpu_custom_call" | custom-call | flops 1400000000 | bytes 2800000 | tf_op jit(solution)/shard_map/sets0/pallas_call | solution.py:371
  20.0 1.4 %sets1.1.refs_3_ = f32[2,4,128,256]{3,2,1,0:T(8,128)S(1)} custom-call(f32[8,16,128]{2,1,0:T(8,128)S(1)} %collective-permute-done.6.refs_0_, f32[64,1024]{1,0:T(8,128)S(1)} %get-tuple-element.23.refs_1_, f32[64,1024]{1,0:T(8,128)S(1)} %get-tuple-element.24.refs_2_, f32[2,4,128,256]{3,2,1,0:T(8,128)S(1)} %sets0.1.refs_3_), custom_call_target="tpu_custom_call", output_to_operand_aliasing={{}: (3, {})} | custom-call | flops 1400000000 | bytes 2800000 | tf_op jit(solution)/shard_map/sets1/pallas_call | solution.py:371
  21.4 1.4 %sets3.1.refs_3_ = f32[2,4,128,256]{3,2,1,0:T(8,128)S(1)} custom-call(f32[8,16,128]{2,1,0:T(8,128)S(1)} %collective-permute-done.5.refs_0_, f32[64,1024]{1,0:T(8,128)S(1)} %get-tuple-element.23.refs_1_, f32[64,1024]{1,0:T(8,128)S(1)} %get-tuple-element.24.refs_2_, f32[2,4,128,256]{3,2,1,0:T(8,128)S(1)} %sets1.1.refs_3_), custom_call_target="tpu_custom_call", output_to_operand_aliasing={{}: (3, {})} | custom-call | flops 1400000000 | bytes 2800000 | tf_op jit(solution)/shard_map/sets3/pallas_call | solution.py:371
  22.9 1.4 %sets2.1 = (f32[2,4,128,256]{3,2,1,0:T(8,128)S(1)}, f32[8,128]{1,0:T(8,128)S(1)}) custom-call(f32[8,16,128]{2,1,0:T(8,128)S(1)} %collective-permute-done.4.refs_0_, f32[64,1024]{1,0:T(8,128)S(1)} %get-tuple-element.23.refs_1_, f32[64,1024]{1,0:T(8,128)S(1)} %get-tuple-element.24.refs_2_, ...), custom_call_target="tpu_custom_call", output_to_operand_aliasing={{0}: (3, {})} | custom-call | flops 1400000000 | bytes 2800000 | tf_op jit(solution)/shard_map/sets2/pallas_call | solution.py:371
  24.3 2.9 %collective-permute-start.7 = (f32[2,4,128,256]{3,2,1,0:T(8,128)S(1)}, f32[2,4,128,256]{3,2,1,0:T(8,128)S(1)}, u32[]{:S(2)}, u32[]{:S(2)}) collective-permute-start(f32[2,4,128,256]{3,2,1,0:T(8,128)S(1)} %get-tuple-element.28.grid_ref), channel_id=1, source_target_pairs={{0,8},{8,0},{16,24},{24,16},{32,40},{40,32},{48,56},{56,48},{64,72... | collective-permute-start | bytes 3145736 | tf_op jit(solution)/shard_map/ppermute | solution.py:400
  27.1 1.2 %collective-permute-start.10 = (f32[8,128]{1,0:T(8,128)S(1)}, f32[8,128]{1,0:T(8,128)S(1)}, u32[]{:S(2)}, u32[]{:S(2)}) collective-permute-start(f32[8,128]{1,0:T(8,128)S(1)} %get-tuple-element.29), channel_id=1, source_target_pairs={{0,9},{1,8},{2,11},{3,10},{4,13},{5,12},{6,15},{7,14},{8,1},{9,0},... | collective-permute-start | bytes 12296 | tf_op jit(solution)/shard_map/ppermute | solution.py:405
  28.6 0.7 %collective-permute-start.8 = (f32[8,128]{1,0:T(8,128)S(1)}, f32[8,128]{1,0:T(8,128)S(1)}, u32[]{:S(2)}, u32[]{:S(2)}) collective-permute-start(f32[8,128]{1,0:T(8,128)S(1)} %get-tuple-element.29), channel_id=1, source_target_pairs={{0,8},{8,0},{16,24},{24,16},{32,40},{40,32},{48,56},{56,48},{64,72... | collective-permute-start | bytes 12296 | tf_op jit(solution)/shard_map/ppermute | solution.py:400
  29.3 2.2 %own1.1 = f32[4,128,1024]{2,1,0:T(8,128)} custom-call(f32[4,128,1024]{2,1,0:T(8,128)S(1)} %get-tuple-element.16.acc_ref.refs_0_, s32[32,128]{1,0:T(8,128)S(1)} %get-tuple-element.17.pos_ref.refs_1_, f32[16,128]{1,0:T(8,128)S(1)} %mine.1.refs_2_, bf16[256,256]{1,0:T(8,128)(2,1)S(1)} %copy-done.2, ...), custom_call_target="tpu_custom_call", output_to_operand_aliasing={{}: (5, {})} | custom-call | flops 2200000000 | bytes 4400000 | tf_op jit(solution)/shard_map/own1/pallas_call | solution.py:345
  31.6 2.6 %collective-permute-start.11 = (f32[8,128]{1,0:T(8,128)S(1)}, f32[8,128]{1,0:T(8,128)S(1)}, u32[]{:S(2)}, u32[]{:S(2)}) collective-permute-start(f32[8,128]{1,0:T(8,128)S(1)} %add_add_fusion), channel_id=1, source_target_pairs={{0,3},{1,2},{2,1},{3,0},{4,7},{5,6},{6,5},{7,4},{8,11},{9,10},{10,... | collective-permute-start | bytes 12296 | tf_op jit(solution)/shard_map/ppermute | solution.py:400
  34.1 0.9 %decode.2.mine_ref = f32[2,128,1024]{2,1,0:T(8,128)S(1)} custom-call(f32[2,4,128,256]{3,2,1,0:T(8,128)S(1)} %get-tuple-element.28.grid_ref, bf16[256,256]{1,0:T(8,128)(2,1)S(1)} %copy-done.2, bf16[256,256]{1,0:T(8,128)(2,1)S(1)} %copy-done.1), custom_call_target="tpu_custom_call" | custom-call | flops 1600000000 | bytes 3200000 | tf_op jit(solution)/shard_map/decode/pallas_call | solution.py:384
  35.0 0.3 collective-permute-done.11
  35.3 3.8 %collective-permute-start.12 = (f32[8,128]{1,0:T(8,128)S(1)}, f32[8,128]{1,0:T(8,128)S(1)}, u32[]{:S(2)}, u32[]{:S(2)}) collective-permute-start(f32[8,128]{1,0:T(8,128)S(1)} %add.15.a_ref), channel_id=1, source_target_pairs={{0,36},{1,37},{2,38},{3,39},{8,44},{9,45},{10,46},{11,47},{16,52},... | collective-permute-start | bytes 12296 | tf_op jit(solution)/shard_map/ppermute | solution.py:417
  39.1 0.9 %decode.3.theirs_ref = f32[2,128,1024]{2,1,0:T(8,128)S(1)} custom-call(f32[2,4,128,256]{3,2,1,0:T(8,128)S(1)} %collective-permute-done.7.grid_ref, bf16[256,256]{1,0:T(8,128)(2,1)S(1)} %copy-done.2, bf16[256,256]{1,0:T(8,128)(2,1)S(1)} %copy-done.1), custom_call_target="tpu_custom_call" | custom-call | flops 1600000000 | bytes 3200000 | tf_op jit(solution)/shard_map/decode/pallas_call | solution.py:384
  40.1 1.5 %rescale.1 = f32[4,128,1024]{2,1,0:T(8,128)} custom-call(f32[2,128,1024]{2,1,0:T(8,128)S(1)} %decode.2.mine_ref, f32[2,128,1024]{2,1,0:T(8,128)S(1)} %decode.3.theirs_ref, f32[8,128]{1,0:T(8,128)S(1)} %add.15.a_ref, f32[8,128]{1,0:T(8,128)S(1)} %collective-permute-done.12.b_ref), custom_call_target="tpu_custom_call" | custom-call | flops 1000000000 | bytes 2000000 | tf_op jit(solution)/shard_map/rescale/pallas_call | solution.py:388
  (26 shorter events, 0.6 us)
Async XLA Ops:
  0.6 6.6 %copy-start.3 = (bf16[256,256]{1,0:T(8,128)(2,1)S(1)}, bf16[256,256]{1,0:T(8,128)(2,1)}, u32[]{:S(2)}) copy-start(bf16[256,256]{1,0:T(8,128)(2,1)} %constant.6.clone.weights_hbm.weights_ref) | copy-start | bytes 393220
  3.9 4.4 %collective-permute-start = (f32[16,128]{1,0:T(8,128)S(1)}, f32[16,128]{1,0:T(8,128)S(1)}, u32[]{:S(2)}, u32[]{:S(2)}) collective-permute-start(f32[16,128]{1,0:T(8,128)S(1)} %get-tuple-element.20.refs_2_), channel_id=1, source_target_pairs={{0,8},{8,0},{16,24},{24,16},{32,40},{40,32},{48,56},{56,48},{64,72... | collective-permute-start | bytes 24584 | tf_op jit(solution)/shard_map/ppermute | solution.py:400
  7.2 4.8 %copy-start.1 = (bf16[256,256]{1,0:T(8,128)(2,1)S(1)}, bf16[256,256]{1,0:T(8,128)(2,1)}, u32[]{:S(2)}) copy-start(bf16[256,256]{1,0:T(8,128)(2,1)} %constant.8.clone.refs_4_.rows_ref) | copy-start | bytes 393220
  7.2 4.8 %copy-start.2 = (bf16[256,256]{1,0:T(8,128)(2,1)S(1)}, bf16[256,256]{1,0:T(8,128)(2,1)}, u32[]{:S(2)}) copy-start(bf16[256,256]{1,0:T(8,128)(2,1)} %constant.7.clone.refs_3_.cols_ref) | copy-start | bytes 393220
  8.4 5.9 %copy-start = (s32[32,4,2,16,32]{4,3,2,1,0:T(8,128)S(1)}, s32[32,4,2,16,32]{4,3,2,1,0:T(8,128)}, u32[]{:S(2)}) copy-start(s32[32,4,2,16,32]{4,3,2,1,0:T(8,128)} %param.8) | copy-start | bytes 1572868
  8.4 6.2 %collective-permute-start.3 = (f32[2,16,128]{2,1,0:T(8,128)S(1)}, f32[2,16,128]{2,1,0:T(8,128)S(1)}, u32[]{:S(2)}, u32[]{:S(2)}) collective-permute-start(f32[2,16,128]{2,1,0:T(8,128)S(1)} %pad_maximum_fusion.1), channel_id=1, source_target_pairs={{0,48},{8,56},{16,32},{24,40},{32,16},{40,24},{48,0},{56,8},{64,11... | collective-permute-start | bytes 49160 | tf_op jit(solution)/shard_map/ppermute | solution.py:400
  11.1 3.6 %collective-permute-start.2 = (f32[2,16,128]{2,1,0:T(8,128)S(1)}, f32[2,16,128]{2,1,0:T(8,128)S(1)}, u32[]{:S(2)}, u32[]{:S(2)}) collective-permute-start(f32[2,16,128]{2,1,0:T(8,128)S(1)} %pad_maximum_fusion.1), channel_id=1, source_target_pairs={{0,32},{8,40},{16,48},{24,56},{32,0},{40,8},{48,16},{56,24},{64,96... | collective-permute-start | bytes 49160 | tf_op jit(solution)/shard_map/ppermute | solution.py:400
  11.1 3.6 %collective-permute-start.1 = (f32[2,16,128]{2,1,0:T(8,128)S(1)}, f32[2,16,128]{2,1,0:T(8,128)S(1)}, u32[]{:S(2)}, u32[]{:S(2)}) collective-permute-start(f32[2,16,128]{2,1,0:T(8,128)S(1)} %pad_maximum_fusion.1), channel_id=1, source_target_pairs={{0,16},{8,24},{16,0},{24,8},{32,48},{40,56},{48,32},{56,40},{64,80... | collective-permute-start | bytes 49160 | tf_op jit(solution)/shard_map/ppermute | solution.py:400
  14.6 5.4 %collective-permute-start.6 = (f32[8,16,128]{2,1,0:T(8,128)S(1)}, f32[8,16,128]{2,1,0:T(8,128)S(1)}, u32[]{:S(2)}, u32[]{:S(2)}) collective-permute-start(f32[8,16,128]{2,1,0:T(8,128)S(1)} %pad_maximum_fusion.refs_0_), channel_id=1, source_target_pairs={{0,64},{8,72},{16,80},{24,88},{32,96},{40,104},{48,112},{56,120},{... | collective-permute-start | bytes 196616 | tf_op jit(solution)/shard_map/ppermute | solution.py:400
  16.0 5.4 %collective-permute-start.5 = (f32[8,16,128]{2,1,0:T(8,128)S(1)}, f32[8,16,128]{2,1,0:T(8,128)S(1)}, u32[]{:S(2)}, u32[]{:S(2)}) collective-permute-start(f32[8,16,128]{2,1,0:T(8,128)S(1)} %pad_maximum_fusion.refs_0_), channel_id=1, source_target_pairs={{0,192},{8,200},{16,208},{24,216},{32,224},{40,232},{48,240},{56,2... | collective-permute-start | bytes 196616 | tf_op jit(solution)/shard_map/ppermute | solution.py:400
  17.9 5.0 %collective-permute-start.4 = (f32[8,16,128]{2,1,0:T(8,128)S(1)}, f32[8,16,128]{2,1,0:T(8,128)S(1)}, u32[]{:S(2)}, u32[]{:S(2)}) collective-permute-start(f32[8,16,128]{2,1,0:T(8,128)S(1)} %pad_maximum_fusion.refs_0_), channel_id=1, source_target_pairs={{0,128},{8,136},{16,144},{24,152},{32,160},{40,168},{48,176},{56,1... | collective-permute-start | bytes 196616 | tf_op jit(solution)/shard_map/ppermute | solution.py:400
  24.3 14.8 %collective-permute-start.7 = (f32[2,4,128,256]{3,2,1,0:T(8,128)S(1)}, f32[2,4,128,256]{3,2,1,0:T(8,128)S(1)}, u32[]{:S(2)}, u32[]{:S(2)}) collective-permute-start(f32[2,4,128,256]{3,2,1,0:T(8,128)S(1)} %get-tuple-element.28.grid_ref), channel_id=1, source_target_pairs={{0,8},{8,0},{16,24},{24,16},{32,40},{40,32},{48,56},{56,48},{64,72... | collective-permute-start | bytes 3145736 | tf_op jit(solution)/shard_map/ppermute | solution.py:400
  27.1 4.4 %collective-permute-start.10 = (f32[8,128]{1,0:T(8,128)S(1)}, f32[8,128]{1,0:T(8,128)S(1)}, u32[]{:S(2)}, u32[]{:S(2)}) collective-permute-start(f32[8,128]{1,0:T(8,128)S(1)} %get-tuple-element.29), channel_id=1, source_target_pairs={{0,9},{1,8},{2,11},{3,10},{4,13},{5,12},{6,15},{7,14},{8,1},{9,0},... | collective-permute-start | bytes 12296 | tf_op jit(solution)/shard_map/ppermute | solution.py:405
  28.3 3.2 %collective-permute-start.9 = (f32[8,128]{1,0:T(8,128)S(1)}, f32[8,128]{1,0:T(8,128)S(1)}, u32[]{:S(2)}, u32[]{:S(2)}) collective-permute-start(f32[8,128]{1,0:T(8,128)S(1)} %get-tuple-element.29), channel_id=1, source_target_pairs={{0,1},{1,0},{2,3},{3,2},{4,5},{5,4},{6,7},{7,6},{8,9},{9,8},{10,11... | collective-permute-start | bytes 12296 | tf_op jit(solution)/shard_map/ppermute | solution.py:400
  28.6 3.0 %collective-permute-start.8 = (f32[8,128]{1,0:T(8,128)S(1)}, f32[8,128]{1,0:T(8,128)S(1)}, u32[]{:S(2)}, u32[]{:S(2)}) collective-permute-start(f32[8,128]{1,0:T(8,128)S(1)} %get-tuple-element.29), channel_id=1, source_target_pairs={{0,8},{8,0},{16,24},{24,16},{32,40},{40,32},{48,56},{56,48},{64,72... | collective-permute-start | bytes 12296 | tf_op jit(solution)/shard_map/ppermute | solution.py:400
  31.6 3.8 %collective-permute-start.11 = (f32[8,128]{1,0:T(8,128)S(1)}, f32[8,128]{1,0:T(8,128)S(1)}, u32[]{:S(2)}, u32[]{:S(2)}) collective-permute-start(f32[8,128]{1,0:T(8,128)S(1)} %add_add_fusion), channel_id=1, source_target_pairs={{0,3},{1,2},{2,1},{3,0},{4,7},{5,6},{6,5},{7,4},{8,11},{9,10},{10,... | collective-permute-start | bytes 12296 | tf_op jit(solution)/shard_map/ppermute | solution.py:400
  35.3 4.8 %collective-permute-start.12 = (f32[8,128]{1,0:T(8,128)S(1)}, f32[8,128]{1,0:T(8,128)S(1)}, u32[]{:S(2)}, u32[]{:S(2)}) collective-permute-start(f32[8,128]{1,0:T(8,128)S(1)} %add.15.a_ref), channel_id=1, source_target_pairs={{0,36},{1,37},{2,38},{3,39},{8,44},{9,45},{10,46},{11,47},{16,52},... | collective-permute-start | bytes 12296 | tf_op jit(solution)/shard_map/ppermute | solution.py:417

commit v6 on v5

--- a/solution.py
+++ b/solution.py
@@ -271,22 +271,30 @@
         body(l, 0)
 
 
-def scale_kernel(mine_ref, theirs_ref, a_ref, b_ref, out_hbm, out_buf, factor_ref, sems):
+def scale_kernel(again, mine_ref, theirs_ref, total_ref, *rest):
+    out_hbm, out_buf, factor_ref, sems = rest[-4:]
     core = lax.axis_index("dp") & 1
-    total = jnp.sum(a_ref[...] + b_ref[...], axis=1, keepdims=True)
-    factor_ref[...] = lax.rsqrt(jnp.broadcast_to(total, (8, 128)) / ENTRIES + epsilon)
-    copies = []
-    for ref, start in ((mine_ref, core * HALF), (theirs_ref, HALF - core * HALF)):
-        for i in range(HALF):
-            l = start + i
-            row = factor_ref[pl.ds(l, 1), :]
-            for t in range(COLS // 128):
-                s = slice(t * 128, t * 128 + 128)
-                out_buf[l, :, s] = ref[i, :, s] * row
-            copies.append(pltpu.make_async_copy(out_buf.at[l], out_hbm.at[l], sems.at[len(copies)]))
-            copies[-1].start()
-    for copy in copies:
-        copy.wait()
+
+    def scale():
+        total = jnp.sum(total_ref[...], axis=1, keepdims=True)
+        factor_ref[...] = lax.rsqrt(jnp.broadcast_to(total, (8, 128)) / ENTRIES + epsilon)
+        copies = []
+        for ref, start in ((mine_ref, core * HALF), (theirs_ref, HALF - core * HALF)):
+            for i in range(HALF):
+                l = start + i
+                row = factor_ref[pl.ds(l, 1), :]
+                for t in range(COLS // 128):
+                    s = slice(t * 128, t * 128 + 128)
+                    out_buf[l, :, s] = ref[i, :, s] * row
+                copies.append(pltpu.make_async_copy(out_buf.at[l], out_hbm.at[l], sems.at[len(copies)]))
+                copies[-1].start()
+        for copy in copies:
+            copy.wait()
+
+    if again:
+        pl.when(core == 0)(scale)
+    else:
+        scale()
 
 
 VM = pl.BlockSpec(memory_space=pltpu.VMEM)
@@ -384,24 +392,29 @@
     return call(decode_kernel, "decode", [VM] * 3, VM, HALVED, (), 1.6)(grid, cols, rows)
 
 
-def rescale(mine, theirs, a, b):
+def rescale(mine, theirs, total, out=None):
+    ins, more = [mine, theirs, total], {}
+    if out is not None:
+        ins.append(out)
+        more = dict(input_output_aliases={3: 0})
     return call(
-        scale_kernel,
-        "rescale",
-        [VM] * 4,
+        lambda *refs: scale_kernel(out is not None, *refs),
+        "rescale" if out is None else "rescale_core0",
+        [VM] * 3 + [HB] * (len(ins) - 3),
         HB,
         DECODED,
         [pltpu.VMEM((LAYERS, ROWS, COLS), F32), pltpu.VMEM((8, 128), F32), pltpu.SemaphoreType.DMA((LAYERS,))],
-        1.0,
-    )(mine, theirs, a, b)
+        1.4,
+        **more,
+    )(*ins)
 
 
 def turn(x, axis, size, bit):
     return lax.ppermute(x, axis, [(i, i ^ bit) for i in range(size)])
 
 
-def near_other_core(x):
-    pairs = [(p * 8 + t, (p ^ 1) * 8 + (t ^ 1)) for p in range(REPLICAS) for t in range(8)]
+def along_x(x, bit):
+    pairs = [(p * 8 + t, p * 8 + (t ^ (bit if p & 1 else 1))) for p in range(REPLICAS) for t in range(8)]
     return lax.ppermute(x, ("dp", "tensor"), pairs)
 
 
@@ -409,11 +422,11 @@
     pairs = []
     for y in range(4):
         for z in range(8):
-            for core in range(2):
-                for tx in range(4):
-                    to = (z + 6) % 8 if z in (0, 1, 4, 5) else (z + 2) % 8
-                    place = [((y * 4 + k % 4) * 2 + core) * 8 + (k // 4) * 4 + tx for k in (z, to)]
-                    pairs.append(tuple(place))
+            for tx in range(4):
+                to = (z + 6) % 8 if z in (0, 1, 4, 5) else (z + 2) % 8
+                place = [((y * 4 + k % 4) * 2 + 1) * 8 + (k // 4) * 4 + tx for k in (z, to)]
+                pairs.append(tuple(place))
+                pairs.append((place[0] - 8, (place[0] - 8) ^ 1))
     return lax.ppermute(x, ("dp", "tensor"), pairs)
 
 
@@ -438,17 +451,20 @@
         (grid,) = add_sets(places, False, sets, fr, fc, grid)
     grid, squares = add_sets(calls[-1], True, sets, fr, fc, grid)
 
+    total = squares + turn(squares, "dp", REPLICAS, 1)
+    total, grid, mine = lax.optimization_barrier((total, grid, mine))
     other_grid = turn(grid, "dp", REPLICAS, 1)
-    beside = turn(squares, "dp", REPLICAS, 1)
-    near = turn(squares, "tensor", 8, 1)
-    across_near = near_other_core(squares)
-    squares, mine = lax.optimization_barrier((squares, mine))
     momentum_out = own_update(1, acc, pos, mine, back_cols, back_rows, momentum_out)
     decoded = decode(grid, back_cols, back_rows)
+    total = total + along_x(total, 1)
+    total, momentum_out, other_grid = lax.optimization_barrier((total, momentum_out, other_grid))
     other = decode(other_grid, back_cols, back_rows)
-    total = squares + beside + near + across_near
-    total = total + turn(total, "tensor", 8, 3)
-    update = rescale(decoded, other, total, across(total))
+    total = total + along_x(total, 3)
+    total, decoded, other = lax.optimization_barrier((total, decoded, other))
+    total = total + across(total)
+    given = turn(total, "dp", REPLICAS, 1)
+    update = rescale(decoded, other, total)
+    update = rescale(decoded, other, given, update)
     return (momentum_out[None], update)
 
 

time: 42.6 us -> 43 us (level); the launches traced: 41.8 us -> 43 us
  waiting for transfers between devices: 0.6 us -> 2.98 us
  starting transfers between devices: 22.3 us -> 21.1 us
    ppermute x11 -> x10, starting transfers between devices: 17.3 us -> 14.2 us  [turn(): return lax.ppermute(x, axis, [(i, i ^ bit) for i in range(size)])]
    ppermute x1 -> x2, starting transfers between devices: 1.2 us -> 3.12 us  [along_x(): return lax.ppermute(x, ('dp', 'tensor'), pairs)]
    ppermute x1 -> x2, waiting for transfers between devices: 0.01 us -> 0.95 us  [along_x(): return lax.ppermute(x, ('dp', 'tensor'), pairs)]
    ppermute x1, waiting for transfers between devices: 0.1 us -> 0.99 us  [across(): return lax.ppermute(x, ('dp', 'tensor'), pairs)]
    ppermute x11 -> x10, waiting for transfers between devices: 0.5 us -> 1.04 us  [turn(): return lax.ppermute(x, axis, [(i, i ^ bit) for i in range(size)])]
    pallas_call x1 -> x2, Pallas kernels: 1.49 us -> 1.55 us  [rescale(): call(lambda *refs: scale_kernel(out is not None, *refs), 'rescale' if out...]
  transfers between devices with their start and end apart: 13 -> 13, of which waited for: 4 -> 5; matrix products, arithmetic and copies ran while one was open for 0% -> 0% of each run, Pallas kernels for 28% -> 31%
where the time goes in v6:
time: 43 us
  starting transfers between devices  21.1 us (49%)
  Pallas kernels  17.9 us (42%)
  waiting for transfers between devices  2.98 us (7%)
  between operations  0.99 us (2%)
    ppermute x10, starting transfers between devices, turn(): return lax.ppermute(x, axis, [(i, i ^ bit) for i in range(size)])  14.2 us
    pallas_call x4, Pallas kernels, add_sets(): call(lambda *refs: set_kernel(places, first, last, *refs), 'sets' + ''.jo...  5.45 us
    pallas_call x2, Pallas kernels, own_update(): call(lambda *refs: own_kernel(which, *refs), f'own{which}', [VM] * 5 + [H...  4.45 us
    ppermute x1, starting transfers between devices, across(): return lax.ppermute(x, ('dp', 'tensor'), pairs)  3.78 us
    pallas_call x1, Pallas kernels, pick_theirs(): call(theirs_kernel, 'theirs', [HB] * 4, [VM] * 3, [jax.ShapeDtypeStruct((...  3.26 us
    ppermute x2, starting transfers between devices, along_x(): return lax.ppermute(x, ('dp', 'tensor'), pairs)  3.12 us
    pallas_call x2, Pallas kernels, decode(): call(decode_kernel, 'decode', [VM] * 3, VM, HALVED, (), 1.6)  1.78 us
    pallas_call x2, Pallas kernels, rescale(): call(lambda *refs: scale_kernel(out is not None, *refs), 'rescale' if out...  1.55 us
  transfers between devices with their start and end apart: 13, of which 5 were waited for; matrix products, arithmetic and copies ran while one was open for 0% of the time, Pallas kernels for 31%

profile of v6, /device:TPU:1, one launch (start us, length us, event | category | flops | bytes accessed | tf_op | source)
XLA Modules:
  0.0 43.0 jit_solution(13060193716480703829)
XLA Ops:
  0.6 3.3 %theirs.1 = (f32[16,128]{1,0:T(8,128)S(1)}, s32[32,128]{1,0:T(8,128)S(1)}, f32[4,128,1024]{2,1,0:T(8,128)S(1)}) custom-call(f32[4,128,1024]{2,1,0:T(8,128)} %bitcast.10, bf16[4,128,1024]{2,1,0:T(8,128)(2,1)} %bitcast.11, s32[4096,32]{1,0:T(8,128)} %bitcast.6, bf16[256,256]{1,0:T(8,128)(2,1)} %constant.6.clone.weights_hbm.weights_ref), custom_call_target="tpu_custom_call" | custom-call | flops 2500000000 | bytes 5000000 | tf_op jit(solution)/shard_map/theirs/pallas_call | solution.py:322
  3.9 3.3 %collective-permute-start = (f32[16,128]{1,0:T(8,128)S(1)}, f32[16,128]{1,0:T(8,128)S(1)}, u32[]{:S(2)}, u32[]{:S(2)}) collective-permute-start(f32[16,128]{1,0:T(8,128)S(1)} %get-tuple-element.27.refs_2_), channel_id=1, source_target_pairs={{0,8},{8,0},{16,24},{24,16},{32,40},{40,32},{48,56},{56,48},{64,72... | collective-permute-start | bytes 24584 | tf_op jit(solution)/shard_map/ppermute | solution.py:413
  7.2 1.1 %mine.1.refs_2_ = f32[16,128]{1,0:T(8,128)S(1)} custom-call(f32[4,128,1024]{2,1,0:T(8,128)S(1)} %get-tuple-element.23.acc_ref.refs_0_, s32[32,128]{1,0:T(8,128)S(1)} %get-tuple-element.24.pos_ref.refs_1_, bf16[256,256]{1,0:T(8,128)(2,1)S(1)} %copy-done.3), custom_call_target="tpu_custom_call" | custom-call | flops 1700000000 | bytes 3400000 | tf_op jit(solution)/shard_map/mine/pallas_call | solution.py:345
  8.4 2.7 %collective-permute-start.3 = (f32[2,16,128]{2,1,0:T(8,128)S(1)}, f32[2,16,128]{2,1,0:T(8,128)S(1)}, u32[]{:S(2)}, u32[]{:S(2)}) collective-permute-start(f32[2,16,128]{2,1,0:T(8,128)S(1)} %pad_maximum_fusion.1), channel_id=1, source_target_pairs={{0,48},{8,56},{16,32},{24,40},{32,16},{40,24},{48,0},{56,8},{64,11... | collective-permute-start | bytes 49160 | tf_op jit(solution)/shard_map/ppermute | solution.py:413
  11.1 0.9 %collective-permute-start.1 = (f32[2,16,128]{2,1,0:T(8,128)S(1)}, f32[2,16,128]{2,1,0:T(8,128)S(1)}, u32[]{:S(2)}, u32[]{:S(2)}) collective-permute-start(f32[2,16,128]{2,1,0:T(8,128)S(1)} %pad_maximum_fusion.1), channel_id=1, source_target_pairs={{0,16},{8,24},{16,0},{24,8},{32,48},{40,56},{48,32},{56,40},{64,80... | collective-permute-start | bytes 49160 | tf_op jit(solution)/shard_map/ppermute | solution.py:413
  12.0 2.2 %own0.1.refs_5_ = f32[4,128,1024]{2,1,0:T(8,128)} custom-call(f32[4,128,1024]{2,1,0:T(8,128)S(1)} %get-tuple-element.23.acc_ref.refs_0_, s32[32,128]{1,0:T(8,128)S(1)} %get-tuple-element.24.pos_ref.refs_1_, f32[16,128]{1,0:T(8,128)S(1)} %get-tuple-element.27.refs_2_, bf16[256,256]{1,0:T(8,128)(2,1)S(1)} %copy-done.2, bf16[256,256]{1,0:T(8,128)(2,1)S(1)} %copy-done.1), custom_call_target="tpu_custom_call" | custom-call | flops 2200000000 | bytes 4400000 | tf_op jit(solution)/shard_map/own0/pallas_call | solution.py:353
  14.6 1.4 %collective-permute-start.6 = (f32[8,16,128]{2,1,0:T(8,128)S(1)}, f32[8,16,128]{2,1,0:T(8,128)S(1)}, u32[]{:S(2)}, u32[]{:S(2)}) collective-permute-start(f32[8,16,128]{2,1,0:T(8,128)S(1)} %pad_maximum_fusion.refs_0_), channel_id=1, source_target_pairs={{0,64},{8,72},{16,80},{24,88},{32,96},{40,104},{48,112},{56,120},{... | collective-permute-start | bytes 196616 | tf_op jit(solution)/shard_map/ppermute | solution.py:413
  16.0 1.9 %collective-permute-start.5 = (f32[8,16,128]{2,1,0:T(8,128)S(1)}, f32[8,16,128]{2,1,0:T(8,128)S(1)}, u32[]{:S(2)}, u32[]{:S(2)}) collective-permute-start(f32[8,16,128]{2,1,0:T(8,128)S(1)} %pad_maximum_fusion.refs_0_), channel_id=1, source_target_pairs={{0,192},{8,200},{16,208},{24,216},{32,224},{40,232},{48,240},{56,2... | collective-permute-start | bytes 196616 | tf_op jit(solution)/shard_map/ppermute | solution.py:413
  17.9 0.7 %collective-permute-start.4 = (f32[8,16,128]{2,1,0:T(8,128)S(1)}, f32[8,16,128]{2,1,0:T(8,128)S(1)}, u32[]{:S(2)}, u32[]{:S(2)}) collective-permute-start(f32[8,16,128]{2,1,0:T(8,128)S(1)} %pad_maximum_fusion.refs_0_), channel_id=1, source_target_pairs={{0,128},{8,136},{16,144},{24,152},{32,160},{40,168},{48,176},{56,1... | collective-permute-start | bytes 196616 | tf_op jit(solution)/shard_map/ppermute | solution.py:413
  18.6 1.4 %sets0.1.refs_3_ = f32[2,4,128,256]{3,2,1,0:T(8,128)S(1)} custom-call(f32[8,16,128]{2,1,0:T(8,128)S(1)} %pad_maximum_fusion.refs_0_, f32[64,1024]{1,0:T(8,128)S(1)} %get-tuple-element.30.refs_1_, f32[64,1024]{1,0:T(8,128)S(1)} %get-tuple-element.31.refs_2_), custom_call_target="tpu_custom_call" | custom-call | flops 1400000000 | bytes 2800000 | tf_op jit(solution)/shard_map/sets0/pallas_call | solution.py:379
  20.0 1.4 %sets1.1.refs_3_ = f32[2,4,128,256]{3,2,1,0:T(8,128)S(1)} custom-call(f32[8,16,128]{2,1,0:T(8,128)S(1)} %collective-permute-done.6.refs_0_, f32[64,1024]{1,0:T(8,128)S(1)} %get-tuple-element.30.refs_1_, f32[64,1024]{1,0:T(8,128)S(1)} %get-tuple-element.31.refs_2_, f32[2,4,128,256]{3,2,1,0:T(8,128)S(1)} %sets0.1.refs_3_), custom_call_target="tpu_custom_call", output_to_operand_aliasing={{}: (3, {})} | custom-call | flops 1400000000 | bytes 2800000 | tf_op jit(solution)/shard_map/sets1/pallas_call | solution.py:379
  21.4 1.4 %sets3.1.refs_3_ = f32[2,4,128,256]{3,2,1,0:T(8,128)S(1)} custom-call(f32[8,16,128]{2,1,0:T(8,128)S(1)} %collective-permute-done.5.refs_0_, f32[64,1024]{1,0:T(8,128)S(1)} %get-tuple-element.30.refs_1_, f32[64,1024]{1,0:T(8,128)S(1)} %get-tuple-element.31.refs_2_, f32[2,4,128,256]{3,2,1,0:T(8,128)S(1)} %sets1.1.refs_3_), custom_call_target="tpu_custom_call", output_to_operand_aliasing={{}: (3, {})} | custom-call | flops 1400000000 | bytes 2800000 | tf_op jit(solution)/shard_map/sets3/pallas_call | solution.py:379
  22.9 1.4 %sets2.1 = (f32[2,4,128,256]{3,2,1,0:T(8,128)S(1)}, f32[8,128]{1,0:T(8,128)S(1)}) custom-call(f32[8,16,128]{2,1,0:T(8,128)S(1)} %collective-permute-done.4.refs_0_, f32[64,1024]{1,0:T(8,128)S(1)} %get-tuple-element.30.refs_1_, f32[64,1024]{1,0:T(8,128)S(1)} %get-tuple-element.31.refs_2_, ...), custom_call_target="tpu_custom_call", output_to_operand_aliasing={{0}: (3, {})} | custom-call | flops 1400000000 | bytes 2800000 | tf_op jit(solution)/shard_map/sets2/pallas_call | solution.py:379
  24.3 2.9 %collective-permute-start.7 = (f32[8,128]{1,0:T(8,128)S(1)}, f32[8,128]{1,0:T(8,128)S(1)}, u32[]{:S(2)}, u32[]{:S(2)}) collective-permute-start(f32[8,128]{1,0:T(8,128)S(1)} %get-tuple-element.32), channel_id=1, source_target_pairs={{0,8},{8,0},{16,24},{24,16},{32,40},{40,32},{48,56},{56,48},{64,72... | collective-permute-start | bytes 12296 | tf_op jit(solution)/shard_map/ppermute | solution.py:413
  27.1 0.8 %collective-permute-done.7 = f32[8,128]{1,0:T(8,128)S(1)} collective-permute-done((f32[8,128]{1,0:T(8,128)S(1)}, f32[8,128]{1,0:T(8,128)S(1)}, u32[]{:S(2)}, u32[]{:S(2)}) %collective-permute-start.7) | collective-permute-done | bytes 4128 | tf_op jit(solution)/shard_map/ppermute | solution.py:413
  28.3 1.2 %collective-permute-start.8 = (f32[8,128]{1,0:T(8,128)S(1)}, f32[8,128]{1,0:T(8,128)S(1)}, u32[]{:S(2)}, u32[]{:S(2)}) collective-permute-start(f32[8,128]{1,0:T(8,128)S(1)} %add.12), channel_id=1, source_target_pairs={{0,1},{1,0},{2,3},{3,2},{4,5},{5,4},{6,7},{7,6},{8,9},{9,8},{10,11... | collective-permute-start | bytes 12296 | tf_op jit(solution)/shard_map/ppermute | solution.py:418
  29.5 2.2 %own1.1 = f32[4,128,1024]{2,1,0:T(8,128)} custom-call(f32[4,128,1024]{2,1,0:T(8,128)S(1)} %get-tuple-element.23.acc_ref.refs_0_, s32[32,128]{1,0:T(8,128)S(1)} %get-tuple-element.24.pos_ref.refs_1_, f32[16,128]{1,0:T(8,128)S(1)} %mine.1.refs_2_, bf16[256,256]{1,0:T(8,128)(2,1)S(1)} %copy-done.2, ...), custom_call_target="tpu_custom_call", output_to_operand_aliasing={{}: (5, {})} | custom-call | flops 2200000000 | bytes 4400000 | tf_op jit(solution)/shard_map/own1/pallas_call | solution.py:353
  31.8 0.9 %decode.2.refs_0_ = f32[2,128,1024]{2,1,0:T(8,128)S(1)} custom-call(f32[2,4,128,256]{3,2,1,0:T(8,128)S(1)} %get-tuple-element.37.grid_ref, bf16[256,256]{1,0:T(8,128)(2,1)S(1)} %copy-done.2, bf16[256,256]{1,0:T(8,128)(2,1)S(1)} %copy-done.1), custom_call_target="tpu_custom_call" | custom-call | flops 1600000000 | bytes 3200000 | tf_op jit(solution)/shard_map/decode/pallas_call | solution.py:392
  32.7 1.9 %collective-permute-start.10 = (f32[8,128]{1,0:T(8,128)S(1)}, f32[8,128]{1,0:T(8,128)S(1)}, u32[]{:S(2)}, u32[]{:S(2)}) collective-permute-start(f32[8,128]{1,0:T(8,128)S(1)} %add.13), channel_id=1, source_target_pairs={{0,1},{1,0},{2,3},{3,2},{4,5},{5,4},{6,7},{7,6},{8,11},{9,10},{10,... | collective-permute-start | bytes 12296 | tf_op jit(solution)/shard_map/ppermute | solution.py:418
  34.6 0.9 %decode.3.refs_1_ = f32[2,128,1024]{2,1,0:T(8,128)S(1)} custom-call(f32[2,4,128,256]{3,2,1,0:T(8,128)S(1)} %collective-permute-done.9.grid_ref, bf16[256,256]{1,0:T(8,128)(2,1)S(1)} %copy-done.2, bf16[256,256]{1,0:T(8,128)(2,1)S(1)} %copy-done.1), custom_call_target="tpu_custom_call" | custom-call | flops 1600000000 | bytes 3200000 | tf_op jit(solution)/shard_map/decode/pallas_call | solution.py:392
  35.5 1.0 %collective-permute-done.10 = f32[8,128]{1,0:T(8,128)S(1)} collective-permute-done((f32[8,128]{1,0:T(8,128)S(1)}, f32[8,128]{1,0:T(8,128)S(1)}, u32[]{:S(2)}, u32[]{:S(2)}) %collective-permute-start.10) | collective-permute-done | bytes 4128 | tf_op jit(solution)/shard_map/ppermute | solution.py:418
  36.4 3.8 %collective-permute-start.11 = (f32[8,128]{1,0:T(8,128)S(1)}, f32[8,128]{1,0:T(8,128)S(1)}, u32[]{:S(2)}, u32[]{:S(2)}) collective-permute-start(f32[8,128]{1,0:T(8,128)S(1)} %add.14), channel_id=1, source_target_pairs={{8,44},{0,1},{9,45},{1,0},{10,46},{2,3},{11,47},{3,2},{24,60},{16,... | collective-permute-start | bytes 12296 | tf_op jit(solution)/shard_map/ppermute | solution.py:430
  40.2 1.0 %collective-permute-done.11 = f32[8,128]{1,0:T(8,128)S(1)} collective-permute-done((f32[8,128]{1,0:T(8,128)S(1)}, f32[8,128]{1,0:T(8,128)S(1)}, u32[]{:S(2)}, u32[]{:S(2)}) %collective-permute-start.11) | collective-permute-done | bytes 4128 | tf_op jit(solution)/shard_map/ppermute | solution.py:430
  41.2 1.5 %rescale.1.refs_3_ = f32[4,128,1024]{2,1,0:T(8,128)} custom-call(f32[2,128,1024]{2,1,0:T(8,128)S(1)} %decode.2.refs_0_, f32[2,128,1024]{2,1,0:T(8,128)S(1)} %decode.3.refs_1_, f32[8,128]{1,0:T(8,128)S(1)} %add.15.refs_2_), custom_call_target="tpu_custom_call" | custom-call | flops 1400000000 | bytes 2800000 | tf_op jit(solution)/shard_map/rescale/pallas_call | solution.py:400
  (29 shorter events, 0.9 us)
Async XLA Ops:
  0.6 6.6 %copy-start.3 = (bf16[256,256]{1,0:T(8,128)(2,1)S(1)}, bf16[256,256]{1,0:T(8,128)(2,1)}, u32[]{:S(2)}) copy-start(bf16[256,256]{1,0:T(8,128)(2,1)} %constant.6.clone.weights_hbm.weights_ref) | copy-start | bytes 393220
  3.9 4.4 %collective-permute-start = (f32[16,128]{1,0:T(8,128)S(1)}, f32[16,128]{1,0:T(8,128)S(1)}, u32[]{:S(2)}, u32[]{:S(2)}) collective-permute-start(f32[16,128]{1,0:T(8,128)S(1)} %get-tuple-element.27.refs_2_), channel_id=1, source_target_pairs={{0,8},{8,0},{16,24},{24,16},{32,40},{40,32},{48,56},{56,48},{64,72... | collective-permute-start | bytes 24584 | tf_op jit(solution)/shard_map/ppermute | solution.py:413
  7.2 4.8 %copy-start.1 = (bf16[256,256]{1,0:T(8,128)(2,1)S(1)}, bf16[256,256]{1,0:T(8,128)(2,1)}, u32[]{:S(2)}) copy-start(bf16[256,256]{1,0:T(8,128)(2,1)} %constant.8.clone.refs_4_.rows_ref) | copy-start | bytes 393220
  7.2 4.8 %copy-start.2 = (bf16[256,256]{1,0:T(8,128)(2,1)S(1)}, bf16[256,256]{1,0:T(8,128)(2,1)}, u32[]{:S(2)}) copy-start(bf16[256,256]{1,0:T(8,128)(2,1)} %constant.7.clone.refs_3_.cols_ref) | copy-start | bytes 393220
  8.4 5.9 %copy-start = (s32[32,4,2,16,32]{4,3,2,1,0:T(8,128)S(1)}, s32[32,4,2,16,32]{4,3,2,1,0:T(8,128)}, u32[]{:S(2)}) copy-start(s32[32,4,2,16,32]{4,3,2,1,0:T(8,128)} %param.8) | copy-start | bytes 1572868
  8.4 6.2 %collective-permute-start.3 = (f32[2,16,128]{2,1,0:T(8,128)S(1)}, f32[2,16,128]{2,1,0:T(8,128)S(1)}, u32[]{:S(2)}, u32[]{:S(2)}) collective-permute-start(f32[2,16,128]{2,1,0:T(8,128)S(1)} %pad_maximum_fusion.1), channel_id=1, source_target_pairs={{0,48},{8,56},{16,32},{24,40},{32,16},{40,24},{48,0},{56,8},{64,11... | collective-permute-start | bytes 49160 | tf_op jit(solution)/shard_map/ppermute | solution.py:413
  11.1 3.6 %collective-permute-start.2 = (f32[2,16,128]{2,1,0:T(8,128)S(1)}, f32[2,16,128]{2,1,0:T(8,128)S(1)}, u32[]{:S(2)}, u32[]{:S(2)}) collective-permute-start(f32[2,16,128]{2,1,0:T(8,128)S(1)} %pad_maximum_fusion.1), channel_id=1, source_target_pairs={{0,32},{8,40},{16,48},{24,56},{32,0},{40,8},{48,16},{56,24},{64,96... | collective-permute-start | bytes 49160 | tf_op jit(solution)/shard_map/ppermute | solution.py:413
  11.1 3.6 %collective-permute-start.1 = (f32[2,16,128]{2,1,0:T(8,128)S(1)}, f32[2,16,128]{2,1,0:T(8,128)S(1)}, u32[]{:S(2)}, u32[]{:S(2)}) collective-permute-start(f32[2,16,128]{2,1,0:T(8,128)S(1)} %pad_maximum_fusion.1), channel_id=1, source_target_pairs={{0,16},{8,24},{16,0},{24,8},{32,48},{40,56},{48,32},{56,40},{64,80... | collective-permute-start | bytes 49160 | tf_op jit(solution)/shard_map/ppermute | solution.py:413
  14.6 5.4 %collective-permute-start.6 = (f32[8,16,128]{2,1,0:T(8,128)S(1)}, f32[8,16,128]{2,1,0:T(8,128)S(1)}, u32[]{:S(2)}, u32[]{:S(2)}) collective-permute-start(f32[8,16,128]{2,1,0:T(8,128)S(1)} %pad_maximum_fusion.refs_0_), channel_id=1, source_target_pairs={{0,64},{8,72},{16,80},{24,88},{32,96},{40,104},{48,112},{56,120},{... | collective-permute-start | bytes 196616 | tf_op jit(solution)/shard_map/ppermute | solution.py:413
  16.0 5.4 %collective-permute-start.5 = (f32[8,16,128]{2,1,0:T(8,128)S(1)}, f32[8,16,128]{2,1,0:T(8,128)S(1)}, u32[]{:S(2)}, u32[]{:S(2)}) collective-permute-start(f32[8,16,128]{2,1,0:T(8,128)S(1)} %pad_maximum_fusion.refs_0_), channel_id=1, source_target_pairs={{0,192},{8,200},{16,208},{24,216},{32,224},{40,232},{48,240},{56,2... | collective-permute-start | bytes 196616 | tf_op jit(solution)/shard_map/ppermute | solution.py:413
  17.9 5.0 %collective-permute-start.4 = (f32[8,16,128]{2,1,0:T(8,128)S(1)}, f32[8,16,128]{2,1,0:T(8,128)S(1)}, u32[]{:S(2)}, u32[]{:S(2)}) collective-permute-start(f32[8,16,128]{2,1,0:T(8,128)S(1)} %pad_maximum_fusion.refs_0_), channel_id=1, source_target_pairs={{0,128},{8,136},{16,144},{24,152},{32,160},{40,168},{48,176},{56,1... | collective-permute-start | bytes 196616 | tf_op jit(solution)/shard_map/ppermute | solution.py:413
  24.3 3.7 %collective-permute-start.7 = (f32[8,128]{1,0:T(8,128)S(1)}, f32[8,128]{1,0:T(8,128)S(1)}, u32[]{:S(2)}, u32[]{:S(2)}) collective-permute-start(f32[8,128]{1,0:T(8,128)S(1)} %get-tuple-element.32), channel_id=1, source_target_pairs={{0,8},{8,0},{16,24},{24,16},{32,40},{40,32},{48,56},{56,48},{64,72... | collective-permute-start | bytes 12296 | tf_op jit(solution)/shard_map/ppermute | solution.py:413
  28.0 4.7 %collective-permute-start.9 = (f32[2,4,128,256]{3,2,1,0:T(8,128)S(1)}, f32[2,4,128,256]{3,2,1,0:T(8,128)S(1)}, u32[]{:S(2)}, u32[]{:S(2)}) collective-permute-start(f32[2,4,128,256]{3,2,1,0:T(8,128)S(1)} %get-tuple-element.37.grid_ref), channel_id=1, source_target_pairs={{0,8},{8,0},{16,24},{24,16},{32,40},{40,32},{48,56},{56,48},{64,72... | collective-permute-start | bytes 3145736 | tf_op jit(solution)/shard_map/ppermute | solution.py:413
  28.3 4.3 %collective-permute-start.8 = (f32[8,128]{1,0:T(8,128)S(1)}, f32[8,128]{1,0:T(8,128)S(1)}, u32[]{:S(2)}, u32[]{:S(2)}) collective-permute-start(f32[8,128]{1,0:T(8,128)S(1)} %add.12), channel_id=1, source_target_pairs={{0,1},{1,0},{2,3},{3,2},{4,5},{5,4},{6,7},{7,6},{8,9},{9,8},{10,11... | collective-permute-start | bytes 12296 | tf_op jit(solution)/shard_map/ppermute | solution.py:418
  32.7 3.8 %collective-permute-start.10 = (f32[8,128]{1,0:T(8,128)S(1)}, f32[8,128]{1,0:T(8,128)S(1)}, u32[]{:S(2)}, u32[]{:S(2)}) collective-permute-start(f32[8,128]{1,0:T(8,128)S(1)} %add.13), channel_id=1, source_target_pairs={{0,1},{1,0},{2,3},{3,2},{4,5},{5,4},{6,7},{7,6},{8,11},{9,10},{10,... | collective-permute-start | bytes 12296 | tf_op jit(solution)/shard_map/ppermute | solution.py:418
  36.4 4.8 %collective-permute-start.11 = (f32[8,128]{1,0:T(8,128)S(1)}, f32[8,128]{1,0:T(8,128)S(1)}, u32[]{:S(2)}, u32[]{:S(2)}) collective-permute-start(f32[8,128]{1,0:T(8,128)S(1)} %add.14), channel_id=1, source_target_pairs={{8,44},{0,1},{9,45},{1,0},{10,46},{2,3},{11,47},{3,2},{24,60},{16,... | collective-permute-start | bytes 12296 | tf_op jit(solution)/shard_map/ppermute | solution.py:430
  41.2 1.5 %collective-permute-start.12 = (f32[8,128]{1,0:T(8,128)S(1)}, f32[8,128]{1,0:T(8,128)S(1)}, u32[]{:S(2)}, u32[]{:S(2)}) collective-permute-start(f32[8,128]{1,0:T(8,128)S(1)} %add.15.refs_2_), channel_id=1, source_target_pairs={{0,8},{8,0},{16,24},{24,16},{32,40},{40,32},{48,56},{56,48},{64,72... | collective-permute-start | bytes 12296 | tf_op jit(solution)/shard_map/ppermute | solution.py:413

commit v7 on v6

--- a/solution.py
+++ b/solution.py
@@ -455,9 +455,9 @@
     total, grid, mine = lax.optimization_barrier((total, grid, mine))
     other_grid = turn(grid, "dp", REPLICAS, 1)
     momentum_out = own_update(1, acc, pos, mine, back_cols, back_rows, momentum_out)
+    total = total + along_x(total, 1)
+    total, momentum_out, grid, other_grid = lax.optimization_barrier((total, momentum_out, grid, other_grid))
     decoded = decode(grid, back_cols, back_rows)
-    total = total + along_x(total, 1)
-    total, momentum_out, other_grid = lax.optimization_barrier((total, momentum_out, other_grid))
     other = decode(other_grid, back_cols, back_rows)
     total = total + along_x(total, 3)
     total, decoded, other = lax.optimization_barrier((total, decoded, other))

time: 43 us -> 42.2 us (0.981)
  waiting for transfers between devices: 2.98 us -> 2.08 us
    ppermute x2, waiting for transfers between devices: 0.95 us -> 0.05 us  [along_x(): return lax.ppermute(x, ('dp', 'tensor'), pairs)]
  transfers between devices with their start and end apart: 13 -> 13, of which waited for: 5 -> 4; matrix products, arithmetic and copies ran while one was open for 0% -> 0% of each run, Pallas kernels for 31% -> 31%
where the time goes in v7:
time: 42.2 us; the launch traced here: 42.1 us
  starting transfers between devices  21.1 us (50%)
  Pallas kernels  17.9 us (42%)
  waiting for transfers between devices  2.08 us (5%)
  between operations  0.99 us (2%)
    ppermute x10, starting transfers between devices, turn(): return lax.ppermute(x, axis, [(i, i ^ bit) for i in range(size)])  14.2 us
    pallas_call x4, Pallas kernels, add_sets(): call(lambda *refs: set_kernel(places, first, last, *refs), 'sets' + ''.jo...  5.45 us
    pallas_call x2, Pallas kernels, own_update(): call(lambda *refs: own_kernel(which, *refs), f'own{which}', [VM] * 5 + [H...  4.45 us
    ppermute x1, starting transfers between devices, across(): return lax.ppermute(x, ('dp', 'tensor'), pairs)  3.84 us
    pallas_call x1, Pallas kernels, pick_theirs(): call(theirs_kernel, 'theirs', [HB] * 4, [VM] * 3, [jax.ShapeDtypeStruct((...  3.26 us
    ppermute x2, starting transfers between devices, along_x(): return lax.ppermute(x, ('dp', 'tensor'), pairs)  3.12 us
    pallas_call x2, Pallas kernels, decode(): call(decode_kernel, 'decode', [VM] * 3, VM, HALVED, (), 1.6)  1.79 us
    pallas_call x2, Pallas kernels, rescale(): call(lambda *refs: scale_kernel(out is not None, *refs), 'rescale' if out...  1.55 us
  transfers between devices with their start and end apart: 13, of which 4 were waited for; matrix products, arithmetic and copies ran while one was open for 0% of the time, Pallas kernels for 31%

profile of v7, /device:TPU:1, one launch (start us, length us, event | category | flops | bytes accessed | tf_op | source)
XLA Modules:
  0.0 42.1 jit_solution(18411897083885241016)
XLA Ops:
  0.6 3.3 %theirs.1 = (f32[16,128]{1,0:T(8,128)S(1)}, s32[32,128]{1,0:T(8,128)S(1)}, f32[4,128,1024]{2,1,0:T(8,128)S(1)}) custom-call(f32[4,128,1024]{2,1,0:T(8,128)} %bitcast.10, bf16[4,128,1024]{2,1,0:T(8,128)(2,1)} %bitcast.11, s32[4096,32]{1,0:T(8,128)} %bitcast.6, bf16[256,256]{1,0:T(8,128)(2,1)} %constant.6.clone.weights_hbm.weights_ref), custom_call_target="tpu_custom_call" | custom-call | flops 2500000000 | bytes 5000000 | tf_op jit(solution)/shard_map/theirs/pallas_call | solution.py:322
  3.9 3.3 %collective-permute-start = (f32[16,128]{1,0:T(8,128)S(1)}, f32[16,128]{1,0:T(8,128)S(1)}, u32[]{:S(2)}, u32[]{:S(2)}) collective-permute-start(f32[16,128]{1,0:T(8,128)S(1)} %get-tuple-element.28.refs_2_), channel_id=1, source_target_pairs={{0,8},{8,0},{16,24},{24,16},{32,40},{40,32},{48,56},{56,48},{64,72... | collective-permute-start | bytes 24584 | tf_op jit(solution)/shard_map/ppermute | solution.py:413
  7.2 1.1 %mine.1.refs_2_ = f32[16,128]{1,0:T(8,128)S(1)} custom-call(f32[4,128,1024]{2,1,0:T(8,128)S(1)} %get-tuple-element.24.acc_ref.refs_0_, s32[32,128]{1,0:T(8,128)S(1)} %get-tuple-element.25.pos_ref.refs_1_, bf16[256,256]{1,0:T(8,128)(2,1)S(1)} %copy-done.3), custom_call_target="tpu_custom_call" | custom-call | flops 1700000000 | bytes 3400000 | tf_op jit(solution)/shard_map/mine/pallas_call | solution.py:345
  8.4 2.7 %collective-permute-start.3 = (f32[2,16,128]{2,1,0:T(8,128)S(1)}, f32[2,16,128]{2,1,0:T(8,128)S(1)}, u32[]{:S(2)}, u32[]{:S(2)}) collective-permute-start(f32[2,16,128]{2,1,0:T(8,128)S(1)} %pad_maximum_fusion.1), channel_id=1, source_target_pairs={{0,48},{8,56},{16,32},{24,40},{32,16},{40,24},{48,0},{56,8},{64,11... | collective-permute-start | bytes 49160 | tf_op jit(solution)/shard_map/ppermute | solution.py:413
  11.1 0.9 %collective-permute-start.1 = (f32[2,16,128]{2,1,0:T(8,128)S(1)}, f32[2,16,128]{2,1,0:T(8,128)S(1)}, u32[]{:S(2)}, u32[]{:S(2)}) collective-permute-start(f32[2,16,128]{2,1,0:T(8,128)S(1)} %pad_maximum_fusion.1), channel_id=1, source_target_pairs={{0,16},{8,24},{16,0},{24,8},{32,48},{40,56},{48,32},{56,40},{64,80... | collective-permute-start | bytes 49160 | tf_op jit(solution)/shard_map/ppermute | solution.py:413
  12.0 2.2 %own0.1.refs_5_ = f32[4,128,1024]{2,1,0:T(8,128)} custom-call(f32[4,128,1024]{2,1,0:T(8,128)S(1)} %get-tuple-element.24.acc_ref.refs_0_, s32[32,128]{1,0:T(8,128)S(1)} %get-tuple-element.25.pos_ref.refs_1_, f32[16,128]{1,0:T(8,128)S(1)} %get-tuple-element.28.refs_2_, bf16[256,256]{1,0:T(8,128)(2,1)S(1)} %copy-done.2, bf16[256,256]{1,0:T(8,128)(2,1)S(1)} %copy-done.1), custom_call_target="tpu_custom_call" | custom-call | flops 2200000000 | bytes 4400000 | tf_op jit(solution)/shard_map/own0/pallas_call | solution.py:353
  14.6 1.4 %collective-permute-start.6 = (f32[8,16,128]{2,1,0:T(8,128)S(1)}, f32[8,16,128]{2,1,0:T(8,128)S(1)}, u32[]{:S(2)}, u32[]{:S(2)}) collective-permute-start(f32[8,16,128]{2,1,0:T(8,128)S(1)} %pad_maximum_fusion.refs_0_), channel_id=1, source_target_pairs={{0,64},{8,72},{16,80},{24,88},{32,96},{40,104},{48,112},{56,120},{... | collective-permute-start | bytes 196616 | tf_op jit(solution)/shard_map/ppermute | solution.py:413
  16.0 1.9 %collective-permute-start.5 = (f32[8,16,128]{2,1,0:T(8,128)S(1)}, f32[8,16,128]{2,1,0:T(8,128)S(1)}, u32[]{:S(2)}, u32[]{:S(2)}) collective-permute-start(f32[8,16,128]{2,1,0:T(8,128)S(1)} %pad_maximum_fusion.refs_0_), channel_id=1, source_target_pairs={{0,192},{8,200},{16,208},{24,216},{32,224},{40,232},{48,240},{56,2... | collective-permute-start | bytes 196616 | tf_op jit(solution)/shard_map/ppermute | solution.py:413
  17.9 0.7 %collective-permute-start.4 = (f32[8,16,128]{2,1,0:T(8,128)S(1)}, f32[8,16,128]{2,1,0:T(8,128)S(1)}, u32[]{:S(2)}, u32[]{:S(2)}) collective-permute-start(f32[8,16,128]{2,1,0:T(8,128)S(1)} %pad_maximum_fusion.refs_0_), channel_id=1, source_target_pairs={{0,128},{8,136},{16,144},{24,152},{32,160},{40,168},{48,176},{56,1... | collective-permute-start | bytes 196616 | tf_op jit(solution)/shard_map/ppermute | solution.py:413
  18.6 1.4 %sets0.1.refs_3_ = f32[2,4,128,256]{3,2,1,0:T(8,128)S(1)} custom-call(f32[8,16,128]{2,1,0:T(8,128)S(1)} %pad_maximum_fusion.refs_0_, f32[64,1024]{1,0:T(8,128)S(1)} %get-tuple-element.31.refs_1_, f32[64,1024]{1,0:T(8,128)S(1)} %get-tuple-element.32.refs_2_), custom_call_target="tpu_custom_call" | custom-call | flops 1400000000 | bytes 2800000 | tf_op jit(solution)/shard_map/sets0/pallas_call | solution.py:379
  20.0 1.4 %sets1.1.refs_3_ = f32[2,4,128,256]{3,2,1,0:T(8,128)S(1)} custom-call(f32[8,16,128]{2,1,0:T(8,128)S(1)} %collective-permute-done.6.refs_0_, f32[64,1024]{1,0:T(8,128)S(1)} %get-tuple-element.31.refs_1_, f32[64,1024]{1,0:T(8,128)S(1)} %get-tuple-element.32.refs_2_, f32[2,4,128,256]{3,2,1,0:T(8,128)S(1)} %sets0.1.refs_3_), custom_call_target="tpu_custom_call", output_to_operand_aliasing={{}: (3, {})} | custom-call | flops 1400000000 | bytes 2800000 | tf_op jit(solution)/shard_map/sets1/pallas_call | solution.py:379
  21.4 1.4 %sets3.1.refs_3_ = f32[2,4,128,256]{3,2,1,0:T(8,128)S(1)} custom-call(f32[8,16,128]{2,1,0:T(8,128)S(1)} %collective-permute-done.5.refs_0_, f32[64,1024]{1,0:T(8,128)S(1)} %get-tuple-element.31.refs_1_, f32[64,1024]{1,0:T(8,128)S(1)} %get-tuple-element.32.refs_2_, f32[2,4,128,256]{3,2,1,0:T(8,128)S(1)} %sets1.1.refs_3_), custom_call_target="tpu_custom_call", output_to_operand_aliasing={{}: (3, {})} | custom-call | flops 1400000000 | bytes 2800000 | tf_op jit(solution)/shard_map/sets3/pallas_call | solution.py:379
  22.9 1.4 %sets2.1 = (f32[2,4,128,256]{3,2,1,0:T(8,128)S(1)}, f32[8,128]{1,0:T(8,128)S(1)}) custom-call(f32[8,16,128]{2,1,0:T(8,128)S(1)} %collective-permute-done.4.refs_0_, f32[64,1024]{1,0:T(8,128)S(1)} %get-tuple-element.31.refs_1_, f32[64,1024]{1,0:T(8,128)S(1)} %get-tuple-element.32.refs_2_, ...), custom_call_target="tpu_custom_call", output_to_operand_aliasing={{0}: (3, {})} | custom-call | flops 1400000000 | bytes 2800000 | tf_op jit(solution)/shard_map/sets2/pallas_call | solution.py:379
  24.3 2.9 %collective-permute-start.7 = (f32[8,128]{1,0:T(8,128)S(1)}, f32[8,128]{1,0:T(8,128)S(1)}, u32[]{:S(2)}, u32[]{:S(2)}) collective-permute-start(f32[8,128]{1,0:T(8,128)S(1)} %get-tuple-element.33), channel_id=1, source_target_pairs={{0,8},{8,0},{16,24},{24,16},{32,40},{40,32},{48,56},{56,48},{64,72... | collective-permute-start | bytes 12296 | tf_op jit(solution)/shard_map/ppermute | solution.py:413
  27.1 0.8 %collective-permute-done.7 = f32[8,128]{1,0:T(8,128)S(1)} collective-permute-done((f32[8,128]{1,0:T(8,128)S(1)}, f32[8,128]{1,0:T(8,128)S(1)}, u32[]{:S(2)}, u32[]{:S(2)}) %collective-permute-start.7) | collective-permute-done | bytes 4128 | tf_op jit(solution)/shard_map/ppermute | solution.py:413
  28.0 0.3 collective-permute-start.9
  28.3 1.2 %collective-permute-start.8 = (f32[8,128]{1,0:T(8,128)S(1)}, f32[8,128]{1,0:T(8,128)S(1)}, u32[]{:S(2)}, u32[]{:S(2)}) collective-permute-start(f32[8,128]{1,0:T(8,128)S(1)} %add.12), channel_id=1, source_target_pairs={{0,1},{1,0},{2,3},{3,2},{4,5},{5,4},{6,7},{7,6},{8,9},{9,8},{10,11... | collective-permute-start | bytes 12296 | tf_op jit(solution)/shard_map/ppermute | solution.py:418
  29.5 2.2 %own1.1 = f32[4,128,1024]{2,1,0:T(8,128)} custom-call(f32[4,128,1024]{2,1,0:T(8,128)S(1)} %get-tuple-element.24.acc_ref.refs_0_, s32[32,128]{1,0:T(8,128)S(1)} %get-tuple-element.25.pos_ref.refs_1_, f32[16,128]{1,0:T(8,128)S(1)} %mine.1.refs_2_, bf16[256,256]{1,0:T(8,128)(2,1)S(1)} %copy-done.2, ...), custom_call_target="tpu_custom_call", output_to_operand_aliasing={{}: (5, {})} | custom-call | flops 2200000000 | bytes 4400000 | tf_op jit(solution)/shard_map/own1/pallas_call | solution.py:353
  31.8 1.9 %collective-permute-start.10 = (f32[8,128]{1,0:T(8,128)S(1)}, f32[8,128]{1,0:T(8,128)S(1)}, u32[]{:S(2)}, u32[]{:S(2)}) collective-permute-start(f32[8,128]{1,0:T(8,128)S(1)} %add.13), channel_id=1, source_target_pairs={{0,1},{1,0},{2,3},{3,2},{4,5},{5,4},{6,7},{7,6},{8,11},{9,10},{10,... | collective-permute-start | bytes 12296 | tf_op jit(solution)/shard_map/ppermute | solution.py:418
  33.7 0.9 %decode.2.refs_0_ = f32[2,128,1024]{2,1,0:T(8,128)S(1)} custom-call(f32[2,4,128,256]{3,2,1,0:T(8,128)S(1)} %get-tuple-element.41.grid_ref, bf16[256,256]{1,0:T(8,128)(2,1)S(1)} %copy-done.2, bf16[256,256]{1,0:T(8,128)(2,1)S(1)} %copy-done.1), custom_call_target="tpu_custom_call" | custom-call | flops 1600000000 | bytes 3200000 | tf_op jit(solution)/shard_map/decode/pallas_call | solution.py:392
  34.6 0.9 %decode.3.refs_1_ = f32[2,128,1024]{2,1,0:T(8,128)S(1)} custom-call(f32[2,4,128,256]{3,2,1,0:T(8,128)S(1)} %collective-permute-done.9.grid_ref, bf16[256,256]{1,0:T(8,128)(2,1)S(1)} %copy-done.2, bf16[256,256]{1,0:T(8,128)(2,1)S(1)} %copy-done.1), custom_call_target="tpu_custom_call" | custom-call | flops 1600000000 | bytes 3200000 | tf_op jit(solution)/shard_map/decode/pallas_call | solution.py:392
  35.5 3.8 %collective-permute-start.11 = (f32[8,128]{1,0:T(8,128)S(1)}, f32[8,128]{1,0:T(8,128)S(1)}, u32[]{:S(2)}, u32[]{:S(2)}) collective-permute-start(f32[8,128]{1,0:T(8,128)S(1)} %add.14), channel_id=1, source_target_pairs={{8,44},{0,1},{9,45},{1,0},{10,46},{2,3},{11,47},{3,2},{24,60},{16,... | collective-permute-start | bytes 12296 | tf_op jit(solution)/shard_map/ppermute | solution.py:430
  39.4 1.0 %collective-permute-done.11 = f32[8,128]{1,0:T(8,128)S(1)} collective-permute-done((f32[8,128]{1,0:T(8,128)S(1)}, f32[8,128]{1,0:T(8,128)S(1)}, u32[]{:S(2)}, u32[]{:S(2)}) %collective-permute-start.11) | collective-permute-done | bytes 4128 | tf_op jit(solution)/shard_map/ppermute | solution.py:430
  40.4 1.5 %rescale.1.refs_3_ = f32[4,128,1024]{2,1,0:T(8,128)} custom-call(f32[2,128,1024]{2,1,0:T(8,128)S(1)} %decode.2.refs_0_, f32[2,128,1024]{2,1,0:T(8,128)S(1)} %decode.3.refs_1_, f32[8,128]{1,0:T(8,128)S(1)} %add.15.refs_2_), custom_call_target="tpu_custom_call" | custom-call | flops 1400000000 | bytes 2800000 | tf_op jit(solution)/shard_map/rescale/pallas_call | solution.py:400
  (29 shorter events, 0.7 us)
Async XLA Ops:
  0.6 6.6 %copy-start.3 = (bf16[256,256]{1,0:T(8,128)(2,1)S(1)}, bf16[256,256]{1,0:T(8,128)(2,1)}, u32[]{:S(2)}) copy-start(bf16[256,256]{1,0:T(8,128)(2,1)} %constant.6.clone.weights_hbm.weights_ref) | copy-start | bytes 393220
  3.9 4.4 %collective-permute-start = (f32[16,128]{1,0:T(8,128)S(1)}, f32[16,128]{1,0:T(8,128)S(1)}, u32[]{:S(2)}, u32[]{:S(2)}) collective-permute-start(f32[16,128]{1,0:T(8,128)S(1)} %get-tuple-element.28.refs_2_), channel_id=1, source_target_pairs={{0,8},{8,0},{16,24},{24,16},{32,40},{40,32},{48,56},{56,48},{64,72... | collective-permute-start | bytes 24584 | tf_op jit(solution)/shard_map/ppermute | solution.py:413
  7.2 4.8 %copy-start.1 = (bf16[256,256]{1,0:T(8,128)(2,1)S(1)}, bf16[256,256]{1,0:T(8,128)(2,1)}, u32[]{:S(2)}) copy-start(bf16[256,256]{1,0:T(8,128)(2,1)} %constant.8.clone.refs_4_.rows_ref) | copy-start | bytes 393220
  7.2 4.8 %copy-start.2 = (bf16[256,256]{1,0:T(8,128)(2,1)S(1)}, bf16[256,256]{1,0:T(8,128)(2,1)}, u32[]{:S(2)}) copy-start(bf16[256,256]{1,0:T(8,128)(2,1)} %constant.7.clone.refs_3_.cols_ref) | copy-start | bytes 393220
  8.4 5.9 %copy-start = (s32[32,4,2,16,32]{4,3,2,1,0:T(8,128)S(1)}, s32[32,4,2,16,32]{4,3,2,1,0:T(8,128)}, u32[]{:S(2)}) copy-start(s32[32,4,2,16,32]{4,3,2,1,0:T(8,128)} %param.8) | copy-start | bytes 1572868
  8.4 6.2 %collective-permute-start.3 = (f32[2,16,128]{2,1,0:T(8,128)S(1)}, f32[2,16,128]{2,1,0:T(8,128)S(1)}, u32[]{:S(2)}, u32[]{:S(2)}) collective-permute-start(f32[2,16,128]{2,1,0:T(8,128)S(1)} %pad_maximum_fusion.1), channel_id=1, source_target_pairs={{0,48},{8,56},{16,32},{24,40},{32,16},{40,24},{48,0},{56,8},{64,11... | collective-permute-start | bytes 49160 | tf_op jit(solution)/shard_map/ppermute | solution.py:413
  11.1 3.6 %collective-permute-start.2 = (f32[2,16,128]{2,1,0:T(8,128)S(1)}, f32[2,16,128]{2,1,0:T(8,128)S(1)}, u32[]{:S(2)}, u32[]{:S(2)}) collective-permute-start(f32[2,16,128]{2,1,0:T(8,128)S(1)} %pad_maximum_fusion.1), channel_id=1, source_target_pairs={{0,32},{8,40},{16,48},{24,56},{32,0},{40,8},{48,16},{56,24},{64,96... | collective-permute-start | bytes 49160 | tf_op jit(solution)/shard_map/ppermute | solution.py:413
  11.1 3.6 %collective-permute-start.1 = (f32[2,16,128]{2,1,0:T(8,128)S(1)}, f32[2,16,128]{2,1,0:T(8,128)S(1)}, u32[]{:S(2)}, u32[]{:S(2)}) collective-permute-start(f32[2,16,128]{2,1,0:T(8,128)S(1)} %pad_maximum_fusion.1), channel_id=1, source_target_pairs={{0,16},{8,24},{16,0},{24,8},{32,48},{40,56},{48,32},{56,40},{64,80... | collective-permute-start | bytes 49160 | tf_op jit(solution)/shard_map/ppermute | solution.py:413
  14.6 5.4 %collective-permute-start.6 = (f32[8,16,128]{2,1,0:T(8,128)S(1)}, f32[8,16,128]{2,1,0:T(8,128)S(1)}, u32[]{:S(2)}, u32[]{:S(2)}) collective-permute-start(f32[8,16,128]{2,1,0:T(8,128)S(1)} %pad_maximum_fusion.refs_0_), channel_id=1, source_target_pairs={{0,64},{8,72},{16,80},{24,88},{32,96},{40,104},{48,112},{56,120},{... | collective-permute-start | bytes 196616 | tf_op jit(solution)/shard_map/ppermute | solution.py:413
  16.0 5.4 %collective-permute-start.5 = (f32[8,16,128]{2,1,0:T(8,128)S(1)}, f32[8,16,128]{2,1,0:T(8,128)S(1)}, u32[]{:S(2)}, u32[]{:S(2)}) collective-permute-start(f32[8,16,128]{2,1,0:T(8,128)S(1)} %pad_maximum_fusion.refs_0_), channel_id=1, source_target_pairs={{0,192},{8,200},{16,208},{24,216},{32,224},{40,232},{48,240},{56,2... | collective-permute-start | bytes 196616 | tf_op jit(solution)/shard_map/ppermute | solution.py:413
  17.9 5.0 %collective-permute-start.4 = (f32[8,16,128]{2,1,0:T(8,128)S(1)}, f32[8,16,128]{2,1,0:T(8,128)S(1)}, u32[]{:S(2)}, u32[]{:S(2)}) collective-permute-start(f32[8,16,128]{2,1,0:T(8,128)S(1)} %pad_maximum_fusion.refs_0_), channel_id=1, source_target_pairs={{0,128},{8,136},{16,144},{24,152},{32,160},{40,168},{48,176},{56,1... | collective-permute-start | bytes 196616 | tf_op jit(solution)/shard_map/ppermute | solution.py:413
  24.3 3.7 %collective-permute-start.7 = (f32[8,128]{1,0:T(8,128)S(1)}, f32[8,128]{1,0:T(8,128)S(1)}, u32[]{:S(2)}, u32[]{:S(2)}) collective-permute-start(f32[8,128]{1,0:T(8,128)S(1)} %get-tuple-element.33), channel_id=1, source_target_pairs={{0,8},{8,0},{16,24},{24,16},{32,40},{40,32},{48,56},{56,48},{64,72... | collective-permute-start | bytes 12296 | tf_op jit(solution)/shard_map/ppermute | solution.py:413
  28.0 3.8 %collective-permute-start.9 = (f32[2,4,128,256]{3,2,1,0:T(8,128)S(1)}, f32[2,4,128,256]{3,2,1,0:T(8,128)S(1)}, u32[]{:S(2)}, u32[]{:S(2)}) collective-permute-start(f32[2,4,128,256]{3,2,1,0:T(8,128)S(1)} %get-tuple-element.41.grid_ref), channel_id=1, source_target_pairs={{0,8},{8,0},{16,24},{24,16},{32,40},{40,32},{48,56},{56,48},{64,72... | collective-permute-start | bytes 3145736 | tf_op jit(solution)/shard_map/ppermute | solution.py:413
  28.3 3.4 %collective-permute-start.8 = (f32[8,128]{1,0:T(8,128)S(1)}, f32[8,128]{1,0:T(8,128)S(1)}, u32[]{:S(2)}, u32[]{:S(2)}) collective-permute-start(f32[8,128]{1,0:T(8,128)S(1)} %add.12), channel_id=1, source_target_pairs={{0,1},{1,0},{2,3},{3,2},{4,5},{5,4},{6,7},{7,6},{8,9},{9,8},{10,11... | collective-permute-start | bytes 12296 | tf_op jit(solution)/shard_map/ppermute | solution.py:418
  31.8 3.8 %collective-permute-start.10 = (f32[8,128]{1,0:T(8,128)S(1)}, f32[8,128]{1,0:T(8,128)S(1)}, u32[]{:S(2)}, u32[]{:S(2)}) collective-permute-start(f32[8,128]{1,0:T(8,128)S(1)} %add.13), channel_id=1, source_target_pairs={{0,1},{1,0},{2,3},{3,2},{4,5},{5,4},{6,7},{7,6},{8,11},{9,10},{10,... | collective-permute-start | bytes 12296 | tf_op jit(solution)/shard_map/ppermute | solution.py:418
  35.5 4.8 %collective-permute-start.11 = (f32[8,128]{1,0:T(8,128)S(1)}, f32[8,128]{1,0:T(8,128)S(1)}, u32[]{:S(2)}, u32[]{:S(2)}) collective-permute-start(f32[8,128]{1,0:T(8,128)S(1)} %add.14), channel_id=1, source_target_pairs={{8,44},{0,1},{9,45},{1,0},{10,46},{2,3},{11,47},{3,2},{24,60},{16,... | collective-permute-start | bytes 12296 | tf_op jit(solution)/shard_map/ppermute | solution.py:430
  40.4 1.5 %collective-permute-start.12 = (f32[8,128]{1,0:T(8,128)S(1)}, f32[8,128]{1,0:T(8,128)S(1)}, u32[]{:S(2)}, u32[]{:S(2)}) collective-permute-start(f32[8,128]{1,0:T(8,128)S(1)} %add.15.refs_2_), channel_id=1, source_target_pairs={{0,8},{8,0},{16,24},{24,16},{32,40},{40,32},{48,56},{56,48},{64,72... | collective-permute-start | bytes 12296 | tf_op jit(solution)/shard_map/ppermute | solution.py:413

commit v8 on v7

--- a/solution.py
+++ b/solution.py
@@ -291,10 +291,7 @@
         for copy in copies:
             copy.wait()
 
-    if again:
-        pl.when(core == 0)(scale)
-    else:
-        scale()
+    pl.when(core == (0 if again else 1))(scale)
 
 
 VM = pl.BlockSpec(memory_space=pltpu.VMEM)

time: 42.2 us -> 42.2 us (level)
  no operation moved by 1% of the time
where the time goes in v8:
time: 42.2 us; the launch traced here: 42.1 us
  starting transfers between devices  21.1 us (50%)
  Pallas kernels  17.9 us (42%)
  waiting for transfers between devices  2.08 us (5%)
  between operations  0.99 us (2%)
    ppermute x10, starting transfers between devices, turn(): return lax.ppermute(x, axis, [(i, i ^ bit) for i in range(size)])  14.2 us
    pallas_call x4, Pallas kernels, add_sets(): call(lambda *refs: set_kernel(places, first, last, *refs), 'sets' + ''.jo...  5.45 us
    pallas_call x2, Pallas kernels, own_update(): call(lambda *refs: own_kernel(which, *refs), f'own{which}', [VM] * 5 + [H...  4.45 us
    ppermute x1, starting transfers between devices, across(): return lax.ppermute(x, ('dp', 'tensor'), pairs)  3.84 us
    pallas_call x1, Pallas kernels, pick_theirs(): call(theirs_kernel, 'theirs', [HB] * 4, [VM] * 3, [jax.ShapeDtypeStruct((...  3.26 us
    ppermute x2, starting transfers between devices, along_x(): return lax.ppermute(x, ('dp', 'tensor'), pairs)  3.12 us
    pallas_call x2, Pallas kernels, decode(): call(decode_kernel, 'decode', [VM] * 3, VM, HALVED, (), 1.6)  1.79 us
    pallas_call x2, Pallas kernels, rescale(): call(lambda *refs: scale_kernel(out is not None, *refs), 'rescale' if out...  1.55 us
  transfers between devices with their start and end apart: 13, of which 4 were waited for; matrix products, arithmetic and copies ran while one was open for 0% of the time, Pallas kernels for 31%

profile of v8, /device:TPU:1, one launch (start us, length us, event | category | flops | bytes accessed | tf_op | source)
XLA Modules:
  0.0 42.1 jit_solution(8632757354210858367)
XLA Ops:
  0.6 3.3 %theirs.1 = (f32[16,128]{1,0:T(8,128)S(1)}, s32[32,128]{1,0:T(8,128)S(1)}, f32[4,128,1024]{2,1,0:T(8,128)S(1)}) custom-call(f32[4,128,1024]{2,1,0:T(8,128)} %bitcast.10, bf16[4,128,1024]{2,1,0:T(8,128)(2,1)} %bitcast.11, s32[4096,32]{1,0:T(8,128)} %bitcast.6, bf16[256,256]{1,0:T(8,128)(2,1)} %constant.6.clone.weights_hbm.weights_ref), custom_call_target="tpu_custom_call" | custom-call | flops 2500000000 | bytes 5000000 | tf_op jit(solution)/shard_map/theirs/pallas_call | solution.py:319
  3.9 3.3 %collective-permute-start = (f32[16,128]{1,0:T(8,128)S(1)}, f32[16,128]{1,0:T(8,128)S(1)}, u32[]{:S(2)}, u32[]{:S(2)}) collective-permute-start(f32[16,128]{1,0:T(8,128)S(1)} %get-tuple-element.28.refs_2_), channel_id=1, source_target_pairs={{0,8},{8,0},{16,24},{24,16},{32,40},{40,32},{48,56},{56,48},{64,72... | collective-permute-start | bytes 24584 | tf_op jit(solution)/shard_map/ppermute | solution.py:410
  7.2 1.1 %mine.1.refs_2_ = f32[16,128]{1,0:T(8,128)S(1)} custom-call(f32[4,128,1024]{2,1,0:T(8,128)S(1)} %get-tuple-element.24.acc_ref.refs_0_, s32[32,128]{1,0:T(8,128)S(1)} %get-tuple-element.25.pos_ref.refs_1_, bf16[256,256]{1,0:T(8,128)(2,1)S(1)} %copy-done.3), custom_call_target="tpu_custom_call" | custom-call | flops 1700000000 | bytes 3400000 | tf_op jit(solution)/shard_map/mine/pallas_call | solution.py:342
  8.4 2.7 %collective-permute-start.3 = (f32[2,16,128]{2,1,0:T(8,128)S(1)}, f32[2,16,128]{2,1,0:T(8,128)S(1)}, u32[]{:S(2)}, u32[]{:S(2)}) collective-permute-start(f32[2,16,128]{2,1,0:T(8,128)S(1)} %pad_maximum_fusion.1), channel_id=1, source_target_pairs={{0,48},{8,56},{16,32},{24,40},{32,16},{40,24},{48,0},{56,8},{64,11... | collective-permute-start | bytes 49160 | tf_op jit(solution)/shard_map/ppermute | solution.py:410
  11.1 0.9 %collective-permute-start.1 = (f32[2,16,128]{2,1,0:T(8,128)S(1)}, f32[2,16,128]{2,1,0:T(8,128)S(1)}, u32[]{:S(2)}, u32[]{:S(2)}) collective-permute-start(f32[2,16,128]{2,1,0:T(8,128)S(1)} %pad_maximum_fusion.1), channel_id=1, source_target_pairs={{0,16},{8,24},{16,0},{24,8},{32,48},{40,56},{48,32},{56,40},{64,80... | collective-permute-start | bytes 49160 | tf_op jit(solution)/shard_map/ppermute | solution.py:410
  12.0 2.2 %own0.1.refs_5_ = f32[4,128,1024]{2,1,0:T(8,128)} custom-call(f32[4,128,1024]{2,1,0:T(8,128)S(1)} %get-tuple-element.24.acc_ref.refs_0_, s32[32,128]{1,0:T(8,128)S(1)} %get-tuple-element.25.pos_ref.refs_1_, f32[16,128]{1,0:T(8,128)S(1)} %get-tuple-element.28.refs_2_, bf16[256,256]{1,0:T(8,128)(2,1)S(1)} %copy-done.2, bf16[256,256]{1,0:T(8,128)(2,1)S(1)} %copy-done.1), custom_call_target="tpu_custom_call" | custom-call | flops 2200000000 | bytes 4400000 | tf_op jit(solution)/shard_map/own0/pallas_call | solution.py:350
  14.6 1.4 %collective-permute-start.6 = (f32[8,16,128]{2,1,0:T(8,128)S(1)}, f32[8,16,128]{2,1,0:T(8,128)S(1)}, u32[]{:S(2)}, u32[]{:S(2)}) collective-permute-start(f32[8,16,128]{2,1,0:T(8,128)S(1)} %pad_maximum_fusion.refs_0_), channel_id=1, source_target_pairs={{0,64},{8,72},{16,80},{24,88},{32,96},{40,104},{48,112},{56,120},{... | collective-permute-start | bytes 196616 | tf_op jit(solution)/shard_map/ppermute | solution.py:410
  16.0 1.9 %collective-permute-start.5 = (f32[8,16,128]{2,1,0:T(8,128)S(1)}, f32[8,16,128]{2,1,0:T(8,128)S(1)}, u32[]{:S(2)}, u32[]{:S(2)}) collective-permute-start(f32[8,16,128]{2,1,0:T(8,128)S(1)} %pad_maximum_fusion.refs_0_), channel_id=1, source_target_pairs={{0,192},{8,200},{16,208},{24,216},{32,224},{40,232},{48,240},{56,2... | collective-permute-start | bytes 196616 | tf_op jit(solution)/shard_map/ppermute | solution.py:410
  17.9 0.7 %collective-permute-start.4 = (f32[8,16,128]{2,1,0:T(8,128)S(1)}, f32[8,16,128]{2,1,0:T(8,128)S(1)}, u32[]{:S(2)}, u32[]{:S(2)}) collective-permute-start(f32[8,16,128]{2,1,0:T(8,128)S(1)} %pad_maximum_fusion.refs_0_), channel_id=1, source_target_pairs={{0,128},{8,136},{16,144},{24,152},{32,160},{40,168},{48,176},{56,1... | collective-permute-start | bytes 196616 | tf_op jit(solution)/shard_map/ppermute | solution.py:410
  18.6 1.4 %sets0.1.refs_3_ = f32[2,4,128,256]{3,2,1,0:T(8,128)S(1)} custom-call(f32[8,16,128]{2,1,0:T(8,128)S(1)} %pad_maximum_fusion.refs_0_, f32[64,1024]{1,0:T(8,128)S(1)} %get-tuple-element.31.refs_1_, f32[64,1024]{1,0:T(8,128)S(1)} %get-tuple-element.32.refs_2_), custom_call_target="tpu_custom_call" | custom-call | flops 1400000000 | bytes 2800000 | tf_op jit(solution)/shard_map/sets0/pallas_call | solution.py:376
  20.0 1.4 %sets1.1.refs_3_ = f32[2,4,128,256]{3,2,1,0:T(8,128)S(1)} custom-call(f32[8,16,128]{2,1,0:T(8,128)S(1)} %collective-permute-done.6.refs_0_, f32[64,1024]{1,0:T(8,128)S(1)} %get-tuple-element.31.refs_1_, f32[64,1024]{1,0:T(8,128)S(1)} %get-tuple-element.32.refs_2_, f32[2,4,128,256]{3,2,1,0:T(8,128)S(1)} %sets0.1.refs_3_), custom_call_target="tpu_custom_call", output_to_operand_aliasing={{}: (3, {})} | custom-call | flops 1400000000 | bytes 2800000 | tf_op jit(solution)/shard_map/sets1/pallas_call | solution.py:376
  21.4 1.4 %sets3.1.refs_3_ = f32[2,4,128,256]{3,2,1,0:T(8,128)S(1)} custom-call(f32[8,16,128]{2,1,0:T(8,128)S(1)} %collective-permute-done.5.refs_0_, f32[64,1024]{1,0:T(8,128)S(1)} %get-tuple-element.31.refs_1_, f32[64,1024]{1,0:T(8,128)S(1)} %get-tuple-element.32.refs_2_, f32[2,4,128,256]{3,2,1,0:T(8,128)S(1)} %sets1.1.refs_3_), custom_call_target="tpu_custom_call", output_to_operand_aliasing={{}: (3, {})} | custom-call | flops 1400000000 | bytes 2800000 | tf_op jit(solution)/shard_map/sets3/pallas_call | solution.py:376
  22.9 1.4 %sets2.1 = (f32[2,4,128,256]{3,2,1,0:T(8,128)S(1)}, f32[8,128]{1,0:T(8,128)S(1)}) custom-call(f32[8,16,128]{2,1,0:T(8,128)S(1)} %collective-permute-done.4.refs_0_, f32[64,1024]{1,0:T(8,128)S(1)} %get-tuple-element.31.refs_1_, f32[64,1024]{1,0:T(8,128)S(1)} %get-tuple-element.32.refs_2_, ...), custom_call_target="tpu_custom_call", output_to_operand_aliasing={{0}: (3, {})} | custom-call | flops 1400000000 | bytes 2800000 | tf_op jit(solution)/shard_map/sets2/pallas_call | solution.py:376
  24.3 2.9 %collective-permute-start.7 = (f32[8,128]{1,0:T(8,128)S(1)}, f32[8,128]{1,0:T(8,128)S(1)}, u32[]{:S(2)}, u32[]{:S(2)}) collective-permute-start(f32[8,128]{1,0:T(8,128)S(1)} %get-tuple-element.33), channel_id=1, source_target_pairs={{0,8},{8,0},{16,24},{24,16},{32,40},{40,32},{48,56},{56,48},{64,72... | collective-permute-start | bytes 12296 | tf_op jit(solution)/shard_map/ppermute | solution.py:410
  27.1 0.8 %collective-permute-done.7 = f32[8,128]{1,0:T(8,128)S(1)} collective-permute-done((f32[8,128]{1,0:T(8,128)S(1)}, f32[8,128]{1,0:T(8,128)S(1)}, u32[]{:S(2)}, u32[]{:S(2)}) %collective-permute-start.7) | collective-permute-done | bytes 4128 | tf_op jit(solution)/shard_map/ppermute | solution.py:410
  28.0 0.3 collective-permute-start.9
  28.3 1.2 %collective-permute-start.8 = (f32[8,128]{1,0:T(8,128)S(1)}, f32[8,128]{1,0:T(8,128)S(1)}, u32[]{:S(2)}, u32[]{:S(2)}) collective-permute-start(f32[8,128]{1,0:T(8,128)S(1)} %add.12), channel_id=1, source_target_pairs={{0,1},{1,0},{2,3},{3,2},{4,5},{5,4},{6,7},{7,6},{8,9},{9,8},{10,11... | collective-permute-start | bytes 12296 | tf_op jit(solution)/shard_map/ppermute | solution.py:415
  29.5 2.2 %own1.1 = f32[4,128,1024]{2,1,0:T(8,128)} custom-call(f32[4,128,1024]{2,1,0:T(8,128)S(1)} %get-tuple-element.24.acc_ref.refs_0_, s32[32,128]{1,0:T(8,128)S(1)} %get-tuple-element.25.pos_ref.refs_1_, f32[16,128]{1,0:T(8,128)S(1)} %mine.1.refs_2_, bf16[256,256]{1,0:T(8,128)(2,1)S(1)} %copy-done.2, ...), custom_call_target="tpu_custom_call", output_to_operand_aliasing={{}: (5, {})} | custom-call | flops 2200000000 | bytes 4400000 | tf_op jit(solution)/shard_map/own1/pallas_call | solution.py:350
  31.8 1.9 %collective-permute-start.10 = (f32[8,128]{1,0:T(8,128)S(1)}, f32[8,128]{1,0:T(8,128)S(1)}, u32[]{:S(2)}, u32[]{:S(2)}) collective-permute-start(f32[8,128]{1,0:T(8,128)S(1)} %add.13), channel_id=1, source_target_pairs={{0,1},{1,0},{2,3},{3,2},{4,5},{5,4},{6,7},{7,6},{8,11},{9,10},{10,... | collective-permute-start | bytes 12296 | tf_op jit(solution)/shard_map/ppermute | solution.py:415
  33.7 0.9 %decode.2.refs_0_ = f32[2,128,1024]{2,1,0:T(8,128)S(1)} custom-call(f32[2,4,128,256]{3,2,1,0:T(8,128)S(1)} %get-tuple-element.41.grid_ref, bf16[256,256]{1,0:T(8,128)(2,1)S(1)} %copy-done.2, bf16[256,256]{1,0:T(8,128)(2,1)S(1)} %copy-done.1), custom_call_target="tpu_custom_call" | custom-call | flops 1600000000 | bytes 3200000 | tf_op jit(solution)/shard_map/decode/pallas_call | solution.py:389
  34.6 0.9 %decode.3.refs_1_ = f32[2,128,1024]{2,1,0:T(8,128)S(1)} custom-call(f32[2,4,128,256]{3,2,1,0:T(8,128)S(1)} %collective-permute-done.9.grid_ref, bf16[256,256]{1,0:T(8,128)(2,1)S(1)} %copy-done.2, bf16[256,256]{1,0:T(8,128)(2,1)S(1)} %copy-done.1), custom_call_target="tpu_custom_call" | custom-call | flops 1600000000 | bytes 3200000 | tf_op jit(solution)/shard_map/decode/pallas_call | solution.py:389
  35.5 3.8 %collective-permute-start.11 = (f32[8,128]{1,0:T(8,128)S(1)}, f32[8,128]{1,0:T(8,128)S(1)}, u32[]{:S(2)}, u32[]{:S(2)}) collective-permute-start(f32[8,128]{1,0:T(8,128)S(1)} %add.14), channel_id=1, source_target_pairs={{8,44},{0,1},{9,45},{1,0},{10,46},{2,3},{11,47},{3,2},{24,60},{16,... | collective-permute-start | bytes 12296 | tf_op jit(solution)/shard_map/ppermute | solution.py:427
  39.4 1.0 %collective-permute-done.11 = f32[8,128]{1,0:T(8,128)S(1)} collective-permute-done((f32[8,128]{1,0:T(8,128)S(1)}, f32[8,128]{1,0:T(8,128)S(1)}, u32[]{:S(2)}, u32[]{:S(2)}) %collective-permute-start.11) | collective-permute-done | bytes 4128 | tf_op jit(solution)/shard_map/ppermute | solution.py:427
  40.4 1.5 %rescale.1.refs_3_ = f32[4,128,1024]{2,1,0:T(8,128)} custom-call(f32[2,128,1024]{2,1,0:T(8,128)S(1)} %decode.2.refs_0_, f32[2,128,1024]{2,1,0:T(8,128)S(1)} %decode.3.refs_1_, f32[8,128]{1,0:T(8,128)S(1)} %add.15.refs_2_), custom_call_target="tpu_custom_call" | custom-call | flops 1400000000 | bytes 2800000 | tf_op jit(solution)/shard_map/rescale/pallas_call | solution.py:397
  (29 shorter events, 0.7 us)
Async XLA Ops:
  0.6 6.6 %copy-start.3 = (bf16[256,256]{1,0:T(8,128)(2,1)S(1)}, bf16[256,256]{1,0:T(8,128)(2,1)}, u32[]{:S(2)}) copy-start(bf16[256,256]{1,0:T(8,128)(2,1)} %constant.6.clone.weights_hbm.weights_ref) | copy-start | bytes 393220
  3.9 4.4 %collective-permute-start = (f32[16,128]{1,0:T(8,128)S(1)}, f32[16,128]{1,0:T(8,128)S(1)}, u32[]{:S(2)}, u32[]{:S(2)}) collective-permute-start(f32[16,128]{1,0:T(8,128)S(1)} %get-tuple-element.28.refs_2_), channel_id=1, source_target_pairs={{0,8},{8,0},{16,24},{24,16},{32,40},{40,32},{48,56},{56,48},{64,72... | collective-permute-start | bytes 24584 | tf_op jit(solution)/shard_map/ppermute | solution.py:410
  7.2 4.8 %copy-start.1 = (bf16[256,256]{1,0:T(8,128)(2,1)S(1)}, bf16[256,256]{1,0:T(8,128)(2,1)}, u32[]{:S(2)}) copy-start(bf16[256,256]{1,0:T(8,128)(2,1)} %constant.8.clone.refs_4_.rows_ref) | copy-start | bytes 393220
  7.2 4.8 %copy-start.2 = (bf16[256,256]{1,0:T(8,128)(2,1)S(1)}, bf16[256,256]{1,0:T(8,128)(2,1)}, u32[]{:S(2)}) copy-start(bf16[256,256]{1,0:T(8,128)(2,1)} %constant.7.clone.refs_3_.cols_ref) | copy-start | bytes 393220
  8.4 5.9 %copy-start = (s32[32,4,2,16,32]{4,3,2,1,0:T(8,128)S(1)}, s32[32,4,2,16,32]{4,3,2,1,0:T(8,128)}, u32[]{:S(2)}) copy-start(s32[32,4,2,16,32]{4,3,2,1,0:T(8,128)} %param.8) | copy-start | bytes 1572868
  8.4 6.2 %collective-permute-start.3 = (f32[2,16,128]{2,1,0:T(8,128)S(1)}, f32[2,16,128]{2,1,0:T(8,128)S(1)}, u32[]{:S(2)}, u32[]{:S(2)}) collective-permute-start(f32[2,16,128]{2,1,0:T(8,128)S(1)} %pad_maximum_fusion.1), channel_id=1, source_target_pairs={{0,48},{8,56},{16,32},{24,40},{32,16},{40,24},{48,0},{56,8},{64,11... | collective-permute-start | bytes 49160 | tf_op jit(solution)/shard_map/ppermute | solution.py:410
  11.1 3.6 %collective-permute-start.2 = (f32[2,16,128]{2,1,0:T(8,128)S(1)}, f32[2,16,128]{2,1,0:T(8,128)S(1)}, u32[]{:S(2)}, u32[]{:S(2)}) collective-permute-start(f32[2,16,128]{2,1,0:T(8,128)S(1)} %pad_maximum_fusion.1), channel_id=1, source_target_pairs={{0,32},{8,40},{16,48},{24,56},{32,0},{40,8},{48,16},{56,24},{64,96... | collective-permute-start | bytes 49160 | tf_op jit(solution)/shard_map/ppermute | solution.py:410
  11.1 3.6 %collective-permute-start.1 = (f32[2,16,128]{2,1,0:T(8,128)S(1)}, f32[2,16,128]{2,1,0:T(8,128)S(1)}, u32[]{:S(2)}, u32[]{:S(2)}) collective-permute-start(f32[2,16,128]{2,1,0:T(8,128)S(1)} %pad_maximum_fusion.1), channel_id=1, source_target_pairs={{0,16},{8,24},{16,0},{24,8},{32,48},{40,56},{48,32},{56,40},{64,80... | collective-permute-start | bytes 49160 | tf_op jit(solution)/shard_map/ppermute | solution.py:410
  14.6 5.4 %collective-permute-start.6 = (f32[8,16,128]{2,1,0:T(8,128)S(1)}, f32[8,16,128]{2,1,0:T(8,128)S(1)}, u32[]{:S(2)}, u32[]{:S(2)}) collective-permute-start(f32[8,16,128]{2,1,0:T(8,128)S(1)} %pad_maximum_fusion.refs_0_), channel_id=1, source_target_pairs={{0,64},{8,72},{16,80},{24,88},{32,96},{40,104},{48,112},{56,120},{... | collective-permute-start | bytes 196616 | tf_op jit(solution)/shard_map/ppermute | solution.py:410
  16.0 5.4 %collective-permute-start.5 = (f32[8,16,128]{2,1,0:T(8,128)S(1)}, f32[8,16,128]{2,1,0:T(8,128)S(1)}, u32[]{:S(2)}, u32[]{:S(2)}) collective-permute-start(f32[8,16,128]{2,1,0:T(8,128)S(1)} %pad_maximum_fusion.refs_0_), channel_id=1, source_target_pairs={{0,192},{8,200},{16,208},{24,216},{32,224},{40,232},{48,240},{56,2... | collective-permute-start | bytes 196616 | tf_op jit(solution)/shard_map/ppermute | solution.py:410
  17.9 5.0 %collective-permute-start.4 = (f32[8,16,128]{2,1,0:T(8,128)S(1)}, f32[8,16,128]{2,1,0:T(8,128)S(1)}, u32[]{:S(2)}, u32[]{:S(2)}) collective-permute-start(f32[8,16,128]{2,1,0:T(8,128)S(1)} %pad_maximum_fusion.refs_0_), channel_id=1, source_target_pairs={{0,128},{8,136},{16,144},{24,152},{32,160},{40,168},{48,176},{56,1... | collective-permute-start | bytes 196616 | tf_op jit(solution)/shard_map/ppermute | solution.py:410
  24.3 3.7 %collective-permute-start.7 = (f32[8,128]{1,0:T(8,128)S(1)}, f32[8,128]{1,0:T(8,128)S(1)}, u32[]{:S(2)}, u32[]{:S(2)}) collective-permute-start(f32[8,128]{1,0:T(8,128)S(1)} %get-tuple-element.33), channel_id=1, source_target_pairs={{0,8},{8,0},{16,24},{24,16},{32,40},{40,32},{48,56},{56,48},{64,72... | collective-permute-start | bytes 12296 | tf_op jit(solution)/shard_map/ppermute | solution.py:410
  28.0 3.8 %collective-permute-start.9 = (f32[2,4,128,256]{3,2,1,0:T(8,128)S(1)}, f32[2,4,128,256]{3,2,1,0:T(8,128)S(1)}, u32[]{:S(2)}, u32[]{:S(2)}) collective-permute-start(f32[2,4,128,256]{3,2,1,0:T(8,128)S(1)} %get-tuple-element.41.grid_ref), channel_id=1, source_target_pairs={{0,8},{8,0},{16,24},{24,16},{32,40},{40,32},{48,56},{56,48},{64,72... | collective-permute-start | bytes 3145736 | tf_op jit(solution)/shard_map/ppermute | solution.py:410
  28.3 3.4 %collective-permute-start.8 = (f32[8,128]{1,0:T(8,128)S(1)}, f32[8,128]{1,0:T(8,128)S(1)}, u32[]{:S(2)}, u32[]{:S(2)}) collective-permute-start(f32[8,128]{1,0:T(8,128)S(1)} %add.12), channel_id=1, source_target_pairs={{0,1},{1,0},{2,3},{3,2},{4,5},{5,4},{6,7},{7,6},{8,9},{9,8},{10,11... | collective-permute-start | bytes 12296 | tf_op jit(solution)/shard_map/ppermute | solution.py:415
  31.8 3.8 %collective-permute-start.10 = (f32[8,128]{1,0:T(8,128)S(1)}, f32[8,128]{1,0:T(8,128)S(1)}, u32[]{:S(2)}, u32[]{:S(2)}) collective-permute-start(f32[8,128]{1,0:T(8,128)S(1)} %add.13), channel_id=1, source_target_pairs={{0,1},{1,0},{2,3},{3,2},{4,5},{5,4},{6,7},{7,6},{8,11},{9,10},{10,... | collective-permute-start | bytes 12296 | tf_op jit(solution)/shard_map/ppermute | solution.py:415
  35.5 4.8 %collective-permute-start.11 = (f32[8,128]{1,0:T(8,128)S(1)}, f32[8,128]{1,0:T(8,128)S(1)}, u32[]{:S(2)}, u32[]{:S(2)}) collective-permute-start(f32[8,128]{1,0:T(8,128)S(1)} %add.14), channel_id=1, source_target_pairs={{8,44},{0,1},{9,45},{1,0},{10,46},{2,3},{11,47},{3,2},{24,60},{16,... | collective-permute-start | bytes 12296 | tf_op jit(solution)/shard_map/ppermute | solution.py:427
  40.4 1.5 %collective-permute-start.12 = (f32[8,128]{1,0:T(8,128)S(1)}, f32[8,128]{1,0:T(8,128)S(1)}, u32[]{:S(2)}, u32[]{:S(2)}) collective-permute-start(f32[8,128]{1,0:T(8,128)S(1)} %add.15.refs_2_), channel_id=1, source_target_pairs={{0,8},{8,0},{16,24},{24,16},{32,40},{40,32},{48,56},{56,48},{64,72... | collective-permute-start | bytes 12296 | tf_op jit(solution)/shard_map/ppermute | solution.py:410
